TPU v7x, 32 devices: a whole 2x2x4 slice. The times are simulated.
32 devices in a mesh: blk: 2 (over x), stripe: 16 (over z, y, core).
Axes of the slice: x: 2, y: 2, z: 4, core: 2. Of those that a mesh axis runs over, the one named last changes fastest.
Arguments:
- points: bfloat16 [16384, 64], P(('blk', 'stripe')), may hold values from -6 to 6
- coefficients: float32 [16384], P(('blk', 'stripe')), may hold values from -0.09375 to 0.09375
- velocity: float32 [16384], P(('blk', 'stripe')), may hold values from -0.09375 to 0.09375
- targets: float32 [16384], P(('blk', 'stripe')), may hold values from -6 to 6
- batch_rows: int32 [2048], P(('blk', 'stripe')), may hold values from 0 to 511
- counts: int32 [2, 16], P('blk', 'stripe'), may hold values from 1 to 64, 512 in all within a row
Outputs:
- new_coefficients: float32 [16384], P(('blk', 'stripe'))
- new_velocity: float32 [16384], P(('blk', 'stripe'))
Inputs may be any that keep to these rules, and one draw needn't show every extreme that they name: In every index of blk, the counts of its 16 devices sum to exactly 512, and some device's count is exactly 64. Only the first count entries of a device's slots are live. `batch_rows`: every entry, live or not, indexes the points of the device that holds it; rows may repeat.
All inputs are finite; a program needn't handle non-finite values.
Results may differ from a plain program's by a relative error of at most 0.0003.
Values may be sent and summed in bfloat16 or wider, within the bound.
No kernel may reach another device: no remote copies, remote signals or barrier semaphores. Data moves between devices by JAX's collectives and lax.ppermute only.
A program may use at most 64 MiB of HBM per device.

v0:
```python
import math

import jax
import jax.numpy as jnp
from jax import lax
from jax.sharding import PartitionSpec as P

MOMENTUM = 0.9
STEP_SIZE = 1.0
NOISE_VAR = 8.0
KERNEL_RATE = 3.0**0.5 / 6.0


def matern_sums(row_feats, row_sq, col_points, col_coef):
    col_sq = jnp.sum(jnp.square(col_points.astype(jnp.float32)), axis=1)
    inner_prod = lax.dot_general(
        row_feats, col_points, (((1,), (1,)), ((), ())), preferred_element_type=jnp.float32
    )
    distance = jnp.sqrt(jnp.maximum(row_sq[:, None] + col_sq[None, :] - 2.0 * inner_prod, 0.0))
    scaled = KERNEL_RATE * distance
    kernel_tile = (1.0 + scaled) * jnp.exp(-scaled)
    return jnp.sum(kernel_tile * col_coef[None, :], axis=1)


def column_sums(row_feats, points, preview):
    row_sq = jnp.sum(jnp.square(row_feats.astype(jnp.float32)), axis=1)
    every_coef = lax.all_gather(preview, "blk", axis=0, tiled=True)
    zeros_init = jnp.zeros((row_feats.shape[0],), jnp.float32)
    piece_points = lax.all_gather(points, "blk", axis=0, tiled=True)
    piece_len = piece_points.shape[0]
    block_len = math.gcd(piece_len, 512)
    point_blocks = piece_points.reshape(-1, block_len, piece_points.shape[1])
    coef_blocks = every_coef.reshape(-1, block_len)

    def advance(partial_sum, column_block):
        return (
            partial_sum + matern_sums(row_feats, row_sq, column_block[0], column_block[1]),
            None,
        )

    result, unused = lax.scan(advance, zeros_init, (point_blocks, coef_blocks))
    return result


def per_device(points, coefficients, velocity, targets, batch_rows, counts):
    preview = coefficients + MOMENTUM * velocity
    slot_total = batch_rows.shape[0]
    local_size = points.shape[0]
    slot_ids = jnp.arange(slot_total, dtype=jnp.int32)
    count_here = counts.reshape((1,))
    in_count = slot_ids < count_here[0]
    picked = jnp.take(points, batch_rows, axis=0)
    group_rows = lax.all_gather(picked, "stripe", axis=0, tiled=True)
    partial_value = column_sums(group_rows, points, preview)
    kernel_rows = lax.psum_scatter(partial_value, "stripe", scatter_dimension=0, tiled=True)
    residual = jnp.where(
        in_count,
        kernel_rows + NOISE_VAR * jnp.take(preview, batch_rows) - jnp.take(targets, batch_rows),
        0.0,
    )
    scatter_rows = (batch_rows[:, None] == jnp.arange(local_size, dtype=jnp.int32)[None, :]).astype(
        jnp.float32
    )
    update_sum = jnp.dot(residual, scatter_rows, precision=lax.Precision.HIGHEST)
    new_velocity = MOMENTUM * velocity - STEP_SIZE * update_sum
    new_coefficients = coefficients + new_velocity
    return (new_coefficients, new_velocity)


def solution(mesh):
    in_specs = (
        P(("blk", "stripe"), None),
        P(("blk", "stripe")),
        P(("blk", "stripe")),
        P(("blk", "stripe")),
        P(("blk", "stripe")),
        P("blk", "stripe"),
    )
    out_specs = (P(("blk", "stripe")), P(("blk", "stripe")))
    return jax.shard_map(
        per_device, mesh=mesh, in_specs=in_specs, out_specs=out_specs, check_vma=False
    )
```

profile of v0, /device:TPU:0, one launch (start us, length us, event | category | flops | bytes accessed | tf_op | source)
XLA Modules:
  0.0 75.3 jit_solution(12476009032031851626)
XLA Ops:
  0.6 0.0 copy-start
  1.3 1.2 %dynamic-slice = u32[1]{0:T(128)} dynamic-slice(u32[32]{0:T(128)} %constant.55, u32[]{:T(128)S(6)} %add.65), dynamic_slice_sizes={1} | dynamic-slice | bytes 12
  3.2 0.7 compare_and_fusion
  3.9 0.7 compare_select_fusion
  4.5 0.7 multiply_add_fusion
  5.2 0.0 copy-done
  5.2 0.8 %gather_fusion.2 = f32[64]{0:T(128)S(1)} fusion(f32[512]{0:T(512)S(1)} %copy-done, s32[1024]{0:T(1024)S(1)} %pad_clamp_fusion), kind=kCustom, calls=%fused_computation.1.clone | custom fusion | bytes 768 | tf_op jit(solution)/shard_map/jit(_take)/gather | solution.py:58
  6.0 0.0 copy-start.1
  6.0 0.8 %gather_fusion.1 = f32[64]{0:T(128)S(1)} fusion(f32[512]{0:T(512)S(1)} %multiply_add_fusion, s32[1024]{0:T(1024)S(1)} %pad_clamp_fusion), kind=kCustom, calls=%fused_computation.clone | custom fusion | bytes 768 | tf_op jit(solution)/shard_map/jit(_take)/gather | solution.py:58
  6.8 5.2 %all-gather = f32[2,1,512]{2,1,0:T(1,128)S(1)} all-gather(f32[1,1,512]{2,1,0:T(1,128)S(1)} %bitcast.38), channel_id=1, replica_groups=mesh['blk'=2,'stripe'=16] {'blk'}, dimensions={0}, use_global_device_ids=true | all-gather | bytes 6144 | tf_op jit(solution)/shard_map/all_gather | solution.py:27
  12.1 0.0 copy-done.1
  12.1 4.9 %all_gather.10 = bf16[1024,64]{0,1:T(8,128)(2,1)S(1)} all-gather(bf16[512,64]{0,1:T(8,128)(2,1)S(1)} %copy-done.1), channel_id=1, replica_groups=mesh['blk'=2,'stripe'=16] {'blk'}, dimensions={0}, use_global_device_ids=true | all-gather | bytes 196608 | tf_op jit(solution)/shard_map/all_gather | solution.py:29
  17.0 0.2 copy.13
  17.2 0.1 copy.12
  17.3 0.6 gather_fusion
  18.0 0.1 broadcast_select_fusion
  18.0 22.9 %all_gather.9 = bf16[1024,64]{1,0:T(8,128)(2,1)S(1)} all-gather(bf16[64,64]{1,0:T(8,128)(2,1)S(1)} %broadcast_select_fusion), channel_id=1, replica_groups=mesh['blk'=2,'stripe'=16] {'stripe'}, dimensions={0}, use_global_device_ids=true | all-gather | bytes 139264 | tf_op jit(solution)/shard_map/all_gather | solution.py:53
  40.9 0.2 multiply_reduce_fusion.2
  41.2 0.0 copy-start.4
  41.2 0.0 copy-start.2
  41.2 0.0 copy-start.3
  41.2 3.4 %while.11 = (s32[]{:T(128)}, f32[1024]{0:T(1024)S(1)}, f32[1024]{0:T(1024)S(1)}, bf16[2,512,64]{2,1,0:T(8,128)(2,1)S(1)}, bf16[1024,64]{1,0:T(8,128)(2,1)S(1)}, /*index=5*/f32[2,512]{1,0:T(2,128)S(1)}, s32[]{:T(128)}, s32[]{:T(128)}) while((s32[]{:T(128)}, f32[1024]{0:T(1024)S(1)}, f32[1024]{0:T(1024)S(1)}, ...), condition=%wide.region_4.5_spmd.clone, body=%wide.region_1.0_spmd.clone.sunk | while | flops 72450560 | bytes 489587 | solution.py:41
  41.2 0.2 multiply_reduce_fusion.5
  41.4 1.5 %multiply_reduce_fusion.6 = f32[1024]{0:T(1024)S(1)} fusion(bf16[1024,64]{1,0:T(8,128)(2,1)S(1)} %get-tuple-element.128, f32[512]{0:T(512)S(1)} %bitcast.40, f32[512]{0:T(512)S(1)} %multiply_reduce_fusion.5, f32[1024]{0:T(1024)S(1)} %get-tuple-element.126, bf16[2,512,64]{2,1,0:T(8,128)(2,1)S(1)} %get-tuple-element.127, s32[]{:T(128)S(6)} %copy.19), kind=kOutput, calls=%fused_computation.7.clone.1 | convolution fusion | flops 72350720 | bytes 405508 | tf_op jit(solution)/shard_map/while/body/eval_jaxpr/dot_general | solution.py:16
  42.9 0.2 multiply_reduce_fusion.5
  43.1 1.5 %multiply_reduce_fusion.6 = f32[1024]{0:T(1024)S(1)} fusion(bf16[1024,64]{1,0:T(8,128)(2,1)S(1)} %get-tuple-element.128, f32[512]{0:T(512)S(1)} %bitcast.40, f32[512]{0:T(512)S(1)} %multiply_reduce_fusion.5, f32[1024]{0:T(1024)S(1)} %get-tuple-element.126, bf16[2,512,64]{2,1,0:T(8,128)(2,1)S(1)} %get-tuple-element.127, s32[]{:T(128)S(6)} %copy.19), kind=kOutput, calls=%fused_computation.7.clone.1 | convolution fusion | flops 72350720 | bytes 405508 | tf_op jit(solution)/shard_map/while/body/eval_jaxpr/dot_general | solution.py:16
  44.6 29.8 %all-reduce = f32[1024]{0:T(1024)S(1)} all-reduce(f32[1024]{0:T(1024)S(1)} %get-tuple-element.35), channel_id=2, replica_groups=mesh['blk'=2,'stripe'=16] {'stripe'}, use_global_device_ids=true, to_apply=%region_5.6.clone | all-reduce | flops 1024 | bytes 8192
  74.5 0.0 copy-done.4
  74.5 0.2 fusion.6
  74.7 0.0 copy-done.2
  74.7 0.0 copy-done.3
  74.7 0.6 fusion.21
  (7 shorter events, 0.0 us)
Async XLA Ops:
  0.6 4.6 %copy-start = (f32[512]{0:T(512)S(1)}, f32[512]{0:T(512)}, u32[]{:S(2)}) copy-start(f32[512]{0:T(512)} %param.13) | copy-start | bytes 6148
  6.0 6.0 %copy-start.1 = (bf16[512,64]{0,1:T(8,128)(2,1)S(1)}, bf16[512,64]{0,1:T(8,128)(2,1)}, u32[]{:S(2)}) copy-start(bf16[512,64]{0,1:T(8,128)(2,1)} %param.10) | copy-start | bytes 196612
  41.2 33.3 %copy-start.4 = (s32[64]{0:T(128)S(1)}, s32[64]{0:T(128)}, u32[]{:S(2)}) copy-start(s32[64]{0:T(128)} %param.14) | copy-start | bytes 772
  41.2 33.5 %copy-start.2 = (f32[512]{0:T(512)S(1)}, f32[512]{0:T(512)}, u32[]{:S(2)}) copy-start(f32[512]{0:T(512)} %param.11) | copy-start | bytes 6148
  41.2 33.5 %copy-start.3 = (f32[512]{0:T(512)S(1)}, f32[512]{0:T(512)}, u32[]{:S(2)}) copy-start(f32[512]{0:T(512)} %param.12) | copy-start | bytes 6148
where the time goes:
time: 75.6 us; the launch traced here: 75.3 us
  blocking collectives  62.9 us (83%)
  local copies, waits for them, and re-layouts  3.83 us (5%)
  matrix products  3.25 us (4%)
  other arithmetic  3.22 us (4%)
  between operations  2.02 us (3%)
    unnamed x1, blocking collectives  29.8 us
    all_gather x1, blocking collectives, per_device(): group_rows = lax.all_gather(picked, 'stripe', axis=0, tiled=True)  22.9 us
    all_gather x1, blocking collectives, column_sums(): every_coef = lax.all_gather(preview, 'blk', axis=0, tiled=True)  5.22 us
    all_gather x1, blocking collectives, column_sums(): piece_points = lax.all_gather(points, 'blk', axis=0, tiled=True)  4.95 us
    dot_general x2, matrix products, matern_sums(): lax.dot_general(row_feats, col_points, (((1,), (1,)), ((), ())), preferre...  3.03 us

commit v1 on v0

v1 whole, which is shorter than its diff:
```python
import functools

import jax
import jax.numpy as jnp
from jax import lax
from jax.experimental import pallas as pl
from jax.experimental.pallas import tpu as pltpu
from jax.sharding import PartitionSpec as P

MOMENTUM = 0.9
STEP_SIZE = 1.0
NOISE_VAR = 8.0
KERNEL_RATE = 3.0**0.5 / 6.0
LOG2_E = 1.4426950408889634
AXES = ("blk", "stripe")
SQ_AT, ONE_AT, COEF_AT, EXTRA = 0, 3, 6, 16

F32, BF16 = jnp.float32, jnp.bfloat16


def pieces(value):
    high = value.astype(BF16).astype(F32)
    rest = value - high
    middle = rest.astype(BF16).astype(F32)
    low = (rest - middle).astype(BF16).astype(F32)
    return high, middle, low


def prepare_kernel(points, coef, velocity, targets, batch, count, payload, rows, base, spots):
    size, feats = points.shape
    slots = batch.shape[1]
    preview = coef[...] + MOMENTUM * velocity[...]
    eye = (
        lax.broadcasted_iota(jnp.int32, (feats, feats), 0)
        == lax.broadcasted_iota(jnp.int32, (feats, feats), 1)
    ).astype(BF16)
    turned = lax.dot_general(
        eye, points[...], (((1,), (1,)), ((), ())), preferred_element_type=F32
    )
    col_sq = jnp.sum(turned * turned, axis=0, keepdims=True)
    line = lax.broadcasted_iota(jnp.int32, (EXTRA, size), 0)
    extra = jnp.where((line >= ONE_AT) & (line < ONE_AT + 3), 1.0, 0.0)
    for at, parts in ((SQ_AT, pieces(col_sq)), (COEF_AT, pieces(preview))):
        for k, part in enumerate(parts):
            extra = jnp.where(line == at + k, part, extra)
    payload[...] = jnp.concatenate([turned, extra], axis=0).astype(BF16)
    diagonal = lax.broadcasted_iota(jnp.int32, (slots, slots), 0) == lax.broadcasted_iota(
        jnp.int32, (slots, slots), 1
    )
    column = jnp.sum(jnp.where(diagonal, batch[...].astype(F32), 0.0), axis=1, keepdims=True)
    place = lax.broadcasted_iota(jnp.int32, (slots, size), 1)
    chosen = place == column.astype(jnp.int32)
    picked = jnp.dot(jnp.where(chosen, 1.0, 0.0).astype(BF16), points[...], preferred_element_type=F32)
    row_sq = jnp.sum(picked * picked, axis=1, keepdims=True)
    lane = lax.broadcasted_iota(jnp.int32, (slots, feats), 1)
    tail = jnp.where((lane >= SQ_AT) & (lane < SQ_AT + 3), 1.0, 0.0)
    for k, part in enumerate(pieces(row_sq)):
        tail = jnp.where(lane == ONE_AT + k, part, tail)
    rows[...] = jnp.concatenate([-2.0 * picked, tail], axis=1).astype(BF16)
    live = lax.broadcasted_iota(jnp.int32, (slots, size), 0) < count[0, 0]
    hits = jnp.where(chosen & live, 1.0, 0.0)
    spots[...] = hits.astype(BF16)
    times = jnp.sum(hits, axis=0, keepdims=True)
    base[...] = MOMENTUM * velocity[...] - STEP_SIZE * (
        times * (NOISE_VAR * preview - targets[...])
    )


def sums_kernel(rows, *refs, feats):
    payloads, (keep, send, total) = refs[:-3], refs[-3:]
    depth = feats + EXTRA
    group = 64
    total[...] = jnp.zeros_like(total)
    lane = lax.broadcasted_iota(jnp.int32, (8, depth), 1)
    pick_coef = jnp.where((lane >= feats + COEF_AT) & (lane < feats + COEF_AT + 3), 1.0, 0.0).astype(BF16)
    for payload in payloads:
        block = payload[...]
        weight = jnp.dot(pick_coef, block, preferred_element_type=F32)
        scaled_weight = KERNEL_RATE * weight

        @pl.loop(0, rows.shape[0] // group)
        def _(step):
            start = pl.multiple_of(step * group, group)
            squares = jnp.dot(
                rows[pl.ds(start, group), :][:, :depth], block, preferred_element_type=F32
            )
            for at in range(0, group, 8):
                square = jnp.maximum(squares[at : at + 8, :], 1e-30)
                distance = square * lax.rsqrt(square)
                value = jnp.exp2((-KERNEL_RATE * LOG2_E) * distance) * (
                    weight + scaled_weight * distance
                )
                part = value[:, :128]
                for lanes in range(128, value.shape[1], 128):
                    part = part + value[:, lanes : lanes + 128]
                total[pl.ds(start + at, 8), :] += part

    flat = lax.dot_general(
        jnp.ones((8, 128), F32),
        total[...],
        (((1,), (1,)), ((), ())),
        precision=lax.Precision.HIGHEST,
        preferred_element_type=F32,
    )
    half = keep.shape[1]
    keep[...] = flat[:1, :half]
    send[...] = flat[:1, half:]


def finish_kernel(own, other, base, coef, spots, new_coef, new_velocity):
    slots = spots.shape[0]
    sums = own[...][:, :slots] + other[...]
    line = lax.broadcasted_iota(jnp.int32, (16, slots), 0)
    split = jnp.zeros((16, slots), F32)
    for k, part in enumerate(pieces(sums)):
        split = jnp.where(line == k, part, split)
    update = jnp.dot(split.astype(BF16), spots[...], preferred_element_type=F32)
    velocity = base[...] - STEP_SIZE * jnp.sum(update, axis=0, keepdims=True)
    new_velocity[...] = velocity
    new_coef[...] = coef[...] + velocity


def vmem(count):
    return [pl.BlockSpec(memory_space=pltpu.VMEM)] * count


def per_device(mesh_shape, points, coefficients, velocity, targets, batch_rows, counts):
    n_blk, n_stripe = mesh_shape["blk"], mesh_shape["stripe"]
    size, feats = points.shape
    slots = batch_rows.shape[0]

    def exchange(value, offset):
        d_blk, d_stripe = offset
        pairs = [
            (b * n_stripe + s, (b ^ d_blk) * n_stripe + (s ^ d_stripe))
            for b in range(n_blk)
            for s in range(n_stripe)
        ]
        return lax.ppermute(value, AXES, pairs)

    point_steps = [(1 << k, 1) for k in range(n_blk.bit_length() - 1)] + [(0, 3)]
    row_steps = [(0, 1)] + [(0, (1 << k) + 1) for k in range(2, n_stripe.bit_length() - 1)]

    coef = coefficients.reshape(1, size)
    payload, rows, base, spots = pl.pallas_call(
        prepare_kernel,
        out_shape=[
            jax.ShapeDtypeStruct((feats + EXTRA, size), BF16),
            jax.ShapeDtypeStruct((slots, 2 * feats), BF16),
            jax.ShapeDtypeStruct((1, size), F32),
            jax.ShapeDtypeStruct((slots, size), BF16),
        ],
        in_specs=vmem(5) + [pl.BlockSpec(memory_space=pltpu.SMEM)],
        out_specs=vmem(4),
        name="prepare",
    )(
        points,
        coef,
        velocity.reshape(1, size),
        targets.reshape(1, size),
        batch_rows.reshape(1, slots),
        counts,
    )

    payloads = [payload]
    for step in point_steps:
        payloads = payloads + [exchange(p, step) for p in payloads]
    for step in row_steps:
        rows = jnp.concatenate([rows, exchange(rows, step)], axis=0)

    half = rows.shape[0] // 2
    keep, send = pl.pallas_call(
        functools.partial(sums_kernel, feats=feats),
        out_shape=[jax.ShapeDtypeStruct((1, half), F32)] * 2,
        in_specs=vmem(1 + len(payloads)),
        out_specs=vmem(2),
        scratch_shapes=[pltpu.VMEM((2 * half, 128), F32)],
        compiler_params=pltpu.CompilerParams(vmem_limit_bytes=32 << 20),
        name="kernel_sums",
    )(rows, *payloads)

    for step in row_steps[:0:-1]:
        both = keep + exchange(send, step)
        half = half // 2
        keep, send = both[:, :half], both[:, half:]
    other = exchange(send, row_steps[0])

    new_coef, new_velocity = pl.pallas_call(
        finish_kernel,
        out_shape=[jax.ShapeDtypeStruct((1, size), F32)] * 2,
        in_specs=vmem(5),
        out_specs=vmem(2),
        name="finish",
    )(keep, other, base, coef, spots)
    return new_coef.reshape(size), new_velocity.reshape(size)


def solution(mesh):
    in_specs = (
        P(("blk", "stripe"), None),
        P(("blk", "stripe")),
        P(("blk", "stripe")),
        P(("blk", "stripe")),
        P(("blk", "stripe")),
        P("blk", "stripe"),
    )
    out_specs = (P(("blk", "stripe")), P(("blk", "stripe")))
    return jax.shard_map(
        functools.partial(per_device, dict(mesh.shape)),
        mesh=mesh,
        in_specs=in_specs,
        out_specs=out_specs,
        check_vma=False,
    )
```

time: 75.6 us -> 38.1 us (0.50)
  blocking collectives: 62.9 us -> 0 us
  starting transfers between devices: 0 us -> 11.8 us
  waiting for transfers between devices: 0 us -> 11 us
  Pallas kernels: 0 us -> 10.3 us
  matrix products: 3.25 us -> 0 us
  other arithmetic: 3.22 us -> 0.74 us
  local copies, waits for them, and re-layouts: 3.83 us -> 2.69 us
    all_gather x3 -> x0, blocking collectives: 33.1 us -> none  [the longest x1 22.9 us: per_device(): group_rows = lax.all_gather(picked, 'stripe', axis=0, tiled=True)]
    unnamed x1 -> x0, blocking collectives: 29.8 us -> none
    ppermute x0 -> x9, starting transfers between devices: none -> 11.8 us  [exchange(): return lax.ppermute(value, AXES, pairs)]
    ppermute x0 -> x9, waiting for transfers between devices: none -> 11 us  [exchange(): return lax.ppermute(value, AXES, pairs)]
    pallas_call x0 -> x3, Pallas kernels: none -> 10.3 us  [the longest x1 6.75 us: per_device(): pl.pallas_call(functools.partial(sums_kernel, feats=feats), out_shape=[ja...]
    dot_general x3 -> x0, matrix products: 3.25 us -> none  [the longest x2 3.03 us: matern_sums(): lax.dot_general(row_feats, col_points, (((1,), (1,)), ((), ())), preferre...]
    gather x3 -> x0, local copies, waits for them, and re-layouts: 2.24 us -> none  [the longest x1 0.8 us: per_device(): jnp.take(preview, batch_rows)]
    add x4 -> x2, other arithmetic: 1.3 us -> 0.01 us  [per_device(): both = keep + exchange(send, step)]
  transfers between devices with their start and end apart: 0 -> 9, of which waited for: 0 -> 8; matrix products, arithmetic and copies ran while one was open for 0% -> 0% of each run, Pallas kernels for 0% -> 0%
where the time goes in v1:
time: 38.1 us; the launch traced here: 37.8 us
  starting transfers between devices  11.8 us (31%)
  waiting for transfers between devices  11 us (29%)
  Pallas kernels  10.3 us (27%)
  local copies, waits for them, and re-layouts  2.69 us (7%)
  between operations  1.3 us (3%)
  other arithmetic  0.74 us (2%)
    ppermute x9, starting transfers between devices, exchange(): return lax.ppermute(value, AXES, pairs)  11.8 us
    ppermute x9, waiting for transfers between devices, exchange(): return lax.ppermute(value, AXES, pairs)  11 us
    pallas_call x1, Pallas kernels, per_device(): pl.pallas_call(functools.partial(sums_kernel, feats=feats), out_shape=[ja...  6.75 us
    unnamed x7, local copies, waits for them, and re-layouts  2.18 us
    pallas_call x1, Pallas kernels, per_device(): pl.pallas_call(prepare_kernel, out_shape=[jax.ShapeDtypeStruct((feats + E...  1.92 us
    pallas_call x1, Pallas kernels, per_device(): pl.pallas_call(finish_kernel, out_shape=[jax.ShapeDtypeStruct((1, size),...  1.59 us
  transfers between devices with their start and end apart: 9, of which 8 were waited for; matrix products, arithmetic and copies ran while one was open for 0% of the time, Pallas kernels for 0%

profile of v1, /device:TPU:0, one launch (start us, length us, event | category | flops | bytes accessed | tf_op | source)
XLA Modules:
  0.0 37.8 jit_solution(7491978435196979644)
XLA Ops:
  1.3 1.6 %copy.8.points = bf16[512,64]{1,0:T(8,128)(2,1)} copy(bf16[512,64]{0,1:T(8,128)(2,1)} %param.6) | data formatting | bytes 131072 | tf_op args[0]
  2.9 1.9 %prepare.1 = (bf16[80,512]{1,0:T(8,128)(2,1)}, bf16[64,128]{1,0:T(8,128)(2,1)}, f32[1,512]{1,0:T(1,128)}, bf16[64,512]{1,0:T(8,128)(2,1)}) custom-call(bf16[512,64]{1,0:T(8,128)(2,1)} %copy.8.points, f32[1,512]{1,0:T(1,128)} %bitcast.6, f32[1,512]{1,0:T(1,128)} %bitcast.8, f32[1,512]{1,0:T(1,128)} %bitcast.9, s32[1,64]{1,0:T(1,128)} %bitcast.10, ...), custom_call_target="tpu_custom_call" | custom-call | tf_op jit(solution)/shard_map/prepare/pallas_call | solution.py:145
  4.8 0.0 copy-start.1
  4.8 0.5 %collective-permute-start = (bf16[64,128]{1,0:T(8,128)(2,1)}, bf16[64,128]{1,0:T(8,128)(2,1)S(1)}, u32[]{:S(2)}, u32[]{:S(2)}) collective-permute-start(bf16[64,128]{1,0:T(8,128)(2,1)} %get-tuple-element.10), channel_id=1, source_target_pairs={{0,1},{1,0},{2,3},{3,2},{4,5},{5,4},{6,7},{7,6},{8,9},{9,8},{10,11... | collective-permute-start | bytes 49160 | tf_op jit(solution)/shard_map/ppermute | solution.py:139
  5.3 1.0 %collective-permute-done = bf16[64,128]{1,0:T(8,128)(2,1)S(1)} collective-permute-done((bf16[64,128]{1,0:T(8,128)(2,1)}, bf16[64,128]{1,0:T(8,128)(2,1)S(1)}, u32[]{:S(2)}, u32[]{:S(2)}) %collective-permute-start) | collective-permute-done | bytes 16416 | tf_op jit(solution)/shard_map/ppermute | solution.py:139
  6.3 0.7 %pad_maximum_fusion.2 = bf16[128,128]{1,0:T(8,128)(2,1)S(1)} fusion(bf16[64,128]{1,0:T(8,128)(2,1)S(1)} %collective-permute-done, bf16[64,128]{1,0:T(8,128)(2,1)} %get-tuple-element.10), kind=kLoop, calls=%fused_computation.2 | loop fusion | flops 65536 | bytes 65536 | tf_op jit(solution)/shard_map/concatenate | solution.py:169
  7.0 0.0 copy-start
  7.0 2.7 %collective-permute-start.1 = (bf16[128,128]{1,0:T(8,128)(2,1)S(1)}, bf16[128,128]{1,0:T(8,128)(2,1)S(1)}, u32[]{:S(2)}, u32[]{:S(2)}) collective-permute-start(bf16[128,128]{1,0:T(8,128)(2,1)S(1)} %pad_maximum_fusion.2), channel_id=1, source_target_pairs={{0,5},{1,4},{2,7},{3,6},{4,1},{5,0},{6,3},{7,2},{8,13},{9,12},{10,... | collective-permute-start | bytes 98312 | tf_op jit(solution)/shard_map/ppermute | solution.py:139
  9.7 1.4 %collective-permute-start.3 = (bf16[80,512]{1,0:T(8,128)(2,1)}, bf16[80,512]{1,0:T(8,128)(2,1)S(1)}, u32[]{:S(2)}, u32[]{:S(2)}) collective-permute-start(bf16[80,512]{1,0:T(8,128)(2,1)} %get-tuple-element.11.refs_0_), channel_id=1, source_target_pairs={{0,17},{1,16},{2,19},{3,18},{4,21},{5,20},{6,23},{7,22},{8,25},{9,... | collective-permute-start | bytes 245768 | tf_op jit(solution)/shard_map/ppermute | solution.py:139
  11.2 0.2 collective-permute-done.1
  11.3 0.0 copy-done.1
  11.3 2.8 %collective-permute-start.2 = (bf16[256,128]{1,0:T(8,128)(2,1)S(1)}, bf16[256,128]{1,0:T(8,128)(2,1)S(1)}, u32[]{:S(2)}, u32[]{:S(2)}) collective-permute-start(bf16[256,128]{1,0:T(8,128)(2,1)S(1)} %pad_maximum_fusion.1), channel_id=1, source_target_pairs={{0,9},{1,8},{2,11},{3,10},{4,13},{5,12},{6,15},{7,14},{8,1},{9,0},... | collective-permute-start | bytes 196616 | tf_op jit(solution)/shard_map/ppermute | solution.py:139
  14.1 0.0 copy-done
  14.1 1.5 %collective-permute-start.4 = (bf16[80,512]{1,0:T(8,128)(2,1)S(1)}, bf16[80,512]{1,0:T(8,128)(2,1)S(1)}, u32[]{:S(2)}, u32[]{:S(2)}) collective-permute-start(bf16[80,512]{1,0:T(8,128)(2,1)S(1)} %copy-done), channel_id=1, source_target_pairs={{0,3},{1,2},{2,1},{3,0},{4,7},{5,6},{6,5},{7,4},{8,11},{9,10},{10,... | collective-permute-start | bytes 245768 | tf_op jit(solution)/shard_map/ppermute | solution.py:139
  15.6 0.0 collective-permute-done.3.refs_1_
  15.6 0.3 collective-permute-start.5
  15.9 0.4 %collective-permute-done.2 = bf16[256,128]{1,0:T(8,128)(2,1)S(1)} collective-permute-done((bf16[256,128]{1,0:T(8,128)(2,1)S(1)}, bf16[256,128]{1,0:T(8,128)(2,1)S(1)}, u32[]{:S(2)}, u32[]{:S(2)}) %collective-permute-start.2) | collective-permute-done | bytes 65568 | tf_op jit(solution)/shard_map/ppermute | solution.py:139
  16.4 2.1 %collective-permute-done.4.refs_2_ = bf16[80,512]{1,0:T(8,128)(2,1)S(1)} collective-permute-done((bf16[80,512]{1,0:T(8,128)(2,1)S(1)}, bf16[80,512]{1,0:T(8,128)(2,1)S(1)}, u32[]{:S(2)}, u32[]{:S(2)}) %collective-permute-start.4) | collective-permute-done | bytes 81952 | tf_op jit(solution)/shard_map/ppermute | solution.py:139
  18.4 1.9 %collective-permute-done.5.refs_3_ = bf16[80,512]{1,0:T(8,128)(2,1)S(1)} collective-permute-done((bf16[80,512]{1,0:T(8,128)(2,1)S(1)}, bf16[80,512]{1,0:T(8,128)(2,1)S(1)}, u32[]{:S(2)}, u32[]{:S(2)}) %collective-permute-start.5) | collective-permute-done | bytes 81952 | tf_op jit(solution)/shard_map/ppermute | solution.py:139
  20.4 6.7 %kernel_sums.1 = (f32[1,256]{1,0:T(1,128)S(1)}, f32[1,256]{1,0:T(1,128)S(1)}) custom-call(bf16[512,128]{1,0:T(8,128)(2,1)S(1)} %pad_maximum_fusion.rows, bf16[80,512]{1,0:T(8,128)(2,1)S(1)} %copy-done, bf16[80,512]{1,0:T(8,128)(2,1)S(1)} %collective-permute-done.3.refs_1_, bf16[80,512]{1,0:T(8,128)(2,1)S(1)} %collective-permute-done.4.refs_2_, ...), custom_call_target="tpu_custom_call" | custom-call | tf_op jit(solution)/shard_map/kernel_sums/pallas_call | solution.py:172
  27.1 0.6 %collective-permute-start.6 = (f32[1,256]{1,0:T(1,128)S(1)}, f32[1,256]{1,0:T(1,128)S(1)}, u32[]{:S(2)}, u32[]{:S(2)}) collective-permute-start(f32[1,256]{1,0:T(1,128)S(1)} %get-tuple-element.13), channel_id=1, source_target_pairs={{0,9},{1,8},{2,11},{3,10},{4,13},{5,12},{6,15},{7,14},{8,1},{9,0},... | collective-permute-start | bytes 3080 | tf_op jit(solution)/shard_map/ppermute | solution.py:139
  27.7 3.3 %collective-permute-done.6 = f32[1,256]{1,0:T(1,128)S(1)} collective-permute-done((f32[1,256]{1,0:T(1,128)S(1)}, f32[1,256]{1,0:T(1,128)S(1)}, u32[]{:S(2)}, u32[]{:S(2)}) %collective-permute-start.6) | collective-permute-done | bytes 1056 | tf_op jit(solution)/shard_map/ppermute | solution.py:139
  31.0 1.7 %collective-permute-start.7 = (f32[1,128]{1,0:T(1,128)S(1)}, f32[1,128]{1,0:T(1,128)S(1)}, u32[]{:S(2)}, u32[]{:S(2)}) collective-permute-start(f32[1,128]{1,0:T(1,128)S(1)} %slice.17), channel_id=1, source_target_pairs={{0,5},{1,4},{2,7},{3,6},{4,1},{5,0},{6,3},{7,2},{8,13},{9,12},{10,... | collective-permute-start | bytes 1544 | tf_op jit(solution)/shard_map/ppermute | solution.py:139
  32.7 1.3 %collective-permute-done.7 = f32[1,128]{1,0:T(1,128)S(1)} collective-permute-done((f32[1,128]{1,0:T(1,128)S(1)}, f32[1,128]{1,0:T(1,128)S(1)}, u32[]{:S(2)}, u32[]{:S(2)}) %collective-permute-start.7) | collective-permute-done | bytes 544 | tf_op jit(solution)/shard_map/ppermute | solution.py:139
  34.0 0.5 %fusion = (f32[1,64]{1,0:T(1,128)S(1)}, f32[1,64]{1,0:T(1,128)}) fusion(f32[1,128]{1,0:T(1,128)S(1)} %slice_add_fusion), kind=kLoop, calls=%fused_computation.4 | loop fusion | bytes 1024 | tf_op jit(solution)/shard_map/slice | solution.py:185
  34.5 0.3 collective-permute-start.8
  34.8 0.8 %collective-permute-done.8.other = f32[1,64]{1,0:T(1,128)S(1)} collective-permute-done((f32[1,64]{1,0:T(1,128)S(1)}, f32[1,64]{1,0:T(1,128)S(1)}, u32[]{:S(2)}, u32[]{:S(2)}) %collective-permute-start.8) | collective-permute-done | bytes 288 | tf_op jit(solution)/shard_map/ppermute | solution.py:139
  35.6 0.0 copy-start.2
  35.6 0.6 %copy-done.2 = f32[1,64]{1,0:T(1,128)} copy-done((f32[1,64]{1,0:T(1,128)}, f32[1,64]{1,0:T(1,128)S(1)}, u32[]{:S(2)}) %copy-start.2) | copy-done | bytes 280
  36.2 1.6 %finish.1 = (f32[1,512]{1,0:T(1,128)}, f32[1,512]{1,0:T(1,128)}) custom-call(f32[1,64]{1,0:T(1,128)} %get-tuple-element.19.own, f32[1,64]{1,0:T(1,128)} %copy-done.2, f32[1,512]{1,0:T(1,128)} %get-tuple-element.14.base, f32[1,512]{1,0:T(1,128)} %bitcast.7, bf16[64,512]{1,0:T(8,128)(2,1)} %get-tuple-element.15.spots), custom_call_target="tpu_custom_call" | custom-call | tf_op jit(solution)/shard_map/finish/pallas_call | solution.py:188
  (5 shorter events, 0.0 us)
Async XLA Ops:
  4.8 6.5 %copy-start.1 = (bf16[64,128]{1,0:T(8,128)(2,1)S(1)}, bf16[64,128]{1,0:T(8,128)(2,1)}, u32[]{:S(2)}) copy-start(bf16[64,128]{1,0:T(8,128)(2,1)} %get-tuple-element.10) | copy-start | bytes 49156
  4.8 1.5 %collective-permute-start = (bf16[64,128]{1,0:T(8,128)(2,1)}, bf16[64,128]{1,0:T(8,128)(2,1)S(1)}, u32[]{:S(2)}, u32[]{:S(2)}) collective-permute-start(bf16[64,128]{1,0:T(8,128)(2,1)} %get-tuple-element.10), channel_id=1, source_target_pairs={{0,1},{1,0},{2,3},{3,2},{4,5},{5,4},{6,7},{7,6},{8,9},{9,8},{10,11... | collective-permute-start | bytes 49160 | tf_op jit(solution)/shard_map/ppermute | solution.py:139
  7.0 7.1 %copy-start = (bf16[80,512]{1,0:T(8,128)(2,1)S(1)}, bf16[80,512]{1,0:T(8,128)(2,1)}, u32[]{:S(2)}) copy-start(bf16[80,512]{1,0:T(8,128)(2,1)} %get-tuple-element.11.refs_0_) | copy-start | bytes 245764
  7.0 4.3 %collective-permute-start.1 = (bf16[128,128]{1,0:T(8,128)(2,1)S(1)}, bf16[128,128]{1,0:T(8,128)(2,1)S(1)}, u32[]{:S(2)}, u32[]{:S(2)}) collective-permute-start(bf16[128,128]{1,0:T(8,128)(2,1)S(1)} %pad_maximum_fusion.2), channel_id=1, source_target_pairs={{0,5},{1,4},{2,7},{3,6},{4,1},{5,0},{6,3},{7,2},{8,13},{9,12},{10,... | collective-permute-start | bytes 98312 | tf_op jit(solution)/shard_map/ppermute | solution.py:139
  9.7 5.9 %collective-permute-start.3 = (bf16[80,512]{1,0:T(8,128)(2,1)}, bf16[80,512]{1,0:T(8,128)(2,1)S(1)}, u32[]{:S(2)}, u32[]{:S(2)}) collective-permute-start(bf16[80,512]{1,0:T(8,128)(2,1)} %get-tuple-element.11.refs_0_), channel_id=1, source_target_pairs={{0,17},{1,16},{2,19},{3,18},{4,21},{5,20},{6,23},{7,22},{8,25},{9,... | collective-permute-start | bytes 245768 | tf_op jit(solution)/shard_map/ppermute | solution.py:139
  11.3 5.0 %collective-permute-start.2 = (bf16[256,128]{1,0:T(8,128)(2,1)S(1)}, bf16[256,128]{1,0:T(8,128)(2,1)S(1)}, u32[]{:S(2)}, u32[]{:S(2)}) collective-permute-start(bf16[256,128]{1,0:T(8,128)(2,1)S(1)} %pad_maximum_fusion.1), channel_id=1, source_target_pairs={{0,9},{1,8},{2,11},{3,10},{4,13},{5,12},{6,15},{7,14},{8,1},{9,0},... | collective-permute-start | bytes 196616 | tf_op jit(solution)/shard_map/ppermute | solution.py:139
  14.1 4.3 %collective-permute-start.4 = (bf16[80,512]{1,0:T(8,128)(2,1)S(1)}, bf16[80,512]{1,0:T(8,128)(2,1)S(1)}, u32[]{:S(2)}, u32[]{:S(2)}) collective-permute-start(bf16[80,512]{1,0:T(8,128)(2,1)S(1)} %copy-done), channel_id=1, source_target_pairs={{0,3},{1,2},{2,1},{3,0},{4,7},{5,6},{6,5},{7,4},{8,11},{9,10},{10,... | collective-permute-start | bytes 245768 | tf_op jit(solution)/shard_map/ppermute | solution.py:139
  15.6 4.7 %collective-permute-start.5 = (bf16[80,512]{1,0:T(8,128)(2,1)S(1)}, bf16[80,512]{1,0:T(8,128)(2,1)S(1)}, u32[]{:S(2)}, u32[]{:S(2)}) collective-permute-start(bf16[80,512]{1,0:T(8,128)(2,1)S(1)} %collective-permute-done.3.refs_1_), channel_id=1, source_target_pairs={{0,3},{1,2},{2,1},{3,0},{4,7},{5,6},{6,5},{7,4},{8,11},{9,10},{10,... | collective-permute-start | bytes 245768 | tf_op jit(solution)/shard_map/ppermute | solution.py:139
  27.1 3.9 %collective-permute-start.6 = (f32[1,256]{1,0:T(1,128)S(1)}, f32[1,256]{1,0:T(1,128)S(1)}, u32[]{:S(2)}, u32[]{:S(2)}) collective-permute-start(f32[1,256]{1,0:T(1,128)S(1)} %get-tuple-element.13), channel_id=1, source_target_pairs={{0,9},{1,8},{2,11},{3,10},{4,13},{5,12},{6,15},{7,14},{8,1},{9,0},... | collective-permute-start | bytes 3080 | tf_op jit(solution)/shard_map/ppermute | solution.py:139
  31.0 3.0 %collective-permute-start.7 = (f32[1,128]{1,0:T(1,128)S(1)}, f32[1,128]{1,0:T(1,128)S(1)}, u32[]{:S(2)}, u32[]{:S(2)}) collective-permute-start(f32[1,128]{1,0:T(1,128)S(1)} %slice.17), channel_id=1, source_target_pairs={{0,5},{1,4},{2,7},{3,6},{4,1},{5,0},{6,3},{7,2},{8,13},{9,12},{10,... | collective-permute-start | bytes 1544 | tf_op jit(solution)/shard_map/ppermute | solution.py:139
  34.5 1.1 %collective-permute-start.8 = (f32[1,64]{1,0:T(1,128)S(1)}, f32[1,64]{1,0:T(1,128)S(1)}, u32[]{:S(2)}, u32[]{:S(2)}) collective-permute-start(f32[1,64]{1,0:T(1,128)S(1)} %get-tuple-element.18), channel_id=1, source_target_pairs={{0,1},{1,0},{2,3},{3,2},{4,5},{5,4},{6,7},{7,6},{8,9},{9,8},{10,11... | collective-permute-start | bytes 776 | tf_op jit(solution)/shard_map/ppermute | solution.py:139
  35.6 0.6 %copy-start.2 = (f32[1,64]{1,0:T(1,128)}, f32[1,64]{1,0:T(1,128)S(1)}, u32[]{:S(2)}) copy-start(f32[1,64]{1,0:T(1,128)S(1)} %collective-permute-done.8.other) | copy-start | bytes 772

commit v2 on v1

--- a/solution.py
+++ b/solution.py
@@ -26,39 +26,53 @@
     return high, middle, low
 
 
-def prepare_kernel(points, coef, velocity, targets, batch, count, payload, rows, base, spots):
-    size, feats = points.shape
+def prepare_kernel(
+    points, coef, velocity, targets, batch, count, payload, rows, base, spots, *scratch
+):
+    held, sems = scratch[:-1], scratch[-1]
+    copies = [
+        pltpu.make_async_copy(source, here, sems.at[k])
+        for k, (source, here) in enumerate(zip((points, batch, coef, velocity, targets, count), held))
+    ]
+    for copy in copies:
+        copy.start()
+    points, batch, coef, velocity, targets, count = held
+    feats, size = points.shape
     slots = batch.shape[1]
-    preview = coef[...] + MOMENTUM * velocity[...]
-    eye = (
-        lax.broadcasted_iota(jnp.int32, (feats, feats), 0)
-        == lax.broadcasted_iota(jnp.int32, (feats, feats), 1)
-    ).astype(BF16)
-    turned = lax.dot_general(
-        eye, points[...], (((1,), (1,)), ((), ())), preferred_element_type=F32
-    )
-    col_sq = jnp.sum(turned * turned, axis=0, keepdims=True)
-    line = lax.broadcasted_iota(jnp.int32, (EXTRA, size), 0)
-    extra = jnp.where((line >= ONE_AT) & (line < ONE_AT + 3), 1.0, 0.0)
-    for at, parts in ((SQ_AT, pieces(col_sq)), (COEF_AT, pieces(preview))):
-        for k, part in enumerate(parts):
-            extra = jnp.where(line == at + k, part, extra)
-    payload[...] = jnp.concatenate([turned, extra], axis=0).astype(BF16)
+    copies[1].wait()
     diagonal = lax.broadcasted_iota(jnp.int32, (slots, slots), 0) == lax.broadcasted_iota(
         jnp.int32, (slots, slots), 1
     )
     column = jnp.sum(jnp.where(diagonal, batch[...].astype(F32), 0.0), axis=1, keepdims=True)
     place = lax.broadcasted_iota(jnp.int32, (slots, size), 1)
     chosen = place == column.astype(jnp.int32)
-    picked = jnp.dot(jnp.where(chosen, 1.0, 0.0).astype(BF16), points[...], preferred_element_type=F32)
+    copies[0].wait()
+    feature = points[...]
+    picked = lax.dot_general(
+        jnp.where(chosen, 1.0, 0.0).astype(BF16),
+        feature,
+        (((1,), (1,)), ((), ())),
+        preferred_element_type=F32,
+    )
     row_sq = jnp.sum(picked * picked, axis=1, keepdims=True)
     lane = lax.broadcasted_iota(jnp.int32, (slots, feats), 1)
     tail = jnp.where((lane >= SQ_AT) & (lane < SQ_AT + 3), 1.0, 0.0)
     for k, part in enumerate(pieces(row_sq)):
         tail = jnp.where(lane == ONE_AT + k, part, tail)
     rows[...] = jnp.concatenate([-2.0 * picked, tail], axis=1).astype(BF16)
-    live = lax.broadcasted_iota(jnp.int32, (slots, size), 0) < count[0, 0]
-    hits = jnp.where(chosen & live, 1.0, 0.0)
+    payload[:feats, :] = feature
+    col_sq = jnp.sum(jnp.square(feature.astype(F32)), axis=0, keepdims=True)
+    for copy in copies[2:]:
+        copy.wait()
+    preview = coef[...] + MOMENTUM * velocity[...]
+    line = lax.broadcasted_iota(jnp.int32, (EXTRA, size), 0)
+    extra = jnp.where((line >= ONE_AT) & (line < ONE_AT + 3), 1.0, 0.0)
+    for at, parts in ((SQ_AT, pieces(col_sq)), (COEF_AT, pieces(preview))):
+        for k, part in enumerate(parts):
+            extra = jnp.where(line == at + k, part, extra)
+    payload[feats:, :] = extra.astype(BF16)
+    live = lax.broadcasted_iota(jnp.int32, (slots, 1), 0) < count[...]
+    hits = jnp.where(place == jnp.where(live, column, -1.0).astype(jnp.int32), 1.0, 0.0)
     spots[...] = hits.astype(BF16)
     times = jnp.sum(hits, axis=0, keepdims=True)
     base[...] = MOMENTUM * velocity[...] - STEP_SIZE * (
@@ -69,7 +83,7 @@
 def sums_kernel(rows, *refs, feats):
     payloads, (keep, send, total) = refs[:-3], refs[-3:]
     depth = feats + EXTRA
-    group = 64
+    group = min(rows.shape[0], 512)
     total[...] = jnp.zeros_like(total)
     lane = lax.broadcasted_iota(jnp.int32, (8, depth), 1)
     pick_coef = jnp.where((lane >= feats + COEF_AT) & (lane < feats + COEF_AT + 3), 1.0, 0.0).astype(BF16)
@@ -95,16 +109,11 @@
                     part = part + value[:, lanes : lanes + 128]
                 total[pl.ds(start + at, 8), :] += part
 
-    flat = lax.dot_general(
-        jnp.ones((8, 128), F32),
-        total[...],
-        (((1,), (1,)), ((), ())),
-        precision=lax.Precision.HIGHEST,
-        preferred_element_type=F32,
-    )
     half = keep.shape[1]
-    keep[...] = flat[:1, :half]
-    send[...] = flat[:1, half:]
+    for out, first in ((keep, 0), (send, half)):
+        for at in range(0, half, 128):
+            turned = total[first + at : first + at + 128, :].T
+            out[:, at : at + 128] = jnp.sum(turned, axis=0, keepdims=True)
 
 
 def finish_kernel(own, other, base, coef, spots, new_coef, new_velocity):
@@ -142,23 +151,29 @@
     row_steps = [(0, 1)] + [(0, (1 << k) + 1) for k in range(2, n_stripe.bit_length() - 1)]
 
     coef = coefficients.reshape(1, size)
+    line, spot = (1, size), (1, slots)
+    held = [(feats, size), spot, line, line, line, (1, 1)]
+    held_types = [BF16, jnp.int32, F32, F32, F32, jnp.int32]
     payload, rows, base, spots = pl.pallas_call(
         prepare_kernel,
         out_shape=[
             jax.ShapeDtypeStruct((feats + EXTRA, size), BF16),
             jax.ShapeDtypeStruct((slots, 2 * feats), BF16),
-            jax.ShapeDtypeStruct((1, size), F32),
+            jax.ShapeDtypeStruct(line, F32),
             jax.ShapeDtypeStruct((slots, size), BF16),
         ],
-        in_specs=vmem(5) + [pl.BlockSpec(memory_space=pltpu.SMEM)],
+        in_specs=[pl.BlockSpec(memory_space=pltpu.HBM)] * 6,
         out_specs=vmem(4),
+        scratch_shapes=[pltpu.VMEM(s, t) for s, t in zip(held, held_types)]
+        + [pltpu.SemaphoreType.DMA((6,))],
+        compiler_params=pltpu.CompilerParams(vmem_limit_bytes=8 << 20),
         name="prepare",
     )(
-        points,
+        points.T,
         coef,
-        velocity.reshape(1, size),
-        targets.reshape(1, size),
-        batch_rows.reshape(1, slots),
+        velocity.reshape(line),
+        targets.reshape(line),
+        batch_rows.reshape(spot),
         counts,
     )
 
@@ -175,7 +190,7 @@
         in_specs=vmem(1 + len(payloads)),
         out_specs=vmem(2),
         scratch_shapes=[pltpu.VMEM((2 * half, 128), F32)],
-        compiler_params=pltpu.CompilerParams(vmem_limit_bytes=32 << 20),
+        compiler_params=pltpu.CompilerParams(vmem_limit_bytes=24 << 20),
         name="kernel_sums",
     )(rows, *payloads)
 
@@ -190,6 +205,7 @@
         out_shape=[jax.ShapeDtypeStruct((1, size), F32)] * 2,
         in_specs=vmem(5),
         out_specs=vmem(2),
+        compiler_params=pltpu.CompilerParams(vmem_limit_bytes=8 << 20),
         name="finish",
     )(keep, other, base, coef, spots)
     return new_coef.reshape(size), new_velocity.reshape(size)

time: 38.1 us -> 29 us (0.76)
  Pallas kernels: 10.3 us -> 3.24 us
  local copies, waits for them, and re-layouts: 2.69 us -> 1.6 us
  other arithmetic: 0.74 us -> 0.03 us
    pallas_call x1, Pallas kernels: 6.75 us -> 1.88 us  [per_device(): pl.pallas_call(functools.partial(sums_kernel, feats=feats), out_shape=[ja...]
    pallas_call x1, Pallas kernels: 1.92 us -> 0.63 us  [per_device(): pl.pallas_call(prepare_kernel, out_shape=[jax.ShapeDtypeStruct((feats + E...]
    pallas_call x1, Pallas kernels: 1.59 us -> 0.73 us  [per_device(): pl.pallas_call(finish_kernel, out_shape=[jax.ShapeDtypeStruct((1, size),...]
    concatenate x3, other arithmetic: 0.73 us -> 0.02 us  [per_device(): rows = jnp.concatenate([rows, exchange(rows, step)], axis=0)]
    unnamed x7 -> x10, local copies, waits for them, and re-layouts: 2.18 us -> 1.52 us
    slice x2, local copies, waits for them, and re-layouts: 0.51 us -> 0.08 us  [per_device(): keep, send = (both[:, :half], both[:, half:])]
where the time goes in v2:
time: 29 us; the launch traced here: 28.8 us
  starting transfers between devices  11.7 us (40%)
  waiting for transfers between devices  11 us (38%)
  Pallas kernels  3.24 us (11%)
  local copies, waits for them, and re-layouts  1.6 us (6%)
  between operations  1.34 us (5%)
    ppermute x9, starting transfers between devices, exchange(): return lax.ppermute(value, AXES, pairs)  11.7 us
    ppermute x9, waiting for transfers between devices, exchange(): return lax.ppermute(value, AXES, pairs)  11 us
    pallas_call x1, Pallas kernels, per_device(): pl.pallas_call(functools.partial(sums_kernel, feats=feats), out_shape=[ja...  1.88 us
    unnamed x10, local copies, waits for them, and re-layouts  1.52 us
    pallas_call x1, Pallas kernels, per_device(): pl.pallas_call(finish_kernel, out_shape=[jax.ShapeDtypeStruct((1, size),...  0.73 us
    pallas_call x1, Pallas kernels, per_device(): pl.pallas_call(prepare_kernel, out_shape=[jax.ShapeDtypeStruct((feats + E...  0.63 us
  transfers between devices with their start and end apart: 9, of which 8 were waited for; matrix products, arithmetic and copies ran while one was open for 0% of the time, Pallas kernels for 0%

profile of v2, /device:TPU:0, one launch (start us, length us, event | category | flops | bytes accessed | tf_op | source)
XLA Modules:
  0.0 28.8 jit_solution(6546726052224477940)
XLA Ops:
  1.3 0.0 copy-start.3
  1.3 0.0 copy-start.2
  1.3 0.0 copy-start.1
  1.3 0.0 copy-start.4
  1.3 0.6 %copy-done.3 = f32[512]{0:T(512)S(1)} copy-done((f32[512]{0:T(512)S(1)}, f32[512]{0:T(512)}, u32[]{:S(2)}) %copy-start.3) | copy-done | bytes 2072
  2.0 0.0 copy-done.2
  2.0 0.0 copy-done.1
  2.0 0.0 copy-done.4
  2.0 0.0 copy-start
  2.0 0.8 %copy-done = bf16[512,64]{0,1:T(8,128)(2,1)S(1)} copy-done((bf16[512,64]{0,1:T(8,128)(2,1)S(1)}, bf16[512,64]{0,1:T(8,128)(2,1)}, u32[]{:S(2)}) %copy-start) | copy-done | bytes 65560
  2.8 0.6 %prepare.1 = (bf16[80,512]{1,0:T(8,128)(2,1)S(1)}, bf16[64,128]{1,0:T(8,128)(2,1)S(1)}, f32[1,512]{1,0:T(1,128)S(1)}, bf16[64,512]{1,0:T(8,128)(2,1)S(1)}) custom-call(bf16[64,512]{1,0:T(8,128)(2,1)S(1)} %bitcast.7, f32[1,512]{1,0:T(1,128)S(1)} %bitcast.8, f32[1,512]{1,0:T(1,128)S(1)} %bitcast.10, f32[1,512]{1,0:T(1,128)S(1)} %bitcast.11, ...), custom_call_target="tpu_custom_call" | custom-call | tf_op jit(solution)/shard_map/prepare/pallas_call | solution.py:157
  3.5 0.5 %collective-permute-start = (bf16[64,128]{1,0:T(8,128)(2,1)S(1)}, bf16[64,128]{1,0:T(8,128)(2,1)S(1)}, u32[]{:S(2)}, u32[]{:S(2)}) collective-permute-start(bf16[64,128]{1,0:T(8,128)(2,1)S(1)} %get-tuple-element.10), channel_id=1, source_target_pairs={{0,1},{1,0},{2,3},{3,2},{4,5},{5,4},{6,7},{7,6},{8,9},{9,8},{10,11... | collective-permute-start | bytes 49160 | tf_op jit(solution)/shard_map/ppermute | solution.py:148
  4.0 0.8 %collective-permute-done = bf16[64,128]{1,0:T(8,128)(2,1)S(1)} collective-permute-done((bf16[64,128]{1,0:T(8,128)(2,1)S(1)}, bf16[64,128]{1,0:T(8,128)(2,1)S(1)}, u32[]{:S(2)}, u32[]{:S(2)}) %collective-permute-start) | collective-permute-done | bytes 16416 | tf_op jit(solution)/shard_map/ppermute | solution.py:148
  4.8 2.7 %collective-permute-start.1 = (bf16[128,128]{1,0:T(8,128)(2,1)S(1)}, bf16[128,128]{1,0:T(8,128)(2,1)S(1)}, u32[]{:S(2)}, u32[]{:S(2)}) collective-permute-start(bf16[128,128]{1,0:T(8,128)(2,1)S(1)} %pad_maximum_fusion.2), channel_id=1, source_target_pairs={{0,5},{1,4},{2,7},{3,6},{4,1},{5,0},{6,3},{7,2},{8,13},{9,12},{10,... | collective-permute-start | bytes 98312 | tf_op jit(solution)/shard_map/ppermute | solution.py:148
  7.5 1.4 %collective-permute-start.3 = (bf16[80,512]{1,0:T(8,128)(2,1)S(1)}, bf16[80,512]{1,0:T(8,128)(2,1)S(1)}, u32[]{:S(2)}, u32[]{:S(2)}) collective-permute-start(bf16[80,512]{1,0:T(8,128)(2,1)S(1)} %get-tuple-element.11.refs_0_), channel_id=1, source_target_pairs={{0,17},{1,16},{2,19},{3,18},{4,21},{5,20},{6,23},{7,22},{8,25},{9,... | collective-permute-start | bytes 245768 | tf_op jit(solution)/shard_map/ppermute | solution.py:148
  9.0 0.2 collective-permute-done.1
  9.1 2.8 %collective-permute-start.2 = (bf16[256,128]{1,0:T(8,128)(2,1)S(1)}, bf16[256,128]{1,0:T(8,128)(2,1)S(1)}, u32[]{:S(2)}, u32[]{:S(2)}) collective-permute-start(bf16[256,128]{1,0:T(8,128)(2,1)S(1)} %pad_maximum_fusion.1), channel_id=1, source_target_pairs={{0,9},{1,8},{2,11},{3,10},{4,13},{5,12},{6,15},{7,14},{8,1},{9,0},... | collective-permute-start | bytes 196616 | tf_op jit(solution)/shard_map/ppermute | solution.py:148
  11.9 1.5 %collective-permute-start.4 = (bf16[80,512]{1,0:T(8,128)(2,1)S(1)}, bf16[80,512]{1,0:T(8,128)(2,1)S(1)}, u32[]{:S(2)}, u32[]{:S(2)}) collective-permute-start(bf16[80,512]{1,0:T(8,128)(2,1)S(1)} %get-tuple-element.11.refs_0_), channel_id=1, source_target_pairs={{0,3},{1,2},{2,1},{3,0},{4,7},{5,6},{6,5},{7,4},{8,11},{9,10},{10,... | collective-permute-start | bytes 245768 | tf_op jit(solution)/shard_map/ppermute | solution.py:148
  13.3 0.0 collective-permute-done.3.refs_1_
  13.4 0.3 collective-permute-start.5
  13.6 0.4 %collective-permute-done.2 = bf16[256,128]{1,0:T(8,128)(2,1)S(1)} collective-permute-done((bf16[256,128]{1,0:T(8,128)(2,1)S(1)}, bf16[256,128]{1,0:T(8,128)(2,1)S(1)}, u32[]{:S(2)}, u32[]{:S(2)}) %collective-permute-start.2) | collective-permute-done | bytes 65568 | tf_op jit(solution)/shard_map/ppermute | solution.py:148
  14.1 2.1 %collective-permute-done.4.refs_2_ = bf16[80,512]{1,0:T(8,128)(2,1)S(1)} collective-permute-done((bf16[80,512]{1,0:T(8,128)(2,1)S(1)}, bf16[80,512]{1,0:T(8,128)(2,1)S(1)}, u32[]{:S(2)}, u32[]{:S(2)}) %collective-permute-start.4) | collective-permute-done | bytes 81952 | tf_op jit(solution)/shard_map/ppermute | solution.py:148
  16.2 1.9 %collective-permute-done.5.refs_3_ = bf16[80,512]{1,0:T(8,128)(2,1)S(1)} collective-permute-done((bf16[80,512]{1,0:T(8,128)(2,1)S(1)}, bf16[80,512]{1,0:T(8,128)(2,1)S(1)}, u32[]{:S(2)}, u32[]{:S(2)}) %collective-permute-start.5) | collective-permute-done | bytes 81952 | tf_op jit(solution)/shard_map/ppermute | solution.py:148
  18.1 1.9 %kernel_sums.1 = (f32[1,256]{1,0:T(1,128)S(1)}, f32[1,256]{1,0:T(1,128)S(1)}) custom-call(bf16[512,128]{1,0:T(8,128)(2,1)S(1)} %pad_maximum_fusion.rows, bf16[80,512]{1,0:T(8,128)(2,1)S(1)} %get-tuple-element.11.refs_0_, bf16[80,512]{1,0:T(8,128)(2,1)S(1)} %collective-permute-done.3.refs_1_, bf16[80,512]{1,0:T(8,128)(2,1)S(1)} %collective-permute-done.4.refs_2_, ...), custom_call_target="tpu_custom_call" | custom-call | tf_op jit(solution)/shard_map/kernel_sums/pallas_call | solution.py:187
  20.0 0.5 %collective-permute-start.6 = (f32[1,256]{1,0:T(1,128)S(1)}, f32[1,256]{1,0:T(1,128)S(1)}, u32[]{:S(2)}, u32[]{:S(2)}) collective-permute-start(f32[1,256]{1,0:T(1,128)S(1)} %get-tuple-element.13), channel_id=1, source_target_pairs={{0,9},{1,8},{2,11},{3,10},{4,13},{5,12},{6,15},{7,14},{8,1},{9,0},... | collective-permute-start | bytes 3080 | tf_op jit(solution)/shard_map/ppermute | solution.py:148
  20.5 3.4 %collective-permute-done.6 = f32[1,256]{1,0:T(1,128)S(1)} collective-permute-done((f32[1,256]{1,0:T(1,128)S(1)}, f32[1,256]{1,0:T(1,128)S(1)}, u32[]{:S(2)}, u32[]{:S(2)}) %collective-permute-start.6) | collective-permute-done | bytes 1056 | tf_op jit(solution)/shard_map/ppermute | solution.py:148
  23.9 1.7 %collective-permute-start.7 = (f32[1,128]{1,0:T(1,128)S(1)}, f32[1,128]{1,0:T(1,128)S(1)}, u32[]{:S(2)}, u32[]{:S(2)}) collective-permute-start(f32[1,128]{1,0:T(1,128)S(1)} %slice.17), channel_id=1, source_target_pairs={{0,5},{1,4},{2,7},{3,6},{4,1},{5,0},{6,3},{7,2},{8,13},{9,12},{10,... | collective-permute-start | bytes 1544 | tf_op jit(solution)/shard_map/ppermute | solution.py:148
  25.6 1.3 %collective-permute-done.7 = f32[1,128]{1,0:T(1,128)S(1)} collective-permute-done((f32[1,128]{1,0:T(1,128)S(1)}, f32[1,128]{1,0:T(1,128)S(1)}, u32[]{:S(2)}, u32[]{:S(2)}) %collective-permute-start.7) | collective-permute-done | bytes 544 | tf_op jit(solution)/shard_map/ppermute | solution.py:148
  26.9 0.1 fusion
  27.0 0.3 %collective-permute-start.8 = (f32[1,64]{1,0:T(1,128)S(1)}, f32[1,64]{1,0:T(1,128)S(1)}, u32[]{:S(2)}, u32[]{:S(2)}) collective-permute-start(f32[1,64]{1,0:T(1,128)S(1)} %get-tuple-element.18), channel_id=1, source_target_pairs={{0,1},{1,0},{2,3},{3,2},{4,5},{5,4},{6,7},{7,6},{8,9},{9,8},{10,11... | collective-permute-start | bytes 776 | tf_op jit(solution)/shard_map/ppermute | solution.py:148
  27.3 0.8 %collective-permute-done.8.other = f32[1,64]{1,0:T(1,128)S(1)} collective-permute-done((f32[1,64]{1,0:T(1,128)S(1)}, f32[1,64]{1,0:T(1,128)S(1)}, u32[]{:S(2)}, u32[]{:S(2)}) %collective-permute-start.8) | collective-permute-done | bytes 288 | tf_op jit(solution)/shard_map/ppermute | solution.py:148
  28.1 0.7 %finish.1 = (f32[1,512]{1,0:T(1,128)}, f32[1,512]{1,0:T(1,128)}) custom-call(f32[1,64]{1,0:T(1,128)S(1)} %get-tuple-element.19.own, f32[1,64]{1,0:T(1,128)S(1)} %collective-permute-done.8.other, f32[1,512]{1,0:T(1,128)S(1)} %get-tuple-element.14.base, f32[1,512]{1,0:T(1,128)S(1)} %bitcast.9, bf16[64,512]{1,0:T(8,128)(2,1)S(1)} %get-tuple-element.15.spots), custom_call_target="tpu_custom_call" | custom-call | tf_op jit(solution)/shard_map/finish/pallas_call | solution.py:203
  (6 shorter events, 0.0 us)
Async XLA Ops:
  1.3 0.7 %copy-start.3 = (f32[512]{0:T(512)S(1)}, f32[512]{0:T(512)}, u32[]{:S(2)}) copy-start(f32[512]{0:T(512)} %param.9) | copy-start | bytes 6148
  1.3 0.7 %copy-start.2 = (f32[512]{0:T(512)S(1)}, f32[512]{0:T(512)}, u32[]{:S(2)}) copy-start(f32[512]{0:T(512)} %param.8) | copy-start | bytes 6148
  1.3 0.7 %copy-start.1 = (f32[512]{0:T(512)S(1)}, f32[512]{0:T(512)}, u32[]{:S(2)}) copy-start(f32[512]{0:T(512)} %param.7) | copy-start | bytes 6148
  1.3 0.7 %copy-start.4 = (s32[64]{0:T(128)S(1)}, s32[64]{0:T(128)}, u32[]{:S(2)}) copy-start(s32[64]{0:T(128)} %param.10) | copy-start | bytes 772
  2.0 0.8 %copy-start = (bf16[512,64]{0,1:T(8,128)(2,1)S(1)}, bf16[512,64]{0,1:T(8,128)(2,1)}, u32[]{:S(2)}) copy-start(bf16[512,64]{0,1:T(8,128)(2,1)} %param.6) | copy-start | bytes 196612
  3.5 1.4 %collective-permute-start = (bf16[64,128]{1,0:T(8,128)(2,1)S(1)}, bf16[64,128]{1,0:T(8,128)(2,1)S(1)}, u32[]{:S(2)}, u32[]{:S(2)}) collective-permute-start(bf16[64,128]{1,0:T(8,128)(2,1)S(1)} %get-tuple-element.10), channel_id=1, source_target_pairs={{0,1},{1,0},{2,3},{3,2},{4,5},{5,4},{6,7},{7,6},{8,9},{9,8},{10,11... | collective-permute-start | bytes 49160 | tf_op jit(solution)/shard_map/ppermute | solution.py:148
  4.8 4.3 %collective-permute-start.1 = (bf16[128,128]{1,0:T(8,128)(2,1)S(1)}, bf16[128,128]{1,0:T(8,128)(2,1)S(1)}, u32[]{:S(2)}, u32[]{:S(2)}) collective-permute-start(bf16[128,128]{1,0:T(8,128)(2,1)S(1)} %pad_maximum_fusion.2), channel_id=1, source_target_pairs={{0,5},{1,4},{2,7},{3,6},{4,1},{5,0},{6,3},{7,2},{8,13},{9,12},{10,... | collective-permute-start | bytes 98312 | tf_op jit(solution)/shard_map/ppermute | solution.py:148
  7.5 5.8 %collective-permute-start.3 = (bf16[80,512]{1,0:T(8,128)(2,1)S(1)}, bf16[80,512]{1,0:T(8,128)(2,1)S(1)}, u32[]{:S(2)}, u32[]{:S(2)}) collective-permute-start(bf16[80,512]{1,0:T(8,128)(2,1)S(1)} %get-tuple-element.11.refs_0_), channel_id=1, source_target_pairs={{0,17},{1,16},{2,19},{3,18},{4,21},{5,20},{6,23},{7,22},{8,25},{9,... | collective-permute-start | bytes 245768 | tf_op jit(solution)/shard_map/ppermute | solution.py:148
  9.1 5.0 %collective-permute-start.2 = (bf16[256,128]{1,0:T(8,128)(2,1)S(1)}, bf16[256,128]{1,0:T(8,128)(2,1)S(1)}, u32[]{:S(2)}, u32[]{:S(2)}) collective-permute-start(bf16[256,128]{1,0:T(8,128)(2,1)S(1)} %pad_maximum_fusion.1), channel_id=1, source_target_pairs={{0,9},{1,8},{2,11},{3,10},{4,13},{5,12},{6,15},{7,14},{8,1},{9,0},... | collective-permute-start | bytes 196616 | tf_op jit(solution)/shard_map/ppermute | solution.py:148
  11.9 4.3 %collective-permute-start.4 = (bf16[80,512]{1,0:T(8,128)(2,1)S(1)}, bf16[80,512]{1,0:T(8,128)(2,1)S(1)}, u32[]{:S(2)}, u32[]{:S(2)}) collective-permute-start(bf16[80,512]{1,0:T(8,128)(2,1)S(1)} %get-tuple-element.11.refs_0_), channel_id=1, source_target_pairs={{0,3},{1,2},{2,1},{3,0},{4,7},{5,6},{6,5},{7,4},{8,11},{9,10},{10,... | collective-permute-start | bytes 245768 | tf_op jit(solution)/shard_map/ppermute | solution.py:148
  13.4 4.7 %collective-permute-start.5 = (bf16[80,512]{1,0:T(8,128)(2,1)S(1)}, bf16[80,512]{1,0:T(8,128)(2,1)S(1)}, u32[]{:S(2)}, u32[]{:S(2)}) collective-permute-start(bf16[80,512]{1,0:T(8,128)(2,1)S(1)} %collective-permute-done.3.refs_1_), channel_id=1, source_target_pairs={{0,3},{1,2},{2,1},{3,0},{4,7},{5,6},{6,5},{7,4},{8,11},{9,10},{10,... | collective-permute-start | bytes 245768 | tf_op jit(solution)/shard_map/ppermute | solution.py:148
  20.0 4.0 %collective-permute-start.6 = (f32[1,256]{1,0:T(1,128)S(1)}, f32[1,256]{1,0:T(1,128)S(1)}, u32[]{:S(2)}, u32[]{:S(2)}) collective-permute-start(f32[1,256]{1,0:T(1,128)S(1)} %get-tuple-element.13), channel_id=1, source_target_pairs={{0,9},{1,8},{2,11},{3,10},{4,13},{5,12},{6,15},{7,14},{8,1},{9,0},... | collective-permute-start | bytes 3080 | tf_op jit(solution)/shard_map/ppermute | solution.py:148
  23.9 3.0 %collective-permute-start.7 = (f32[1,128]{1,0:T(1,128)S(1)}, f32[1,128]{1,0:T(1,128)S(1)}, u32[]{:S(2)}, u32[]{:S(2)}) collective-permute-start(f32[1,128]{1,0:T(1,128)S(1)} %slice.17), channel_id=1, source_target_pairs={{0,5},{1,4},{2,7},{3,6},{4,1},{5,0},{6,3},{7,2},{8,13},{9,12},{10,... | collective-permute-start | bytes 1544 | tf_op jit(solution)/shard_map/ppermute | solution.py:148
  27.0 1.1 %collective-permute-start.8 = (f32[1,64]{1,0:T(1,128)S(1)}, f32[1,64]{1,0:T(1,128)S(1)}, u32[]{:S(2)}, u32[]{:S(2)}) collective-permute-start(f32[1,64]{1,0:T(1,128)S(1)} %get-tuple-element.18), channel_id=1, source_target_pairs={{0,1},{1,0},{2,3},{3,2},{4,5},{5,4},{6,7},{7,6},{8,9},{9,8},{10,11... | collective-permute-start | bytes 776 | tf_op jit(solution)/shard_map/ppermute | solution.py:148

commit v3 on v1

v3 whole, which is shorter than its diff:
```python
import functools

import jax
import jax.numpy as jnp
from jax import lax
from jax.experimental import pallas as pl
from jax.experimental.pallas import tpu as pltpu
from jax.sharding import PartitionSpec as P

MOMENTUM = 0.9
STEP_SIZE = 1.0
NOISE_VAR = 8.0
KERNEL_RATE = 3.0**0.5 / 6.0
LOG2_E = 1.4426950408889634
AXES = ("blk", "stripe")
SQ_AT, ONE_AT, COEF_AT, EXTRA = 0, 3, 6, 16

F32, BF16 = jnp.float32, jnp.bfloat16


def pieces(value):
    high = value.astype(BF16).astype(F32)
    rest = value - high
    middle = rest.astype(BF16).astype(F32)
    low = (rest - middle).astype(BF16).astype(F32)
    return high, middle, low


def payload_kernel(points, coef, velocity, batch, payload, slots):
    feats, size = points.shape
    feature = points[...]
    payload[:feats, :] = feature
    slots[...] = batch[...]
    col_sq = jnp.sum(jnp.square(feature.astype(F32)), axis=0, keepdims=True)
    preview = coef[...] + MOMENTUM * velocity[...]
    line = lax.broadcasted_iota(jnp.int32, (EXTRA, size), 0)
    extra = jnp.where((line >= ONE_AT) & (line < ONE_AT + 3), 1.0, 0.0)
    for at, parts in ((SQ_AT, pieces(col_sq)), (COEF_AT, pieces(preview))):
        for k, part in enumerate(parts):
            extra = jnp.where(line == at + k, part, extra)
    payload[feats:, :] = extra.astype(BF16)


def slot_column(batch):
    slots = batch.shape[1]
    diagonal = lax.broadcasted_iota(jnp.int32, (slots, slots), 0) == lax.broadcasted_iota(
        jnp.int32, (slots, slots), 1
    )
    return jnp.sum(jnp.where(diagonal, batch[...].astype(F32), 0.0), axis=1, keepdims=True)


def rows_kernel(batch, payload, rows):
    feats, size = payload.shape[0] - EXTRA, payload.shape[1]
    slots = batch.shape[1]
    place = lax.broadcasted_iota(jnp.int32, (slots, size), 1)
    chosen = place == slot_column(batch).astype(jnp.int32)
    picked = lax.dot_general(
        jnp.where(chosen, 1.0, 0.0).astype(BF16),
        payload[:feats, :],
        (((1,), (1,)), ((), ())),
        preferred_element_type=F32,
    )
    row_sq = jnp.sum(picked * picked, axis=1, keepdims=True)
    lane = lax.broadcasted_iota(jnp.int32, (slots, feats), 1)
    tail = jnp.where((lane >= SQ_AT) & (lane < SQ_AT + 3), 1.0, 0.0)
    for k, part in enumerate(pieces(row_sq)):
        tail = jnp.where(lane == ONE_AT + k, part, tail)
    rows[...] = jnp.concatenate([-2.0 * picked, tail], axis=1).astype(BF16)


def terms_kernel(batch, coef, velocity, targets, base, spots):
    slots, size = spots.shape
    column = slot_column(batch).astype(jnp.int32)
    place = lax.broadcasted_iota(jnp.int32, (slots, size), 1)
    hits = jnp.where(place == column, 1.0, 0.0)
    spots[...] = hits.astype(BF16)
    times = jnp.sum(hits, axis=0, keepdims=True)
    preview = coef[...] + MOMENTUM * velocity[...]
    base[...] = MOMENTUM * velocity[...] - STEP_SIZE * (
        times * (NOISE_VAR * preview - targets[...])
    )


def sums_kernel(rows, *refs, first):
    if first:
        payloads, (sums, weights, total) = refs[:-3], refs[-3:]
    else:
        weights, payloads, (sums, total) = refs[0], refs[1:-2], refs[-2:]
    amount = rows.shape[0]
    depth = payloads[0].shape[0]
    group = min(amount, 256)
    total[...] = jnp.zeros_like(total)
    if first:
        at = depth - EXTRA + COEF_AT
        lane = lax.broadcasted_iota(jnp.int32, (8, depth), 1)
        pick = jnp.where((lane >= at) & (lane < at + 3), 1.0, 0.0).astype(BF16)
        for k, payload in enumerate(payloads):
            weights[8 * k : 8 * k + 8, :] = jnp.dot(
                pick, payload[...], preferred_element_type=F32
            )
    for k, payload in enumerate(payloads):
        block = payload[...]
        weight = weights[8 * k : 8 * k + 8, :]
        scaled_weight = KERNEL_RATE * weight

        @pl.loop(0, amount // group)
        def _(step):
            start = pl.multiple_of(step * group, group)
            squares = jnp.dot(
                rows[pl.ds(start, group), :][:, :depth], block, preferred_element_type=F32
            )
            for at in range(0, group, 8):
                square = jnp.maximum(squares[at : at + 8, :], 1e-30)
                distance = square * lax.rsqrt(square)
                value = jnp.exp2((-KERNEL_RATE * LOG2_E) * distance) * (
                    weight + scaled_weight * distance
                )
                part = value[:, :128]
                for lanes in range(128, value.shape[1], 128):
                    part = part + value[:, lanes : lanes + 128]
                total[pl.ds(start + at, 8), :] += part

    for at in range(0, amount, 128):
        turned = total[at : at + 128, :].T
        sums[:, at : at + 128] = jnp.sum(turned, axis=0, keepdims=True)


def finish_kernel(own, other, base, coef, spots, new_coef, new_velocity):
    slots = spots.shape[0]
    sums = own[...][:, :slots] + other[...]
    line = lax.broadcasted_iota(jnp.int32, (16, slots), 0)
    split = jnp.zeros((16, slots), F32)
    for k, part in enumerate(pieces(sums)):
        split = jnp.where(line == k, part, split)
    update = jnp.dot(split.astype(BF16), spots[...], preferred_element_type=F32)
    velocity = base[...] - STEP_SIZE * jnp.sum(update, axis=0, keepdims=True)
    new_velocity[...] = velocity
    new_coef[...] = coef[...] + velocity


def call(kernel, name, outs, *operands, limit=8 << 20, scratch=(), cost=None):
    return pl.pallas_call(
        kernel,
        out_shape=[jax.ShapeDtypeStruct(shape, kind) for shape, kind in outs],
        in_specs=[pl.BlockSpec(memory_space=pltpu.VMEM)] * len(operands),
        out_specs=[pl.BlockSpec(memory_space=pltpu.VMEM)] * len(outs),
        scratch_shapes=scratch,
        compiler_params=pltpu.CompilerParams(vmem_limit_bytes=limit),
        cost_estimate=cost,
        name=name,
    )(*operands)


def per_device(mesh_shape, points, coefficients, velocity, targets, batch_rows, counts):
    n_blk, n_stripe = mesh_shape["blk"], mesh_shape["stripe"]
    size, feats = points.shape
    slots = batch_rows.shape[0]

    def exchange(value, offset):
        d_blk, d_stripe = offset
        pairs = [
            (b * n_stripe + s, (b ^ d_blk) * n_stripe + (s ^ d_stripe))
            for b in range(n_blk)
            for s in range(n_stripe)
        ]
        return lax.ppermute(value, AXES, pairs)

    point_steps = [(1 << k, 1) for k in range(n_blk.bit_length() - 1)] + [(0, 3)]
    row_steps = [(0, 1)] + [(0, (1 << k) + 1) for k in range(2, n_stripe.bit_length() - 1)]

    line, spot = (1, size), (1, slots)
    coef, velocity, targets = (x.reshape(line) for x in (coefficients, velocity, targets))
    batch = batch_rows.reshape(spot)
    live = lax.broadcasted_iota(jnp.int32, spot, 1) < counts.reshape(1, 1)
    live_batch = jnp.where(live, batch, -1)
    payload, batch = call(
        payload_kernel,
        "payload",
        [((feats + EXTRA, size), BF16), (spot, jnp.int32)],
        points.T,
        coef,
        velocity,
        batch,
    )
    (rows,) = call(rows_kernel, "rows", [((slots, 2 * feats), BF16)], batch, payload)
    own = payload
    for step in row_steps[:-1]:
        rows = jnp.concatenate([rows, exchange(rows, step)], axis=0)
        if step is row_steps[0]:
            own, rows = lax.optimization_barrier((own, rows))
    more_rows = exchange(rows, row_steps[-1])
    payloads = [payload, exchange(payload, point_steps[0])]
    for step in point_steps[1:]:
        payloads = payloads + [exchange(own if k == 0 else p, step) for k, p in enumerate(payloads)]

    half = rows.shape[0]
    amount = half * size * len(payloads)
    options = dict(
        limit=16 << 20,
        scratch=[pltpu.VMEM((half, 128), F32)],
        cost=pl.CostEstimate(
            flops=2 * feats * amount, bytes_accessed=1 << 16, transcendentals=2 * amount
        ),
    )
    keep, weights = call(
        functools.partial(sums_kernel, first=True),
        "sums_here",
        [((1, half), F32), ((8 * len(payloads), size), F32)],
        rows,
        *payloads,
        **options,
    )
    (send,) = call(
        functools.partial(sums_kernel, first=False),
        "sums_away",
        [((1, half), F32)],
        more_rows,
        weights,
        *payloads,
        **options,
    )
    base, spots = call(
        terms_kernel,
        "terms",
        [(line, F32), ((slots, size), BF16)],
        live_batch,
        coef,
        velocity,
        targets,
    )
    keep, base, spots = lax.optimization_barrier((keep, base, spots))

    for step in row_steps[:0:-1]:
        both = keep + exchange(send, step)
        half = half // 2
        keep, send = both[:, :half], both[:, half:]
    other = exchange(send, row_steps[0])

    new_coef, new_velocity = call(
        finish_kernel, "finish", [(line, F32)] * 2, keep, other, base, coef, spots
    )
    return new_coef.reshape(size), new_velocity.reshape(size)


def solution(mesh):
    in_specs = (
        P(("blk", "stripe"), None),
        P(("blk", "stripe")),
        P(("blk", "stripe")),
        P(("blk", "stripe")),
        P(("blk", "stripe")),
        P("blk", "stripe"),
    )
    out_specs = (P(("blk", "stripe")), P(("blk", "stripe")))
    return jax.shard_map(
        functools.partial(per_device, dict(mesh.shape)),
        mesh=mesh,
        in_specs=in_specs,
        out_specs=out_specs,
        check_vma=False,
    )
```

time: 38.1 us -> 26.8 us (0.70)
  Pallas kernels: 10.3 us -> 3.29 us
  waiting for transfers between devices: 11 us -> 7.29 us
  other arithmetic: 0.74 us -> 0.01 us
  starting transfers between devices: 11.8 us -> 12.3 us
  local copies, waits for them, and re-layouts: 2.69 us -> 2.29 us
    pallas_call x3 -> x6, Pallas kernels: 10.3 us -> 3.29 us  [call(): pl.pallas_call(kernel, out_shape=[jax.ShapeDtypeStruct(shape, kind) for s...]
    ppermute x9, waiting for transfers between devices: 11 us -> 7.29 us  [exchange(): return lax.ppermute(value, AXES, pairs)]
    concatenate x3 -> x1, other arithmetic: 0.73 us -> 0.01 us  [per_device(): rows = jnp.concatenate([rows, exchange(rows, step)], axis=0)]
    ppermute x9, starting transfers between devices: 11.8 us -> 12.3 us  [exchange(): return lax.ppermute(value, AXES, pairs)]
    slice x2, local copies, waits for them, and re-layouts: 0.51 us -> 0.08 us  [per_device(): keep, send = (both[:, :half], both[:, half:])]
    unnamed x7 -> x11, local copies, waits for them, and re-layouts: 2.18 us -> 2.2 us
  transfers between devices with their start and end apart: 9 -> 9, of which waited for: 8 -> 5; matrix products, arithmetic and copies ran while one was open for 0% -> 0% of each run, Pallas kernels for 0% -> 4%
where the time goes in v3:
time: 26.8 us; the launch traced here: 26.6 us
  starting transfers between devices  12.3 us (46%)
  waiting for transfers between devices  7.29 us (27%)
  Pallas kernels  3.29 us (12%)
  local copies, waits for them, and re-layouts  2.29 us (9%)
  between operations  1.34 us (5%)
    ppermute x9, starting transfers between devices, exchange(): return lax.ppermute(value, AXES, pairs)  12.3 us
    ppermute x9, waiting for transfers between devices, exchange(): return lax.ppermute(value, AXES, pairs)  7.29 us
    pallas_call x6, Pallas kernels, call(): pl.pallas_call(kernel, out_shape=[jax.ShapeDtypeStruct(shape, kind) for s...  3.29 us
    unnamed x11, local copies, waits for them, and re-layouts  2.2 us
  transfers between devices with their start and end apart: 9, of which 5 were waited for; matrix products, arithmetic and copies ran while one was open for 0% of the time, Pallas kernels for 4%

profile of v3, /device:TPU:0, one launch (start us, length us, event | category | flops | bytes accessed | tf_op | source)
XLA Modules:
  0.0 26.6 jit_solution(14076303769206887710)
XLA Ops:
  0.6 0.0 copy-start.2
  0.6 0.0 copy-start.1
  0.7 0.0 copy-start.4
  0.7 0.7 %copy-done.2 = f32[512]{0:T(512)S(1)} copy-done((f32[512]{0:T(512)S(1)}, f32[512]{0:T(512)}, u32[]{:S(2)}) %copy-start.2) | copy-done | bytes 2072
  1.3 0.0 copy-done.1
  1.3 0.0 copy-done.4
  1.3 0.0 copy-start
  1.3 0.8 %copy-done = bf16[512,64]{0,1:T(8,128)(2,1)S(1)} copy-done((bf16[512,64]{0,1:T(8,128)(2,1)S(1)}, bf16[512,64]{0,1:T(8,128)(2,1)}, u32[]{:S(2)}) %copy-start) | copy-done | bytes 65560
  2.2 0.4 %rows.1 = bf16[64,128]{1,0:T(8,128)(2,1)S(1)} custom-call(s32[1,64]{1,0:T(1,128)S(1)} %get-tuple-element.16.batch, bf16[80,512]{1,0:T(8,128)(2,1)S(1)} %get-tuple-element.18.payload.refs_0_.refs_1_), custom_call_target="tpu_custom_call" | custom-call | tf_op jit(solution)/shard_map/rows/pallas_call | solution.py:142
  2.6 0.5 %collective-permute-start = (bf16[64,128]{1,0:T(8,128)(2,1)S(1)}, bf16[64,128]{1,0:T(8,128)(2,1)S(1)}, u32[]{:S(2)}, u32[]{:S(2)}) collective-permute-start(bf16[64,128]{1,0:T(8,128)(2,1)S(1)} %rows.1), channel_id=1, source_target_pairs={{0,1},{1,0},{2,3},{3,2},{4,5},{5,4},{6,7},{7,6},{8,9},{9,8},{10,11... | collective-permute-start | bytes 49160 | tf_op jit(solution)/shard_map/ppermute | solution.py:166
  3.1 2.6 %collective-permute-start.2 = (bf16[80,512]{1,0:T(8,128)(2,1)S(1)}, bf16[80,512]{1,0:T(8,128)(2,1)S(1)}, u32[]{:S(2)}, u32[]{:S(2)}) collective-permute-start(bf16[80,512]{1,0:T(8,128)(2,1)S(1)} %get-tuple-element.18.payload.refs_0_.refs_1_), channel_id=1, source_target_pairs={{0,17},{1,16},{2,19},{3,18},{4,21},{5,20},{6,23},{7,22},{8,25},{9,... | collective-permute-start | bytes 245768 | tf_op jit(solution)/shard_map/ppermute | solution.py:166
  5.7 0.0 collective-permute-done
  5.7 1.2 %collective-permute-start.1 = (bf16[128,128]{1,0:T(8,128)(2,1)S(1)}, bf16[128,128]{1,0:T(8,128)(2,1)S(1)}, u32[]{:S(2)}, u32[]{:S(2)}) collective-permute-start(bf16[128,128]{1,0:T(8,128)(2,1)S(1)} %pad_maximum_fusion), channel_id=1, source_target_pairs={{0,5},{1,4},{2,7},{3,6},{4,1},{5,0},{6,3},{7,2},{8,13},{9,12},{10,... | collective-permute-start | bytes 98312 | tf_op jit(solution)/shard_map/ppermute | solution.py:166
  7.0 1.6 %collective-permute-start.3 = (bf16[80,512]{1,0:T(8,128)(2,1)S(1)}, bf16[80,512]{1,0:T(8,128)(2,1)S(1)}, u32[]{:S(2)}, u32[]{:S(2)}) collective-permute-start(bf16[80,512]{1,0:T(8,128)(2,1)S(1)} %get-tuple-element.18.payload.refs_0_.refs_1_), channel_id=1, source_target_pairs={{0,3},{1,2},{2,1},{3,0},{4,7},{5,6},{6,5},{7,4},{8,11},{9,10},{10,... | collective-permute-start | bytes 245768 | tf_op jit(solution)/shard_map/ppermute | solution.py:166
  8.5 0.0 collective-permute-done.2.refs_1_.refs_2_
  8.5 1.6 %collective-permute-start.4 = (bf16[80,512]{1,0:T(8,128)(2,1)S(1)}, bf16[80,512]{1,0:T(8,128)(2,1)S(1)}, u32[]{:S(2)}, u32[]{:S(2)}) collective-permute-start(bf16[80,512]{1,0:T(8,128)(2,1)S(1)} %collective-permute-done.2.refs_1_.refs_2_), channel_id=1, source_target_pairs={{0,3},{1,2},{2,1},{3,0},{4,7},{5,6},{6,5},{7,4},{8,11},{9,10},{10,... | collective-permute-start | bytes 245768 | tf_op jit(solution)/shard_map/ppermute | solution.py:166
  10.2 0.0 collective-permute-done.1
  10.2 2.1 %collective-permute-start.5 = (bf16[256,128]{1,0:T(8,128)(2,1)S(1)}, bf16[256,128]{1,0:T(8,128)(2,1)S(1)}, u32[]{:S(2)}, u32[]{:S(2)}) collective-permute-start(bf16[256,128]{1,0:T(8,128)(2,1)S(1)} %constant_dynamic-update-slice_fusion.rows), channel_id=1, source_target_pairs={{0,9},{1,8},{2,11},{3,10},{4,13},{5,12},{6,15},{7,14},{8,1},{9,0},... | collective-permute-start | bytes 196616 | tf_op jit(solution)/shard_map/ppermute | solution.py:166
  12.9 0.0 collective-permute-done.3.refs_2_.refs_3_
  12.9 0.4 %collective-permute-done.4.refs_3_.refs_4_ = bf16[80,512]{1,0:T(8,128)(2,1)S(1)} collective-permute-done((bf16[80,512]{1,0:T(8,128)(2,1)S(1)}, bf16[80,512]{1,0:T(8,128)(2,1)S(1)}, u32[]{:S(2)}, u32[]{:S(2)}) %collective-permute-start.4) | collective-permute-done | bytes 81952 | tf_op jit(solution)/shard_map/ppermute | solution.py:166
  13.3 1.0 %sums_here.1 = (f32[1,256]{1,0:T(1,128)S(1)}, f32[32,512]{1,0:T(8,128)S(1)}) custom-call(bf16[256,128]{1,0:T(8,128)(2,1)S(1)} %constant_dynamic-update-slice_fusion.rows, bf16[80,512]{1,0:T(8,128)(2,1)S(1)} %get-tuple-element.18.payload.refs_0_.refs_1_, bf16[80,512]{1,0:T(8,128)(2,1)S(1)} %collective-permute-done.2.refs_1_.refs_2_, ...), custom_call_target="tpu_custom_call" | custom-call | flops 67108864 | bytes 65536 | tf_op jit(solution)/shard_map/sums_here/pallas_call | solution.py:142
  14.3 2.4 %collective-permute-done.5.rows = bf16[256,128]{1,0:T(8,128)(2,1)S(1)} collective-permute-done((bf16[256,128]{1,0:T(8,128)(2,1)S(1)}, bf16[256,128]{1,0:T(8,128)(2,1)S(1)}, u32[]{:S(2)}, u32[]{:S(2)}) %collective-permute-start.5) | collective-permute-done | bytes 65568 | tf_op jit(solution)/shard_map/ppermute | solution.py:166
  16.7 1.0 %sums_away.1 = f32[1,256]{1,0:T(1,128)S(1)} custom-call(bf16[256,128]{1,0:T(8,128)(2,1)S(1)} %collective-permute-done.5.rows, f32[32,512]{1,0:T(8,128)S(1)} %get-tuple-element.23.refs_0_, bf16[80,512]{1,0:T(8,128)(2,1)S(1)} %get-tuple-element.18.payload.refs_0_.refs_1_, bf16[80,512]{1,0:T(8,128)(2,1)S(1)} %collective-permute-done.2.refs_1_.refs_2_, ...), custom_call_target="tpu_custom_call" | custom-call | flops 67108864 | bytes 65536 | tf_op jit(solution)/shard_map/sums_away/pallas_call | solution.py:142
  17.7 1.2 %collective-permute-start.6 = (f32[1,256]{1,0:T(1,128)S(1)}, f32[1,256]{1,0:T(1,128)S(1)}, u32[]{:S(2)}, u32[]{:S(2)}) collective-permute-start(f32[1,256]{1,0:T(1,128)S(1)} %sums_away.1), channel_id=1, source_target_pairs={{0,9},{1,8},{2,11},{3,10},{4,13},{5,12},{6,15},{7,14},{8,1},{9,0},... | collective-permute-start | bytes 3080 | tf_op jit(solution)/shard_map/ppermute | solution.py:166
  18.9 0.0 copy-start.3
  18.9 0.7 %copy-done.3 = f32[512]{0:T(512)S(1)} copy-done((f32[512]{0:T(512)S(1)}, f32[512]{0:T(512)}, u32[]{:S(2)}) %copy-start.3) | copy-done | bytes 2072
  19.6 0.1 terms.1
  19.7 2.0 %collective-permute-done.6 = f32[1,256]{1,0:T(1,128)S(1)} collective-permute-done((f32[1,256]{1,0:T(1,128)S(1)}, f32[1,256]{1,0:T(1,128)S(1)}, u32[]{:S(2)}, u32[]{:S(2)}) %collective-permute-start.6) | collective-permute-done | bytes 1056 | tf_op jit(solution)/shard_map/ppermute | solution.py:166
  21.7 1.4 %collective-permute-start.7 = (f32[1,128]{1,0:T(1,128)S(1)}, f32[1,128]{1,0:T(1,128)S(1)}, u32[]{:S(2)}, u32[]{:S(2)}) collective-permute-start(f32[1,128]{1,0:T(1,128)S(1)} %slice.17), channel_id=1, source_target_pairs={{0,5},{1,4},{2,7},{3,6},{4,1},{5,0},{6,3},{7,2},{8,13},{9,12},{10,... | collective-permute-start | bytes 1544 | tf_op jit(solution)/shard_map/ppermute | solution.py:166
  23.1 1.6 %collective-permute-done.7 = f32[1,128]{1,0:T(1,128)S(1)} collective-permute-done((f32[1,128]{1,0:T(1,128)S(1)}, f32[1,128]{1,0:T(1,128)S(1)}, u32[]{:S(2)}, u32[]{:S(2)}) %collective-permute-start.7) | collective-permute-done | bytes 544 | tf_op jit(solution)/shard_map/ppermute | solution.py:166
  24.6 0.1 fusion.1
  24.7 0.1 collective-permute-start.8
  24.8 1.0 %collective-permute-done.8.other = f32[1,64]{1,0:T(1,128)S(1)} collective-permute-done((f32[1,64]{1,0:T(1,128)S(1)}, f32[1,64]{1,0:T(1,128)S(1)}, u32[]{:S(2)}, u32[]{:S(2)}) %collective-permute-start.8) | collective-permute-done | bytes 288 | tf_op jit(solution)/shard_map/ppermute | solution.py:166
  25.8 0.7 %finish.1 = (f32[1,512]{1,0:T(1,128)}, f32[1,512]{1,0:T(1,128)}) custom-call(f32[1,64]{1,0:T(1,128)S(1)} %get-tuple-element.29.own, f32[1,64]{1,0:T(1,128)S(1)} %collective-permute-done.8.other, f32[1,512]{1,0:T(1,128)S(1)} %get-tuple-element.24.base, f32[1,512]{1,0:T(1,128)S(1)} %bitcast.14, bf16[64,512]{1,0:T(8,128)(2,1)S(1)} %get-tuple-element.25.spots), custom_call_target="tpu_custom_call" | custom-call | tf_op jit(solution)/shard_map/finish/pallas_call | solution.py:142
  (8 shorter events, 0.1 us)
Async XLA Ops:
  0.6 0.7 %copy-start.2 = (f32[512]{0:T(512)S(1)}, f32[512]{0:T(512)}, u32[]{:S(2)}) copy-start(f32[512]{0:T(512)} %param.8) | copy-start | bytes 6148
  0.6 0.7 %copy-start.1 = (f32[512]{0:T(512)S(1)}, f32[512]{0:T(512)}, u32[]{:S(2)}) copy-start(f32[512]{0:T(512)} %param.7) | copy-start | bytes 6148
  0.7 0.7 %copy-start.4 = (s32[64]{0:T(128)S(1)}, s32[64]{0:T(128)}, u32[]{:S(2)}) copy-start(s32[64]{0:T(128)} %param.10) | copy-start | bytes 772
  1.3 0.8 %copy-start = (bf16[512,64]{0,1:T(8,128)(2,1)S(1)}, bf16[512,64]{0,1:T(8,128)(2,1)}, u32[]{:S(2)}) copy-start(bf16[512,64]{0,1:T(8,128)(2,1)} %param.6) | copy-start | bytes 196612
  2.6 3.1 %collective-permute-start = (bf16[64,128]{1,0:T(8,128)(2,1)S(1)}, bf16[64,128]{1,0:T(8,128)(2,1)S(1)}, u32[]{:S(2)}, u32[]{:S(2)}) collective-permute-start(bf16[64,128]{1,0:T(8,128)(2,1)S(1)} %rows.1), channel_id=1, source_target_pairs={{0,1},{1,0},{2,3},{3,2},{4,5},{5,4},{6,7},{7,6},{8,9},{9,8},{10,11... | collective-permute-start | bytes 49160 | tf_op jit(solution)/shard_map/ppermute | solution.py:166
  3.1 5.4 %collective-permute-start.2 = (bf16[80,512]{1,0:T(8,128)(2,1)S(1)}, bf16[80,512]{1,0:T(8,128)(2,1)S(1)}, u32[]{:S(2)}, u32[]{:S(2)}) collective-permute-start(bf16[80,512]{1,0:T(8,128)(2,1)S(1)} %get-tuple-element.18.payload.refs_0_.refs_1_), channel_id=1, source_target_pairs={{0,17},{1,16},{2,19},{3,18},{4,21},{5,20},{6,23},{7,22},{8,25},{9,... | collective-permute-start | bytes 245768 | tf_op jit(solution)/shard_map/ppermute | solution.py:166
  5.7 4.4 %collective-permute-start.1 = (bf16[128,128]{1,0:T(8,128)(2,1)S(1)}, bf16[128,128]{1,0:T(8,128)(2,1)S(1)}, u32[]{:S(2)}, u32[]{:S(2)}) collective-permute-start(bf16[128,128]{1,0:T(8,128)(2,1)S(1)} %pad_maximum_fusion), channel_id=1, source_target_pairs={{0,5},{1,4},{2,7},{3,6},{4,1},{5,0},{6,3},{7,2},{8,13},{9,12},{10,... | collective-permute-start | bytes 98312 | tf_op jit(solution)/shard_map/ppermute | solution.py:166
  7.0 5.9 %collective-permute-start.3 = (bf16[80,512]{1,0:T(8,128)(2,1)S(1)}, bf16[80,512]{1,0:T(8,128)(2,1)S(1)}, u32[]{:S(2)}, u32[]{:S(2)}) collective-permute-start(bf16[80,512]{1,0:T(8,128)(2,1)S(1)} %get-tuple-element.18.payload.refs_0_.refs_1_), channel_id=1, source_target_pairs={{0,3},{1,2},{2,1},{3,0},{4,7},{5,6},{6,5},{7,4},{8,11},{9,10},{10,... | collective-permute-start | bytes 245768 | tf_op jit(solution)/shard_map/ppermute | solution.py:166
  8.5 4.7 %collective-permute-start.4 = (bf16[80,512]{1,0:T(8,128)(2,1)S(1)}, bf16[80,512]{1,0:T(8,128)(2,1)S(1)}, u32[]{:S(2)}, u32[]{:S(2)}) collective-permute-start(bf16[80,512]{1,0:T(8,128)(2,1)S(1)} %collective-permute-done.2.refs_1_.refs_2_), channel_id=1, source_target_pairs={{0,3},{1,2},{2,1},{3,0},{4,7},{5,6},{6,5},{7,4},{8,11},{9,10},{10,... | collective-permute-start | bytes 245768 | tf_op jit(solution)/shard_map/ppermute | solution.py:166
  10.2 6.5 %collective-permute-start.5 = (bf16[256,128]{1,0:T(8,128)(2,1)S(1)}, bf16[256,128]{1,0:T(8,128)(2,1)S(1)}, u32[]{:S(2)}, u32[]{:S(2)}) collective-permute-start(bf16[256,128]{1,0:T(8,128)(2,1)S(1)} %constant_dynamic-update-slice_fusion.rows), channel_id=1, source_target_pairs={{0,9},{1,8},{2,11},{3,10},{4,13},{5,12},{6,15},{7,14},{8,1},{9,0},... | collective-permute-start | bytes 196616 | tf_op jit(solution)/shard_map/ppermute | solution.py:166
  17.7 4.0 %collective-permute-start.6 = (f32[1,256]{1,0:T(1,128)S(1)}, f32[1,256]{1,0:T(1,128)S(1)}, u32[]{:S(2)}, u32[]{:S(2)}) collective-permute-start(f32[1,256]{1,0:T(1,128)S(1)} %sums_away.1), channel_id=1, source_target_pairs={{0,9},{1,8},{2,11},{3,10},{4,13},{5,12},{6,15},{7,14},{8,1},{9,0},... | collective-permute-start | bytes 3080 | tf_op jit(solution)/shard_map/ppermute | solution.py:166
  18.9 0.7 %copy-start.3 = (f32[512]{0:T(512)S(1)}, f32[512]{0:T(512)}, u32[]{:S(2)}) copy-start(f32[512]{0:T(512)} %param.9) | copy-start | bytes 6148
  21.7 3.0 %collective-permute-start.7 = (f32[1,128]{1,0:T(1,128)S(1)}, f32[1,128]{1,0:T(1,128)S(1)}, u32[]{:S(2)}, u32[]{:S(2)}) collective-permute-start(f32[1,128]{1,0:T(1,128)S(1)} %slice.17), channel_id=1, source_target_pairs={{0,5},{1,4},{2,7},{3,6},{4,1},{5,0},{6,3},{7,2},{8,13},{9,12},{10,... | collective-permute-start | bytes 1544 | tf_op jit(solution)/shard_map/ppermute | solution.py:166
  24.7 1.1 %collective-permute-start.8 = (f32[1,64]{1,0:T(1,128)S(1)}, f32[1,64]{1,0:T(1,128)S(1)}, u32[]{:S(2)}, u32[]{:S(2)}) collective-permute-start(f32[1,64]{1,0:T(1,128)S(1)} %get-tuple-element.28), channel_id=1, source_target_pairs={{0,1},{1,0},{2,3},{3,2},{4,5},{5,4},{6,7},{7,6},{8,9},{9,8},{10,11... | collective-permute-start | bytes 776 | tf_op jit(solution)/shard_map/ppermute | solution.py:166

commit v4 on v3

--- a/solution.py
+++ b/solution.py
@@ -26,12 +26,22 @@
     return high, middle, low
 
 
-def payload_kernel(points, coef, velocity, batch, payload, slots):
-    feats, size = points.shape
-    feature = points[...]
-    payload[:feats, :] = feature
-    slots[...] = batch[...]
-    col_sq = jnp.sum(jnp.square(feature.astype(F32)), axis=0, keepdims=True)
+def payload_kernel(points, coef, velocity, batch, payload, slots, *scratch):
+    held, sems = scratch[:-1], scratch[-1]
+    feats = points.shape[0]
+    targets = (payload.at[:feats], *held, slots)
+    copies = [
+        pltpu.make_async_copy(source, target, sems.at[k])
+        for k, (source, target) in enumerate(zip((points, coef, velocity, batch), targets))
+    ]
+    for copy in copies:
+        copy.start()
+    for copy in copies:
+        copy.wait()
+    coef, velocity = held
+    size = coef.shape[1]
+    feature = payload[:feats, :].astype(F32)
+    col_sq = jnp.sum(feature * feature, axis=0, keepdims=True)
     preview = coef[...] + MOMENTUM * velocity[...]
     line = lax.broadcasted_iota(jnp.int32, (EXTRA, size), 0)
     extra = jnp.where((line >= ONE_AT) & (line < ONE_AT + 3), 1.0, 0.0)
@@ -41,38 +51,23 @@
     payload[feats:, :] = extra.astype(BF16)
 
 
-def slot_column(batch):
-    slots = batch.shape[1]
-    diagonal = lax.broadcasted_iota(jnp.int32, (slots, slots), 0) == lax.broadcasted_iota(
-        jnp.int32, (slots, slots), 1
-    )
-    return jnp.sum(jnp.where(diagonal, batch[...].astype(F32), 0.0), axis=1, keepdims=True)
-
-
 def rows_kernel(batch, payload, rows):
     feats, size = payload.shape[0] - EXTRA, payload.shape[1]
     slots = batch.shape[1]
-    place = lax.broadcasted_iota(jnp.int32, (slots, size), 1)
-    chosen = place == slot_column(batch).astype(jnp.int32)
-    picked = lax.dot_general(
-        jnp.where(chosen, 1.0, 0.0).astype(BF16),
-        payload[:feats, :],
-        (((1,), (1,)), ((), ())),
-        preferred_element_type=F32,
-    )
-    row_sq = jnp.sum(picked * picked, axis=1, keepdims=True)
-    lane = lax.broadcasted_iota(jnp.int32, (slots, feats), 1)
-    tail = jnp.where((lane >= SQ_AT) & (lane < SQ_AT + 3), 1.0, 0.0)
-    for k, part in enumerate(pieces(row_sq)):
-        tail = jnp.where(lane == ONE_AT + k, part, tail)
-    rows[...] = jnp.concatenate([-2.0 * picked, tail], axis=1).astype(BF16)
+    chosen = lax.broadcasted_iota(jnp.int32, (size, slots), 0) == batch[...]
+    rows[...] = jnp.dot(
+        payload[:feats, :], jnp.where(chosen, 1.0, 0.0).astype(BF16), preferred_element_type=F32
+    ).astype(BF16)
 
 
 def terms_kernel(batch, coef, velocity, targets, base, spots):
     slots, size = spots.shape
-    column = slot_column(batch).astype(jnp.int32)
+    diagonal = lax.broadcasted_iota(jnp.int32, (slots, slots), 0) == lax.broadcasted_iota(
+        jnp.int32, (slots, slots), 1
+    )
+    column = jnp.sum(jnp.where(diagonal, batch[...].astype(F32), 0.0), axis=1, keepdims=True)
     place = lax.broadcasted_iota(jnp.int32, (slots, size), 1)
-    hits = jnp.where(place == column, 1.0, 0.0)
+    hits = jnp.where(place == column.astype(jnp.int32), 1.0, 0.0)
     spots[...] = hits.astype(BF16)
     times = jnp.sum(hits, axis=0, keepdims=True)
     preview = coef[...] + MOMENTUM * velocity[...]
@@ -83,15 +78,23 @@
 
 def sums_kernel(rows, *refs, first):
     if first:
-        payloads, (sums, weights, total) = refs[:-3], refs[-3:]
+        payloads, (sums, weights, total, left) = refs[:-4], refs[-4:]
     else:
-        weights, payloads, (sums, total) = refs[0], refs[1:-2], refs[-2:]
-    amount = rows.shape[0]
-    depth = payloads[0].shape[0]
+        weights, payloads, (sums, total, left) = refs[0], refs[1:-3], refs[-3:]
+    feats, amount = rows.shape
+    depth = feats + EXTRA
     group = min(amount, 256)
+    for at in range(0, amount, group):
+        features = rows[:, at : at + group].astype(F32)
+        norms = jnp.sum(features * features, axis=0, keepdims=True)
+        line = lax.broadcasted_iota(jnp.int32, (128 - feats, group), 0)
+        tail = jnp.where((line >= SQ_AT) & (line < SQ_AT + 3), 1.0, 0.0)
+        for k, part in enumerate(pieces(norms)):
+            tail = jnp.where(line == ONE_AT + k, part, tail)
+        left[at : at + group, :] = jnp.concatenate([-2.0 * features, tail], axis=0).T.astype(BF16)
     total[...] = jnp.zeros_like(total)
     if first:
-        at = depth - EXTRA + COEF_AT
+        at = feats + COEF_AT
         lane = lax.broadcasted_iota(jnp.int32, (8, depth), 1)
         pick = jnp.where((lane >= at) & (lane < at + 3), 1.0, 0.0).astype(BF16)
         for k, payload in enumerate(payloads):
@@ -107,7 +110,7 @@
         def _(step):
             start = pl.multiple_of(step * group, group)
             squares = jnp.dot(
-                rows[pl.ds(start, group), :][:, :depth], block, preferred_element_type=F32
+                left[pl.ds(start, group), :][:, :depth], block, preferred_element_type=F32
             )
             for at in range(0, group, 8):
                 square = jnp.maximum(squares[at : at + 8, :], 1e-30)
@@ -138,11 +141,11 @@
     new_coef[...] = coef[...] + velocity
 
 
-def call(kernel, name, outs, *operands, limit=8 << 20, scratch=(), cost=None):
+def call(kernel, name, outs, *operands, limit=8 << 20, scratch=(), cost=None, space=pltpu.VMEM):
     return pl.pallas_call(
         kernel,
         out_shape=[jax.ShapeDtypeStruct(shape, kind) for shape, kind in outs],
-        in_specs=[pl.BlockSpec(memory_space=pltpu.VMEM)] * len(operands),
+        in_specs=[pl.BlockSpec(memory_space=space)] * len(operands),
         out_specs=[pl.BlockSpec(memory_space=pltpu.VMEM)] * len(outs),
         scratch_shapes=scratch,
         compiler_params=pltpu.CompilerParams(vmem_limit_bytes=limit),
@@ -177,15 +180,14 @@
         payload_kernel,
         "payload",
         [((feats + EXTRA, size), BF16), (spot, jnp.int32)],
-        points.T,
-        coef,
-        velocity,
-        batch,
-    )
-    (rows,) = call(rows_kernel, "rows", [((slots, 2 * feats), BF16)], batch, payload)
+        *(pltpu.with_memory_space_constraint(x, pltpu.HBM) for x in (points.T, coef, velocity, batch)),
+        scratch=[pltpu.VMEM(line, F32)] * 2 + [pltpu.SemaphoreType.DMA((4,))],
+        space=pltpu.HBM,
+    )
+    (rows,) = call(rows_kernel, "rows", [((feats, slots), BF16)], batch, payload)
     own = payload
     for step in row_steps[:-1]:
-        rows = jnp.concatenate([rows, exchange(rows, step)], axis=0)
+        rows = jnp.concatenate([rows, exchange(rows, step)], axis=1)
         if step is row_steps[0]:
             own, rows = lax.optimization_barrier((own, rows))
     more_rows = exchange(rows, row_steps[-1])
@@ -193,11 +195,11 @@
     for step in point_steps[1:]:
         payloads = payloads + [exchange(own if k == 0 else p, step) for k, p in enumerate(payloads)]
 
-    half = rows.shape[0]
+    half = rows.shape[1]
     amount = half * size * len(payloads)
     options = dict(
         limit=16 << 20,
-        scratch=[pltpu.VMEM((half, 128), F32)],
+        scratch=[pltpu.VMEM((half, 128), F32), pltpu.VMEM((half, 128), BF16)],
         cost=pl.CostEstimate(
             flops=2 * feats * amount, bytes_accessed=1 << 16, transcendentals=2 * amount
         ),

time: 26.8 us -> 24.3 us (0.907)
  waiting for transfers between devices: 7.29 us -> 3.42 us
  starting transfers between devices: 12.3 us -> 14.3 us
  local copies, waits for them, and re-layouts: 2.29 us -> 0.78 us
  Pallas kernels: 3.29 us -> 4.12 us
    ppermute x9, waiting for transfers between devices: 7.29 us -> 3.42 us  [exchange(): return lax.ppermute(value, AXES, pairs)]
    ppermute x9, starting transfers between devices: 12.3 us -> 14.3 us  [exchange(): return lax.ppermute(value, AXES, pairs)]
    unnamed x11 -> x9, local copies, waits for them, and re-layouts: 2.2 us -> 0.69 us
    pallas_call x6, Pallas kernels: 3.29 us -> 4.12 us  [call(): pl.pallas_call(kernel, out_shape=[jax.ShapeDtypeStruct(shape, kind) for s...]
  transfers between devices with their start and end apart: 9 -> 9, of which waited for: 5 -> 5; matrix products, arithmetic and copies ran while one was open for 0% -> 0% of each run, Pallas kernels for 4% -> 5%
where the time goes in v4:
time: 24.3 us; the launch traced here: 24.1 us
  starting transfers between devices  14.3 us (59%)
  Pallas kernels  4.12 us (17%)
  waiting for transfers between devices  3.42 us (14%)
  between operations  1.34 us (6%)
  local copies, waits for them, and re-layouts  0.78 us (3%)
    ppermute x9, starting transfers between devices, exchange(): return lax.ppermute(value, AXES, pairs)  14.3 us
    pallas_call x6, Pallas kernels, call(): pl.pallas_call(kernel, out_shape=[jax.ShapeDtypeStruct(shape, kind) for s...  4.12 us
    ppermute x9, waiting for transfers between devices, exchange(): return lax.ppermute(value, AXES, pairs)  3.42 us
    unnamed x9, local copies, waits for them, and re-layouts  0.69 us
  transfers between devices with their start and end apart: 9, of which 5 were waited for; matrix products, arithmetic and copies ran while one was open for 0% of the time, Pallas kernels for 5%

profile of v4, /device:TPU:0, one launch (start us, length us, event | category | flops | bytes accessed | tf_op | source)
XLA Modules:
  0.0 24.1 jit_solution(16165379788261728470)
XLA Ops:
  0.6 0.9 %payload.1 = (bf16[80,512]{1,0:T(8,128)(2,1)S(1)}, s32[1,64]{1,0:T(1,128)S(1)}) custom-call(bf16[64,512]{1,0:T(8,128)(2,1)} %bitcast.17, f32[1,512]{1,0:T(1,128)} %bitcast.11, f32[1,512]{1,0:T(1,128)} %bitcast.14, s32[1,64]{1,0:T(1,128)} %bitcast.18), custom_call_target="tpu_custom_call" | custom-call | tf_op jit(solution)/shard_map/payload/pallas_call | solution.py:145
  1.5 0.2 rows.1
  1.7 0.5 %collective-permute-start = (bf16[64,64]{1,0:T(8,128)(2,1)S(1)}, bf16[64,64]{1,0:T(8,128)(2,1)S(1)}, u32[]{:S(2)}, u32[]{:S(2)}) collective-permute-start(bf16[64,64]{1,0:T(8,128)(2,1)S(1)} %rows.1), channel_id=1, source_target_pairs={{0,1},{1,0},{2,3},{3,2},{4,5},{5,4},{6,7},{7,6},{8,9},{9,8},{10,11... | collective-permute-start | bytes 24584 | tf_op jit(solution)/shard_map/ppermute | solution.py:169
  2.2 2.6 %collective-permute-start.2 = (bf16[80,512]{1,0:T(8,128)(2,1)S(1)}, bf16[80,512]{1,0:T(8,128)(2,1)S(1)}, u32[]{:S(2)}, u32[]{:S(2)}) collective-permute-start(bf16[80,512]{1,0:T(8,128)(2,1)S(1)} %get-tuple-element.18.payload.refs_0_.refs_1_), channel_id=1, source_target_pairs={{0,17},{1,16},{2,19},{3,18},{4,21},{5,20},{6,23},{7,22},{8,25},{9,... | collective-permute-start | bytes 245768 | tf_op jit(solution)/shard_map/ppermute | solution.py:169
  4.8 0.0 collective-permute-done
  4.8 0.1 pad_maximum_fusion
  4.9 1.2 %collective-permute-start.1 = (bf16[64,128]{1,0:T(8,128)(2,1)S(1)}, bf16[64,128]{1,0:T(8,128)(2,1)S(1)}, u32[]{:S(2)}, u32[]{:S(2)}) collective-permute-start(bf16[64,128]{1,0:T(8,128)(2,1)S(1)} %pad_maximum_fusion), channel_id=1, source_target_pairs={{0,5},{1,4},{2,7},{3,6},{4,1},{5,0},{6,3},{7,2},{8,13},{9,12},{10,... | collective-permute-start | bytes 49160 | tf_op jit(solution)/shard_map/ppermute | solution.py:169
  6.2 1.6 %collective-permute-start.3 = (bf16[80,512]{1,0:T(8,128)(2,1)S(1)}, bf16[80,512]{1,0:T(8,128)(2,1)S(1)}, u32[]{:S(2)}, u32[]{:S(2)}) collective-permute-start(bf16[80,512]{1,0:T(8,128)(2,1)S(1)} %get-tuple-element.18.payload.refs_0_.refs_1_), channel_id=1, source_target_pairs={{0,3},{1,2},{2,1},{3,0},{4,7},{5,6},{6,5},{7,4},{8,11},{9,10},{10,... | collective-permute-start | bytes 245768 | tf_op jit(solution)/shard_map/ppermute | solution.py:169
  7.7 0.0 collective-permute-done.2.refs_1_.refs_2_
  7.8 1.5 %collective-permute-start.4 = (bf16[80,512]{1,0:T(8,128)(2,1)S(1)}, bf16[80,512]{1,0:T(8,128)(2,1)S(1)}, u32[]{:S(2)}, u32[]{:S(2)}) collective-permute-start(bf16[80,512]{1,0:T(8,128)(2,1)S(1)} %collective-permute-done.2.refs_1_.refs_2_), channel_id=1, source_target_pairs={{0,3},{1,2},{2,1},{3,0},{4,7},{5,6},{6,5},{7,4},{8,11},{9,10},{10,... | collective-permute-start | bytes 245768 | tf_op jit(solution)/shard_map/ppermute | solution.py:169
  9.3 0.0 collective-permute-done.1
  9.3 2.1 %collective-permute-start.5 = (bf16[64,256]{1,0:T(8,128)(2,1)S(1)}, bf16[64,256]{1,0:T(8,128)(2,1)S(1)}, u32[]{:S(2)}, u32[]{:S(2)}) collective-permute-start(bf16[64,256]{1,0:T(8,128)(2,1)S(1)} %constant_dynamic-update-slice_fusion.rows), channel_id=1, source_target_pairs={{0,9},{1,8},{2,11},{3,10},{4,13},{5,12},{6,15},{7,14},{8,1},{9,0},... | collective-permute-start | bytes 98312 | tf_op jit(solution)/shard_map/ppermute | solution.py:169
  12.0 0.0 collective-permute-done.3.refs_2_.refs_3_
  12.0 0.4 %collective-permute-done.4.refs_3_.refs_4_ = bf16[80,512]{1,0:T(8,128)(2,1)S(1)} collective-permute-done((bf16[80,512]{1,0:T(8,128)(2,1)S(1)}, bf16[80,512]{1,0:T(8,128)(2,1)S(1)}, u32[]{:S(2)}, u32[]{:S(2)}) %collective-permute-start.4) | collective-permute-done | bytes 81952 | tf_op jit(solution)/shard_map/ppermute | solution.py:169
  12.5 1.1 %sums_here.1 = (f32[1,256]{1,0:T(1,128)S(1)}, f32[32,512]{1,0:T(8,128)S(1)}) custom-call(bf16[64,256]{1,0:T(8,128)(2,1)S(1)} %constant_dynamic-update-slice_fusion.rows, bf16[80,512]{1,0:T(8,128)(2,1)S(1)} %get-tuple-element.18.payload.refs_0_.refs_1_, bf16[80,512]{1,0:T(8,128)(2,1)S(1)} %collective-permute-done.2.refs_1_.refs_2_, ...), custom_call_target="tpu_custom_call" | custom-call | flops 67108864 | bytes 65536 | tf_op jit(solution)/shard_map/sums_here/pallas_call | solution.py:145
  13.6 0.1 collective-permute-done.5.rows
  13.7 0.0 copy-start.2
  13.7 1.1 %sums_away.1 = f32[1,256]{1,0:T(1,128)S(1)} custom-call(bf16[64,256]{1,0:T(8,128)(2,1)S(1)} %collective-permute-done.5.rows, f32[32,512]{1,0:T(8,128)S(1)} %get-tuple-element.23.refs_0_, bf16[80,512]{1,0:T(8,128)(2,1)S(1)} %get-tuple-element.18.payload.refs_0_.refs_1_, bf16[80,512]{1,0:T(8,128)(2,1)S(1)} %collective-permute-done.2.refs_1_.refs_2_, ...), custom_call_target="tpu_custom_call" | custom-call | flops 67108864 | bytes 65536 | tf_op jit(solution)/shard_map/sums_away/pallas_call | solution.py:145
  14.8 0.0 copy-start.3
  14.8 2.6 %collective-permute-start.6 = (f32[1,256]{1,0:T(1,128)S(1)}, f32[1,256]{1,0:T(1,128)S(1)}, u32[]{:S(2)}, u32[]{:S(2)}) collective-permute-start(f32[1,256]{1,0:T(1,128)S(1)} %sums_away.1), channel_id=1, source_target_pairs={{0,9},{1,8},{2,11},{3,10},{4,13},{5,12},{6,15},{7,14},{8,1},{9,0},... | collective-permute-start | bytes 3080 | tf_op jit(solution)/shard_map/ppermute | solution.py:169
  17.4 0.0 copy-start.1
  17.4 0.0 copy-done.3
  17.4 0.0 copy-start
  17.4 0.0 copy-done.2
  17.5 0.7 %copy-done.1 = f32[512]{0:T(512)S(1)} copy-done((f32[512]{0:T(512)S(1)}, f32[512]{0:T(512)}, u32[]{:S(2)}) %copy-start.1) | copy-done | bytes 2072
  18.1 0.0 copy-done
  18.1 0.1 terms.1
  18.2 0.5 %collective-permute-done.6 = f32[1,256]{1,0:T(1,128)S(1)} collective-permute-done((f32[1,256]{1,0:T(1,128)S(1)}, f32[1,256]{1,0:T(1,128)S(1)}, u32[]{:S(2)}, u32[]{:S(2)}) %collective-permute-start.6) | collective-permute-done | bytes 1056 | tf_op jit(solution)/shard_map/ppermute | solution.py:169
  18.8 2.1 %collective-permute-start.7 = (f32[1,128]{1,0:T(1,128)S(1)}, f32[1,128]{1,0:T(1,128)S(1)}, u32[]{:S(2)}, u32[]{:S(2)}) collective-permute-start(f32[1,128]{1,0:T(1,128)S(1)} %slice.17), channel_id=1, source_target_pairs={{0,5},{1,4},{2,7},{3,6},{4,1},{5,0},{6,3},{7,2},{8,13},{9,12},{10,... | collective-permute-start | bytes 1544 | tf_op jit(solution)/shard_map/ppermute | solution.py:169
  20.9 1.3 %collective-permute-done.7 = f32[1,128]{1,0:T(1,128)S(1)} collective-permute-done((f32[1,128]{1,0:T(1,128)S(1)}, f32[1,128]{1,0:T(1,128)S(1)}, u32[]{:S(2)}, u32[]{:S(2)}) %collective-permute-start.7) | collective-permute-done | bytes 544 | tf_op jit(solution)/shard_map/ppermute | solution.py:169
  22.2 0.1 fusion.1
  22.2 0.1 collective-permute-start.8
  22.3 1.0 %collective-permute-done.8.other = f32[1,64]{1,0:T(1,128)S(1)} collective-permute-done((f32[1,64]{1,0:T(1,128)S(1)}, f32[1,64]{1,0:T(1,128)S(1)}, u32[]{:S(2)}, u32[]{:S(2)}) %collective-permute-start.8) | collective-permute-done | bytes 288 | tf_op jit(solution)/shard_map/ppermute | solution.py:169
  23.4 0.7 %finish.1 = (f32[1,512]{1,0:T(1,128)}, f32[1,512]{1,0:T(1,128)}) custom-call(f32[1,64]{1,0:T(1,128)S(1)} %get-tuple-element.29.own, f32[1,64]{1,0:T(1,128)S(1)} %collective-permute-done.8.other, f32[1,512]{1,0:T(1,128)S(1)} %get-tuple-element.24.base, f32[1,512]{1,0:T(1,128)S(1)} %bitcast.13, bf16[64,512]{1,0:T(8,128)(2,1)S(1)} %get-tuple-element.25.spots), custom_call_target="tpu_custom_call" | custom-call | tf_op jit(solution)/shard_map/finish/pallas_call | solution.py:145
  (6 shorter events, 0.0 us)
Async XLA Ops:
  1.7 3.1 %collective-permute-start = (bf16[64,64]{1,0:T(8,128)(2,1)S(1)}, bf16[64,64]{1,0:T(8,128)(2,1)S(1)}, u32[]{:S(2)}, u32[]{:S(2)}) collective-permute-start(bf16[64,64]{1,0:T(8,128)(2,1)S(1)} %rows.1), channel_id=1, source_target_pairs={{0,1},{1,0},{2,3},{3,2},{4,5},{5,4},{6,7},{7,6},{8,9},{9,8},{10,11... | collective-permute-start | bytes 24584 | tf_op jit(solution)/shard_map/ppermute | solution.py:169
  2.2 5.5 %collective-permute-start.2 = (bf16[80,512]{1,0:T(8,128)(2,1)S(1)}, bf16[80,512]{1,0:T(8,128)(2,1)S(1)}, u32[]{:S(2)}, u32[]{:S(2)}) collective-permute-start(bf16[80,512]{1,0:T(8,128)(2,1)S(1)} %get-tuple-element.18.payload.refs_0_.refs_1_), channel_id=1, source_target_pairs={{0,17},{1,16},{2,19},{3,18},{4,21},{5,20},{6,23},{7,22},{8,25},{9,... | collective-permute-start | bytes 245768 | tf_op jit(solution)/shard_map/ppermute | solution.py:169
  4.9 4.4 %collective-permute-start.1 = (bf16[64,128]{1,0:T(8,128)(2,1)S(1)}, bf16[64,128]{1,0:T(8,128)(2,1)S(1)}, u32[]{:S(2)}, u32[]{:S(2)}) collective-permute-start(bf16[64,128]{1,0:T(8,128)(2,1)S(1)} %pad_maximum_fusion), channel_id=1, source_target_pairs={{0,5},{1,4},{2,7},{3,6},{4,1},{5,0},{6,3},{7,2},{8,13},{9,12},{10,... | collective-permute-start | bytes 49160 | tf_op jit(solution)/shard_map/ppermute | solution.py:169
  6.2 5.9 %collective-permute-start.3 = (bf16[80,512]{1,0:T(8,128)(2,1)S(1)}, bf16[80,512]{1,0:T(8,128)(2,1)S(1)}, u32[]{:S(2)}, u32[]{:S(2)}) collective-permute-start(bf16[80,512]{1,0:T(8,128)(2,1)S(1)} %get-tuple-element.18.payload.refs_0_.refs_1_), channel_id=1, source_target_pairs={{0,3},{1,2},{2,1},{3,0},{4,7},{5,6},{6,5},{7,4},{8,11},{9,10},{10,... | collective-permute-start | bytes 245768 | tf_op jit(solution)/shard_map/ppermute | solution.py:169
  7.8 4.7 %collective-permute-start.4 = (bf16[80,512]{1,0:T(8,128)(2,1)S(1)}, bf16[80,512]{1,0:T(8,128)(2,1)S(1)}, u32[]{:S(2)}, u32[]{:S(2)}) collective-permute-start(bf16[80,512]{1,0:T(8,128)(2,1)S(1)} %collective-permute-done.2.refs_1_.refs_2_), channel_id=1, source_target_pairs={{0,3},{1,2},{2,1},{3,0},{4,7},{5,6},{6,5},{7,4},{8,11},{9,10},{10,... | collective-permute-start | bytes 245768 | tf_op jit(solution)/shard_map/ppermute | solution.py:169
  9.3 4.4 %collective-permute-start.5 = (bf16[64,256]{1,0:T(8,128)(2,1)S(1)}, bf16[64,256]{1,0:T(8,128)(2,1)S(1)}, u32[]{:S(2)}, u32[]{:S(2)}) collective-permute-start(bf16[64,256]{1,0:T(8,128)(2,1)S(1)} %constant_dynamic-update-slice_fusion.rows), channel_id=1, source_target_pairs={{0,9},{1,8},{2,11},{3,10},{4,13},{5,12},{6,15},{7,14},{8,1},{9,0},... | collective-permute-start | bytes 98312 | tf_op jit(solution)/shard_map/ppermute | solution.py:169
  13.7 3.7 %copy-start.2 = (f32[512]{0:T(512)S(1)}, f32[512]{0:T(512)}, u32[]{:S(2)}) copy-start(f32[512]{0:T(512)} %param.9) | copy-start | bytes 6148
  14.8 2.6 %copy-start.3 = (s32[64]{0:T(128)S(1)}, s32[64]{0:T(128)}, u32[]{:S(2)}) copy-start(s32[64]{0:T(128)} %param.10) | copy-start | bytes 772
  14.8 4.0 %collective-permute-start.6 = (f32[1,256]{1,0:T(1,128)S(1)}, f32[1,256]{1,0:T(1,128)S(1)}, u32[]{:S(2)}, u32[]{:S(2)}) collective-permute-start(f32[1,256]{1,0:T(1,128)S(1)} %sums_away.1), channel_id=1, source_target_pairs={{0,9},{1,8},{2,11},{3,10},{4,13},{5,12},{6,15},{7,14},{8,1},{9,0},... | collective-permute-start | bytes 3080 | tf_op jit(solution)/shard_map/ppermute | solution.py:169
  17.4 0.7 %copy-start.1 = (f32[512]{0:T(512)S(1)}, f32[512]{0:T(512)}, u32[]{:S(2)}) copy-start(f32[512]{0:T(512)} %param.8) | copy-start | bytes 6148
  17.4 0.7 %copy-start = (f32[512]{0:T(512)S(1)}, f32[512]{0:T(512)}, u32[]{:S(2)}) copy-start(f32[512]{0:T(512)} %param.7) | copy-start | bytes 6148
  18.8 3.4 %collective-permute-start.7 = (f32[1,128]{1,0:T(1,128)S(1)}, f32[1,128]{1,0:T(1,128)S(1)}, u32[]{:S(2)}, u32[]{:S(2)}) collective-permute-start(f32[1,128]{1,0:T(1,128)S(1)} %slice.17), channel_id=1, source_target_pairs={{0,5},{1,4},{2,7},{3,6},{4,1},{5,0},{6,3},{7,2},{8,13},{9,12},{10,... | collective-permute-start | bytes 1544 | tf_op jit(solution)/shard_map/ppermute | solution.py:169
  22.2 1.1 %collective-permute-start.8 = (f32[1,64]{1,0:T(1,128)S(1)}, f32[1,64]{1,0:T(1,128)S(1)}, u32[]{:S(2)}, u32[]{:S(2)}) collective-permute-start(f32[1,64]{1,0:T(1,128)S(1)} %get-tuple-element.28), channel_id=1, source_target_pairs={{0,1},{1,0},{2,3},{3,2},{4,5},{5,4},{6,7},{7,6},{8,9},{9,8},{10,11... | collective-permute-start | bytes 776 | tf_op jit(solution)/shard_map/ppermute | solution.py:169

commit v5 on v4

v5 whole, which is shorter than its diff:
```python
import functools

import jax
import jax.numpy as jnp
from jax import lax
from jax.experimental import pallas as pl
from jax.experimental.pallas import tpu as pltpu
from jax.sharding import PartitionSpec as P

MOMENTUM = 0.9
STEP_SIZE = 1.0
NOISE_VAR = 8.0
KERNEL_RATE = 3.0**0.5 / 6.0
LOG2_E = 1.4426950408889634
AXES = ("blk", "stripe")
SQ_AT, ONE_AT, COEF_AT, EXTRA = 0, 3, 6, 16

F32, BF16 = jnp.float32, jnp.bfloat16


def pieces(value):
    high = value.astype(BF16).astype(F32)
    rest = value - high
    middle = rest.astype(BF16).astype(F32)
    low = (rest - middle).astype(BF16).astype(F32)
    return high, middle, low


def payload_kernel(*refs):
    sources, (payload, slots, preview, slowed, coef, targets), rest = refs[:5], refs[5:11], refs[11:]
    velocity, sems = rest
    feats = sources[0].shape[0]
    copies = [
        pltpu.make_async_copy(source, target, sems.at[k])
        for k, (source, target) in enumerate(
            zip(sources, (payload.at[:feats], slots, coef, velocity, targets))
        )
    ]
    for copy in copies:
        copy.start()
    for copy in copies:
        copy.wait()
    size = coef.shape[1]
    feature = payload[:feats, :].astype(F32)
    col_sq = jnp.sum(feature * feature, axis=0, keepdims=True)
    slowed[...] = MOMENTUM * velocity[...]
    preview[...] = coef[...] + slowed[...]
    line = lax.broadcasted_iota(jnp.int32, (EXTRA, size), 0)
    extra = jnp.where((line >= ONE_AT) & (line < ONE_AT + 3), 1.0, 0.0)
    for at, parts in ((SQ_AT, pieces(col_sq)), (COEF_AT, pieces(preview[...]))):
        for k, part in enumerate(parts):
            extra = jnp.where(line == at + k, part, extra)
    payload[feats:, :] = extra.astype(BF16)


def rows_kernel(batch, payload, rows):
    feats, size = payload.shape[0] - EXTRA, payload.shape[1]
    slots = batch.shape[1]
    chosen = lax.broadcasted_iota(jnp.int32, (size, slots), 0) == batch[...]
    rows[...] = jnp.dot(
        payload[:feats, :], jnp.where(chosen, 1.0, 0.0).astype(BF16), preferred_element_type=F32
    ).astype(BF16)


def terms_kernel(batch, count, preview, slowed, targets, base, spots):
    slots, size = spots.shape
    diagonal = lax.broadcasted_iota(jnp.int32, (slots, slots), 0) == lax.broadcasted_iota(
        jnp.int32, (slots, slots), 1
    )
    live = lax.broadcasted_iota(jnp.int32, (1, slots), 1) < count[:, :1]
    row = jnp.where(live, batch[...], -1).astype(F32)
    column = jnp.sum(jnp.where(diagonal, row, 0.0), axis=1, keepdims=True)
    place = lax.broadcasted_iota(jnp.int32, (slots, size), 1)
    hits = jnp.where(place == column.astype(jnp.int32), 1.0, 0.0)
    spots[...] = hits.astype(BF16)
    times = jnp.sum(hits, axis=0, keepdims=True)
    base[...] = slowed[...] - STEP_SIZE * (times * (NOISE_VAR * preview[...] - targets[...]))


def add_sums(left, payload, total):
    depth = payload.shape[0]
    amount = left.shape[0]
    group = min(amount, 256)
    at = depth - EXTRA + COEF_AT
    lane = lax.broadcasted_iota(jnp.int32, (8, depth), 1)
    pick = jnp.where((lane >= at) & (lane < at + 3), 1.0, 0.0).astype(BF16)
    block = payload[...]
    weight = jnp.dot(pick, block, preferred_element_type=F32)
    scaled_weight = KERNEL_RATE * weight

    def add_group(start):
        squares = jnp.dot(
            left[pl.ds(start, group), :][:, :depth], block, preferred_element_type=F32
        )
        for at in range(0, group, 8):
            square = jnp.maximum(squares[at : at + 8, :], 1e-30)
            distance = square * lax.rsqrt(square)
            value = jnp.exp2((-KERNEL_RATE * LOG2_E) * distance) * (
                weight + scaled_weight * distance
            )
            part = value[:, :128]
            for lanes in range(128, value.shape[1], 128):
                part = part + value[:, lanes : lanes + 128]
            total[pl.ds(start + at, 8), :] += part

    if amount == group:
        add_group(0)
    else:
        pl.loop(0, amount // group)(lambda step: add_group(pl.multiple_of(step * group, group)))


def sums_kernel(rows, *refs):
    payloads, (sums, left, total) = refs[:-3], refs[-3:]
    feats, amount = rows.shape
    group = min(amount, 256)
    for at in range(0, amount, group):
        features = rows[:, at : at + group].astype(F32)
        norms = jnp.sum(features * features, axis=0, keepdims=True)
        line = lax.broadcasted_iota(jnp.int32, (128 - feats, group), 0)
        tail = jnp.where((line >= SQ_AT) & (line < SQ_AT + 3), 1.0, 0.0)
        for k, part in enumerate(pieces(norms)):
            tail = jnp.where(line == ONE_AT + k, part, tail)
        left[at : at + group, :] = jnp.concatenate([-2.0 * features, tail], axis=0).T.astype(BF16)
    total[...] = jnp.zeros_like(total)
    for payload in payloads:
        add_sums(left, payload, total)
    for at in range(0, amount, 128):
        turned = total[at : at + 128, :].T
        sums[:, at : at + 128] = jnp.sum(turned, axis=0, keepdims=True)


def finish_kernel(own, other, base, coef, spots, new_coef, new_velocity):
    slots = spots.shape[0]
    sums = own[...][:, :slots] + other[...]
    line = lax.broadcasted_iota(jnp.int32, (16, slots), 0)
    split = jnp.zeros((16, slots), F32)
    for k, part in enumerate(pieces(sums)):
        split = jnp.where(line == k, part, split)
    update = jnp.dot(split.astype(BF16), spots[...], preferred_element_type=F32)
    velocity = base[...] - STEP_SIZE * jnp.sum(update, axis=0, keepdims=True)
    new_velocity[...] = velocity
    new_coef[...] = coef[...] + velocity


def call(kernel, name, outs, *operands, limit=8 << 20, scratch=(), cost=None, space=pltpu.VMEM):
    return pl.pallas_call(
        kernel,
        out_shape=[jax.ShapeDtypeStruct(shape, kind) for shape, kind in outs],
        in_specs=[pl.BlockSpec(memory_space=space)] * len(operands),
        out_specs=[pl.BlockSpec(memory_space=pltpu.VMEM)] * len(outs),
        scratch_shapes=scratch,
        compiler_params=pltpu.CompilerParams(vmem_limit_bytes=limit),
        cost_estimate=cost,
        name=name,
    )(*operands)


def per_device(mesh_shape, points, coefficients, velocity, targets, batch_rows, counts):
    n_blk, n_stripe = mesh_shape["blk"], mesh_shape["stripe"]
    size, feats = points.shape
    slots = batch_rows.shape[0]

    def exchange(value, offset):
        d_blk, d_stripe = offset
        pairs = [
            (b * n_stripe + s, (b ^ d_blk) * n_stripe + (s ^ d_stripe))
            for b in range(n_blk)
            for s in range(n_stripe)
        ]
        return lax.ppermute(value, AXES, pairs)

    offsets = [(b, s) for s in (0, 2) for b in range(n_blk)]
    point_offsets = [(b, s | 1) for b, s in offsets[1:]]
    row_steps = [(0, (1 << k) + 1) for k in range(n_stripe.bit_length() - 2, 1, -1)]
    other_core = (0, 1)

    line, spot = (1, size), (1, slots)
    batch = batch_rows.reshape(spot)
    vectors = [x.reshape(line) for x in (coefficients, velocity, targets)]
    payload, batch, preview, slowed, coef, targets = call(
        payload_kernel,
        "payload",
        [((feats + EXTRA, size), BF16)] + [(spot, jnp.int32)] + [(line, F32)] * 4,
        *(
            pltpu.with_memory_space_constraint(x, pltpu.HBM)
            for x in (points.T, batch, *vectors)
        ),
        scratch=[
            pltpu.VMEM(line, F32),
            pltpu.SemaphoreType.DMA((5,)),
        ],
        space=pltpu.HBM,
    )
    (rows,) = call(rows_kernel, "rows", [((feats, slots), BF16)], batch, payload)
    beside = exchange(payload, other_core)
    rows, beside = lax.optimization_barrier((rows, beside))
    for step in row_steps[:-1]:
        rows = jnp.concatenate([rows, exchange(rows, step)], axis=1)
    more_rows = exchange(rows, row_steps[-1])
    payloads = [payload] + [exchange(payload, o) for o in point_offsets]
    payloads = payloads + [beside] + [exchange(p, other_core) for p in payloads[1:]]

    half = rows.shape[1]
    amount = half * size * len(payloads)
    cost = pl.CostEstimate(
        flops=2 * feats * amount, bytes_accessed=1 << 16, transcendentals=2 * amount
    )
    (keep,), (send,) = (
        call(
            sums_kernel,
            name,
            [((1, half), F32)],
            some_rows,
            *payloads,
            limit=16 << 20,
            scratch=[pltpu.VMEM((half, 128), BF16), pltpu.VMEM((half, 128), F32)],
            cost=cost,
        )
        for name, some_rows in (("sums_here", rows), ("sums_away", more_rows))
    )
    count = jnp.pad(counts, ((0, 0), (0, slots - counts.shape[1])))
    base, spots = call(
        terms_kernel,
        "terms",
        [(line, F32), ((slots, size), BF16)],
        batch,
        count,
        preview,
        slowed,
        targets,
    )
    keep, base, spots = lax.optimization_barrier((keep, base, spots))

    for step in row_steps[:0:-1]:
        both = keep + exchange(send, step)
        half = half // 2
        keep, send = both[:, :half], both[:, half:]
    other = exchange(send, row_steps[0])

    new_coef, new_velocity = call(
        finish_kernel, "finish", [(line, F32)] * 2, keep, other, base, coef, spots
    )
    return new_coef.reshape(size), new_velocity.reshape(size)


def solution(mesh):
    in_specs = (
        P(("blk", "stripe"), None),
        P(("blk", "stripe")),
        P(("blk", "stripe")),
        P(("blk", "stripe")),
        P(("blk", "stripe")),
        P("blk", "stripe"),
    )
    out_specs = (P(("blk", "stripe")), P(("blk", "stripe")))
    return jax.shard_map(
        functools.partial(per_device, dict(mesh.shape)),
        mesh=mesh,
        in_specs=in_specs,
        out_specs=out_specs,
        check_vma=False,
    )
```

time: 24.3 us -> 23.6 us (0.971)
  waiting for transfers between devices: 3.42 us -> 4.73 us
  starting transfers between devices: 14.3 us -> 13 us
  local copies, waits for them, and re-layouts: 0.78 us -> 0.08 us
    ppermute x9 -> x11, starting transfers between devices: 14.3 us -> 13 us  [exchange(): return lax.ppermute(value, AXES, pairs)]
    ppermute x9 -> x11, waiting for transfers between devices: 3.42 us -> 4.73 us  [exchange(): return lax.ppermute(value, AXES, pairs)]
    unnamed x9 -> x0, local copies, waits for them, and re-layouts: 0.69 us -> none
  transfers between devices with their start and end apart: 9 -> 11, of which waited for: 5 -> 5; matrix products, arithmetic and copies ran while one was open for 0% -> 0% of each run, Pallas kernels for 5% -> 6%
where the time goes in v5:
time: 23.6 us; the launch traced here: 23.4 us
  starting transfers between devices  13 us (55%)
  waiting for transfers between devices  4.73 us (20%)
  Pallas kernels  4.22 us (18%)
  between operations  1.33 us (6%)
    ppermute x11, starting transfers between devices, exchange(): return lax.ppermute(value, AXES, pairs)  13 us
    ppermute x11, waiting for transfers between devices, exchange(): return lax.ppermute(value, AXES, pairs)  4.73 us
    pallas_call x6, Pallas kernels, call(): pl.pallas_call(kernel, out_shape=[jax.ShapeDtypeStruct(shape, kind) for s...  4.22 us
  transfers between devices with their start and end apart: 11, of which 5 were waited for; matrix products, arithmetic and copies ran while one was open for 0% of the time, Pallas kernels for 6%

profile of v5, /device:TPU:0, one launch (start us, length us, event | category | flops | bytes accessed | tf_op | source)
XLA Modules:
  0.0 23.4 jit_solution(14052421088715560374)
XLA Ops:
  0.6 0.9 %payload.1 = (bf16[80,512]{1,0:T(8,128)(2,1)S(1)}, s32[1,64]{1,0:T(1,128)S(1)}, f32[1,512]{1,0:T(1,128)S(1)}, f32[1,512]{1,0:T(1,128)S(1)}, f32[1,512]{1,0:T(1,128)S(1)}, /*index=5*/f32[1,512]{1,0:T(1,128)S(1)}) custom-call(bf16[64,512]{1,0:T(8,128)(2,1)} %bitcast.7, s32[1,64]{1,0:T(1,128)} %bitcast.11, f32[1,512]{1,0:T(1,128)} %bitcast.8, ...), custom_call_target="tpu_custom_call" | custom-call | tf_op jit(solution)/shard_map/payload/pallas_call | solution.py:146
  1.6 0.5 %collective-permute-start = (bf16[80,512]{1,0:T(8,128)(2,1)S(1)}, bf16[80,512]{1,0:T(8,128)(2,1)S(1)}, u32[]{:S(2)}, u32[]{:S(2)}) collective-permute-start(bf16[80,512]{1,0:T(8,128)(2,1)S(1)} %get-tuple-element.18.payload.refs_0_), channel_id=1, source_target_pairs={{0,1},{1,0},{2,3},{3,2},{4,5},{5,4},{6,7},{7,6},{8,9},{9,8},{10,11... | collective-permute-start | bytes 245768 | tf_op jit(solution)/shard_map/ppermute | solution.py:170
  2.1 2.6 %collective-permute-start.2 = (bf16[80,512]{1,0:T(8,128)(2,1)S(1)}, bf16[80,512]{1,0:T(8,128)(2,1)S(1)}, u32[]{:S(2)}, u32[]{:S(2)}) collective-permute-start(bf16[80,512]{1,0:T(8,128)(2,1)S(1)} %get-tuple-element.18.payload.refs_0_), channel_id=1, source_target_pairs={{0,17},{1,16},{2,19},{3,18},{4,21},{5,20},{6,23},{7,22},{8,25},{9,... | collective-permute-start | bytes 245768 | tf_op jit(solution)/shard_map/ppermute | solution.py:170
  4.7 1.2 %collective-permute-start.3 = (bf16[80,512]{1,0:T(8,128)(2,1)S(1)}, bf16[80,512]{1,0:T(8,128)(2,1)S(1)}, u32[]{:S(2)}, u32[]{:S(2)}) collective-permute-start(bf16[80,512]{1,0:T(8,128)(2,1)S(1)} %get-tuple-element.18.payload.refs_0_), channel_id=1, source_target_pairs={{0,3},{1,2},{2,1},{3,0},{4,7},{5,6},{6,5},{7,4},{8,11},{9,10},{10,... | collective-permute-start | bytes 245768 | tf_op jit(solution)/shard_map/ppermute | solution.py:170
  5.9 0.0 collective-permute-start.4
  5.9 0.2 rows.1
  6.1 0.0 collective-permute-done.refs_4_
  6.1 2.8 %collective-permute-start.1 = (bf16[64,64]{1,0:T(8,128)(2,1)S(1)}, bf16[64,64]{1,0:T(8,128)(2,1)S(1)}, u32[]{:S(2)}, u32[]{:S(2)}) collective-permute-start(bf16[64,64]{1,0:T(8,128)(2,1)S(1)} %rows.1), channel_id=1, source_target_pairs={{0,9},{1,8},{2,11},{3,10},{4,13},{5,12},{6,15},{7,14},{8,1},{9,0},... | collective-permute-start | bytes 24584 | tf_op jit(solution)/shard_map/ppermute | solution.py:170
  8.9 0.0 collective-permute-done.2.refs_1_
  8.9 0.4 %collective-permute-start.5 = (bf16[80,512]{1,0:T(8,128)(2,1)S(1)}, bf16[80,512]{1,0:T(8,128)(2,1)S(1)}, u32[]{:S(2)}, u32[]{:S(2)}) collective-permute-start(bf16[80,512]{1,0:T(8,128)(2,1)S(1)} %collective-permute-done.2.refs_1_), channel_id=1, source_target_pairs={{0,1},{1,0},{2,3},{3,2},{4,5},{5,4},{6,7},{7,6},{8,9},{9,8},{10,11... | collective-permute-start | bytes 245768 | tf_op jit(solution)/shard_map/ppermute | solution.py:170
  9.4 0.9 %collective-permute-done.3.refs_2_ = bf16[80,512]{1,0:T(8,128)(2,1)S(1)} collective-permute-done((bf16[80,512]{1,0:T(8,128)(2,1)S(1)}, bf16[80,512]{1,0:T(8,128)(2,1)S(1)}, u32[]{:S(2)}, u32[]{:S(2)}) %collective-permute-start.3) | collective-permute-done | bytes 81952 | tf_op jit(solution)/shard_map/ppermute | solution.py:170
  10.3 0.0 collective-permute-start.6
  10.3 0.7 %collective-permute-done.4.refs_3_ = bf16[80,512]{1,0:T(8,128)(2,1)S(1)} collective-permute-done((bf16[80,512]{1,0:T(8,128)(2,1)S(1)}, bf16[80,512]{1,0:T(8,128)(2,1)S(1)}, u32[]{:S(2)}, u32[]{:S(2)}) %collective-permute-start.4) | collective-permute-done | bytes 81952 | tf_op jit(solution)/shard_map/ppermute | solution.py:170
  11.0 0.4 %collective-permute-start.7 = (bf16[80,512]{1,0:T(8,128)(2,1)S(1)}, bf16[80,512]{1,0:T(8,128)(2,1)S(1)}, u32[]{:S(2)}, u32[]{:S(2)}) collective-permute-start(bf16[80,512]{1,0:T(8,128)(2,1)S(1)} %collective-permute-done.4.refs_3_), channel_id=1, source_target_pairs={{0,1},{1,0},{2,3},{3,2},{4,5},{5,4},{6,7},{7,6},{8,9},{9,8},{10,11... | collective-permute-start | bytes 245768 | tf_op jit(solution)/shard_map/ppermute | solution.py:170
  11.4 0.0 collective-permute-done.1
  11.4 0.1 pad_maximum_fusion.rows
  11.4 1.3 %collective-permute-start.8 = (bf16[64,128]{1,0:T(8,128)(2,1)S(1)}, bf16[64,128]{1,0:T(8,128)(2,1)S(1)}, u32[]{:S(2)}, u32[]{:S(2)}) collective-permute-start(bf16[64,128]{1,0:T(8,128)(2,1)S(1)} %pad_maximum_fusion.rows), channel_id=1, source_target_pairs={{0,5},{1,4},{2,7},{3,6},{4,1},{5,0},{6,3},{7,2},{8,13},{9,12},{10,... | collective-permute-start | bytes 49160 | tf_op jit(solution)/shard_map/ppermute | solution.py:170
  13.4 0.2 terms.1
  13.6 1.0 %collective-permute-done.8.rows = bf16[64,128]{1,0:T(8,128)(2,1)S(1)} collective-permute-done((bf16[64,128]{1,0:T(8,128)(2,1)S(1)}, bf16[64,128]{1,0:T(8,128)(2,1)S(1)}, u32[]{:S(2)}, u32[]{:S(2)}) %collective-permute-start.8) | collective-permute-done | bytes 16416 | tf_op jit(solution)/shard_map/ppermute | solution.py:170
  14.6 0.0 collective-permute-done.5.refs_5_
  14.6 0.0 collective-permute-done.6.refs_6_
  14.6 0.0 collective-permute-done.7.refs_7_
  14.6 1.1 %sums_away.1 = f32[1,128]{1,0:T(1,128)S(1)} custom-call(bf16[64,128]{1,0:T(8,128)(2,1)S(1)} %collective-permute-done.8.rows, bf16[80,512]{1,0:T(8,128)(2,1)S(1)} %get-tuple-element.18.payload.refs_0_, bf16[80,512]{1,0:T(8,128)(2,1)S(1)} %collective-permute-done.2.refs_1_, bf16[80,512]{1,0:T(8,128)(2,1)S(1)} %collective-permute-done.3.refs_2_, ...), custom_call_target="tpu_custom_call" | custom-call | flops 67108864 | bytes 65536 | tf_op jit(solution)/shard_map/sums_away/pallas_call | solution.py:146
  15.7 1.4 %collective-permute-start.9 = (f32[1,128]{1,0:T(1,128)S(1)}, f32[1,128]{1,0:T(1,128)S(1)}, u32[]{:S(2)}, u32[]{:S(2)}) collective-permute-start(f32[1,128]{1,0:T(1,128)S(1)} %sums_away.1), channel_id=1, source_target_pairs={{0,5},{1,4},{2,7},{3,6},{4,1},{5,0},{6,3},{7,2},{8,13},{9,12},{10,... | collective-permute-start | bytes 1544 | tf_op jit(solution)/shard_map/ppermute | solution.py:170
  17.1 1.1 %sums_here.1 = f32[1,128]{1,0:T(1,128)S(1)} custom-call(bf16[64,128]{1,0:T(8,128)(2,1)S(1)} %pad_maximum_fusion.rows, bf16[80,512]{1,0:T(8,128)(2,1)S(1)} %get-tuple-element.18.payload.refs_0_, bf16[80,512]{1,0:T(8,128)(2,1)S(1)} %collective-permute-done.2.refs_1_, bf16[80,512]{1,0:T(8,128)(2,1)S(1)} %collective-permute-done.3.refs_2_, ...), custom_call_target="tpu_custom_call" | custom-call | flops 67108864 | bytes 65536 | tf_op jit(solution)/shard_map/sums_here/pallas_call | solution.py:146
  18.2 0.5 %collective-permute-done.9 = f32[1,128]{1,0:T(1,128)S(1)} collective-permute-done((f32[1,128]{1,0:T(1,128)S(1)}, f32[1,128]{1,0:T(1,128)S(1)}, u32[]{:S(2)}, u32[]{:S(2)}) %collective-permute-start.9) | collective-permute-done | bytes 544 | tf_op jit(solution)/shard_map/ppermute | solution.py:170
  18.8 0.1 fusion
  18.9 2.3 %collective-permute-start.10 = (f32[1,64]{1,0:T(1,128)S(1)}, f32[1,64]{1,0:T(1,128)S(1)}, u32[]{:S(2)}, u32[]{:S(2)}) collective-permute-start(f32[1,64]{1,0:T(1,128)S(1)} %get-tuple-element.32), channel_id=1, source_target_pairs={{0,9},{1,8},{2,11},{3,10},{4,13},{5,12},{6,15},{7,14},{8,1},{9,0},... | collective-permute-start | bytes 776 | tf_op jit(solution)/shard_map/ppermute | solution.py:170
  21.2 1.6 %collective-permute-done.10.other = f32[1,64]{1,0:T(1,128)S(1)} collective-permute-done((f32[1,64]{1,0:T(1,128)S(1)}, f32[1,64]{1,0:T(1,128)S(1)}, u32[]{:S(2)}, u32[]{:S(2)}) %collective-permute-start.10) | collective-permute-done | bytes 288 | tf_op jit(solution)/shard_map/ppermute | solution.py:170
  22.7 0.7 %finish.1 = (f32[1,512]{1,0:T(1,128)}, f32[1,512]{1,0:T(1,128)}) custom-call(f32[1,64]{1,0:T(1,128)S(1)} %get-tuple-element.33.own, f32[1,64]{1,0:T(1,128)S(1)} %collective-permute-done.10.other, f32[1,512]{1,0:T(1,128)S(1)} %get-tuple-element.27.base, f32[1,512]{1,0:T(1,128)S(1)} %get-tuple-element.28.coef, bf16[64,512]{1,0:T(8,128)(2,1)S(1)} %get-tuple-element.29.spots), custom_call_target="tpu_custom_call" | custom-call | tf_op jit(solution)/shard_map/finish/pallas_call | solution.py:146
  (2 shorter events, 0.0 us)
Async XLA Ops:
  1.6 4.5 %collective-permute-start = (bf16[80,512]{1,0:T(8,128)(2,1)S(1)}, bf16[80,512]{1,0:T(8,128)(2,1)S(1)}, u32[]{:S(2)}, u32[]{:S(2)}) collective-permute-start(bf16[80,512]{1,0:T(8,128)(2,1)S(1)} %get-tuple-element.18.payload.refs_0_), channel_id=1, source_target_pairs={{0,1},{1,0},{2,3},{3,2},{4,5},{5,4},{6,7},{7,6},{8,9},{9,8},{10,11... | collective-permute-start | bytes 245768 | tf_op jit(solution)/shard_map/ppermute | solution.py:170
  2.1 6.8 %collective-permute-start.2 = (bf16[80,512]{1,0:T(8,128)(2,1)S(1)}, bf16[80,512]{1,0:T(8,128)(2,1)S(1)}, u32[]{:S(2)}, u32[]{:S(2)}) collective-permute-start(bf16[80,512]{1,0:T(8,128)(2,1)S(1)} %get-tuple-element.18.payload.refs_0_), channel_id=1, source_target_pairs={{0,17},{1,16},{2,19},{3,18},{4,21},{5,20},{6,23},{7,22},{8,25},{9,... | collective-permute-start | bytes 245768 | tf_op jit(solution)/shard_map/ppermute | solution.py:170
  4.7 5.6 %collective-permute-start.3 = (bf16[80,512]{1,0:T(8,128)(2,1)S(1)}, bf16[80,512]{1,0:T(8,128)(2,1)S(1)}, u32[]{:S(2)}, u32[]{:S(2)}) collective-permute-start(bf16[80,512]{1,0:T(8,128)(2,1)S(1)} %get-tuple-element.18.payload.refs_0_), channel_id=1, source_target_pairs={{0,3},{1,2},{2,1},{3,0},{4,7},{5,6},{6,5},{7,4},{8,11},{9,10},{10,... | collective-permute-start | bytes 245768 | tf_op jit(solution)/shard_map/ppermute | solution.py:170
  5.9 5.1 %collective-permute-start.4 = (bf16[80,512]{1,0:T(8,128)(2,1)S(1)}, bf16[80,512]{1,0:T(8,128)(2,1)S(1)}, u32[]{:S(2)}, u32[]{:S(2)}) collective-permute-start(bf16[80,512]{1,0:T(8,128)(2,1)S(1)} %get-tuple-element.18.payload.refs_0_), channel_id=1, source_target_pairs={{0,19},{1,18},{2,17},{3,16},{4,23},{5,22},{6,21},{7,20},{8,27},{9,... | collective-permute-start | bytes 245768 | tf_op jit(solution)/shard_map/ppermute | solution.py:170
  6.1 5.3 %collective-permute-start.1 = (bf16[64,64]{1,0:T(8,128)(2,1)S(1)}, bf16[64,64]{1,0:T(8,128)(2,1)S(1)}, u32[]{:S(2)}, u32[]{:S(2)}) collective-permute-start(bf16[64,64]{1,0:T(8,128)(2,1)S(1)} %rows.1), channel_id=1, source_target_pairs={{0,9},{1,8},{2,11},{3,10},{4,13},{5,12},{6,15},{7,14},{8,1},{9,0},... | collective-permute-start | bytes 24584 | tf_op jit(solution)/shard_map/ppermute | solution.py:170
  8.9 5.7 %collective-permute-start.5 = (bf16[80,512]{1,0:T(8,128)(2,1)S(1)}, bf16[80,512]{1,0:T(8,128)(2,1)S(1)}, u32[]{:S(2)}, u32[]{:S(2)}) collective-permute-start(bf16[80,512]{1,0:T(8,128)(2,1)S(1)} %collective-permute-done.2.refs_1_), channel_id=1, source_target_pairs={{0,1},{1,0},{2,3},{3,2},{4,5},{5,4},{6,7},{7,6},{8,9},{9,8},{10,11... | collective-permute-start | bytes 245768 | tf_op jit(solution)/shard_map/ppermute | solution.py:170
  10.3 4.3 %collective-permute-start.6 = (bf16[80,512]{1,0:T(8,128)(2,1)S(1)}, bf16[80,512]{1,0:T(8,128)(2,1)S(1)}, u32[]{:S(2)}, u32[]{:S(2)}) collective-permute-start(bf16[80,512]{1,0:T(8,128)(2,1)S(1)} %collective-permute-done.3.refs_2_), channel_id=1, source_target_pairs={{0,1},{1,0},{2,3},{3,2},{4,5},{5,4},{6,7},{7,6},{8,9},{9,8},{10,11... | collective-permute-start | bytes 245768 | tf_op jit(solution)/shard_map/ppermute | solution.py:170
  11.0 3.7 %collective-permute-start.7 = (bf16[80,512]{1,0:T(8,128)(2,1)S(1)}, bf16[80,512]{1,0:T(8,128)(2,1)S(1)}, u32[]{:S(2)}, u32[]{:S(2)}) collective-permute-start(bf16[80,512]{1,0:T(8,128)(2,1)S(1)} %collective-permute-done.4.refs_3_), channel_id=1, source_target_pairs={{0,1},{1,0},{2,3},{3,2},{4,5},{5,4},{6,7},{7,6},{8,9},{9,8},{10,11... | collective-permute-start | bytes 245768 | tf_op jit(solution)/shard_map/ppermute | solution.py:170
  11.4 3.2 %collective-permute-start.8 = (bf16[64,128]{1,0:T(8,128)(2,1)S(1)}, bf16[64,128]{1,0:T(8,128)(2,1)S(1)}, u32[]{:S(2)}, u32[]{:S(2)}) collective-permute-start(bf16[64,128]{1,0:T(8,128)(2,1)S(1)} %pad_maximum_fusion.rows), channel_id=1, source_target_pairs={{0,5},{1,4},{2,7},{3,6},{4,1},{5,0},{6,3},{7,2},{8,13},{9,12},{10,... | collective-permute-start | bytes 49160 | tf_op jit(solution)/shard_map/ppermute | solution.py:170
  15.7 3.0 %collective-permute-start.9 = (f32[1,128]{1,0:T(1,128)S(1)}, f32[1,128]{1,0:T(1,128)S(1)}, u32[]{:S(2)}, u32[]{:S(2)}) collective-permute-start(f32[1,128]{1,0:T(1,128)S(1)} %sums_away.1), channel_id=1, source_target_pairs={{0,5},{1,4},{2,7},{3,6},{4,1},{5,0},{6,3},{7,2},{8,13},{9,12},{10,... | collective-permute-start | bytes 1544 | tf_op jit(solution)/shard_map/ppermute | solution.py:170
  18.9 3.9 %collective-permute-start.10 = (f32[1,64]{1,0:T(1,128)S(1)}, f32[1,64]{1,0:T(1,128)S(1)}, u32[]{:S(2)}, u32[]{:S(2)}) collective-permute-start(f32[1,64]{1,0:T(1,128)S(1)} %get-tuple-element.32), channel_id=1, source_target_pairs={{0,9},{1,8},{2,11},{3,10},{4,13},{5,12},{6,15},{7,14},{8,1},{9,0},... | collective-permute-start | bytes 776 | tf_op jit(solution)/shard_map/ppermute | solution.py:170

commit v6 on v5

--- a/solution.py
+++ b/solution.py
@@ -170,7 +170,7 @@
         return lax.ppermute(value, AXES, pairs)
 
     offsets = [(b, s) for s in (0, 2) for b in range(n_blk)]
-    point_offsets = [(b, s | 1) for b, s in offsets[1:]]
+    point_offsets = [(b, s | 1) for b, s in offsets[:0:-1]]
     row_steps = [(0, (1 << k) + 1) for k in range(n_stripe.bit_length() - 2, 1, -1)]
     other_core = (0, 1)
 
@@ -193,7 +193,6 @@
     )
     (rows,) = call(rows_kernel, "rows", [((feats, slots), BF16)], batch, payload)
     beside = exchange(payload, other_core)
-    rows, beside = lax.optimization_barrier((rows, beside))
     for step in row_steps[:-1]:
         rows = jnp.concatenate([rows, exchange(rows, step)], axis=1)
     more_rows = exchange(rows, row_steps[-1])

time: 23.6 us -> 23 us (0.975)
  waiting for transfers between devices: 4.73 us -> 3.2 us
  starting transfers between devices: 13 us -> 13.9 us
    ppermute x11, waiting for transfers between devices: 4.73 us -> 3.2 us  [exchange(): return lax.ppermute(value, AXES, pairs)]
    ppermute x11, starting transfers between devices: 13 us -> 13.9 us  [exchange(): return lax.ppermute(value, AXES, pairs)]
where the time goes in v6:
time: 23 us; the launch traced here: 22.8 us
  starting transfers between devices  13.9 us (60%)
  Pallas kernels  4.23 us (18%)
  waiting for transfers between devices  3.2 us (14%)
  between operations  1.33 us (6%)
    ppermute x11, starting transfers between devices, exchange(): return lax.ppermute(value, AXES, pairs)  13.9 us
    pallas_call x6, Pallas kernels, call(): pl.pallas_call(kernel, out_shape=[jax.ShapeDtypeStruct(shape, kind) for s...  4.23 us
    ppermute x11, waiting for transfers between devices, exchange(): return lax.ppermute(value, AXES, pairs)  3.2 us
  transfers between devices with their start and end apart: 11, of which 5 were waited for; matrix products, arithmetic and copies ran while one was open for 0% of the time, Pallas kernels for 6%

profile of v6, /device:TPU:0, one launch (start us, length us, event | category | flops | bytes accessed | tf_op | source)
XLA Modules:
  0.0 22.8 jit_solution(8609356002895426083)
XLA Ops:
  0.6 0.9 %payload.1 = (bf16[80,512]{1,0:T(8,128)(2,1)S(1)}, s32[1,64]{1,0:T(1,128)S(1)}, f32[1,512]{1,0:T(1,128)S(1)}, f32[1,512]{1,0:T(1,128)S(1)}, f32[1,512]{1,0:T(1,128)S(1)}, /*index=5*/f32[1,512]{1,0:T(1,128)S(1)}) custom-call(bf16[64,512]{1,0:T(8,128)(2,1)} %bitcast.7, s32[1,64]{1,0:T(1,128)} %bitcast.11, f32[1,512]{1,0:T(1,128)} %bitcast.8, ...), custom_call_target="tpu_custom_call" | custom-call | tf_op jit(solution)/shard_map/payload/pallas_call | solution.py:146
  1.6 3.4 %collective-permute-start.1 = (bf16[80,512]{1,0:T(8,128)(2,1)S(1)}, bf16[80,512]{1,0:T(8,128)(2,1)S(1)}, u32[]{:S(2)}, u32[]{:S(2)}) collective-permute-start(bf16[80,512]{1,0:T(8,128)(2,1)S(1)} %get-tuple-element.16.payload.refs_0_), channel_id=1, source_target_pairs={{0,19},{1,18},{2,17},{3,16},{4,23},{5,22},{6,21},{7,20},{8,27},{9,... | collective-permute-start | bytes 245768 | tf_op jit(solution)/shard_map/ppermute | solution.py:170
  5.0 0.8 %collective-permute-start.2 = (bf16[80,512]{1,0:T(8,128)(2,1)S(1)}, bf16[80,512]{1,0:T(8,128)(2,1)S(1)}, u32[]{:S(2)}, u32[]{:S(2)}) collective-permute-start(bf16[80,512]{1,0:T(8,128)(2,1)S(1)} %get-tuple-element.16.payload.refs_0_), channel_id=1, source_target_pairs={{0,3},{1,2},{2,1},{3,0},{4,7},{5,6},{6,5},{7,4},{8,11},{9,10},{10,... | collective-permute-start | bytes 245768 | tf_op jit(solution)/shard_map/ppermute | solution.py:170
  5.8 0.1 collective-permute-start.3
  5.9 0.2 rows.1
  6.1 2.8 %collective-permute-start = (bf16[64,64]{1,0:T(8,128)(2,1)S(1)}, bf16[64,64]{1,0:T(8,128)(2,1)S(1)}, u32[]{:S(2)}, u32[]{:S(2)}) collective-permute-start(bf16[64,64]{1,0:T(8,128)(2,1)S(1)} %rows.1), channel_id=1, source_target_pairs={{0,9},{1,8},{2,11},{3,10},{4,13},{5,12},{6,15},{7,14},{8,1},{9,0},... | collective-permute-start | bytes 24584 | tf_op jit(solution)/shard_map/ppermute | solution.py:170
  8.8 0.0 collective-permute-start.4
  8.8 0.0 collective-permute-done.1.refs_1_
  8.8 0.5 %collective-permute-start.5 = (bf16[80,512]{1,0:T(8,128)(2,1)S(1)}, bf16[80,512]{1,0:T(8,128)(2,1)S(1)}, u32[]{:S(2)}, u32[]{:S(2)}) collective-permute-start(bf16[80,512]{1,0:T(8,128)(2,1)S(1)} %collective-permute-done.1.refs_1_), channel_id=1, source_target_pairs={{0,1},{1,0},{2,3},{3,2},{4,5},{5,4},{6,7},{7,6},{8,9},{9,8},{10,11... | collective-permute-start | bytes 245768 | tf_op jit(solution)/shard_map/ppermute | solution.py:170
  9.3 0.2 collective-permute-done.2.refs_2_
  9.5 0.3 %collective-permute-start.6 = (bf16[80,512]{1,0:T(8,128)(2,1)S(1)}, bf16[80,512]{1,0:T(8,128)(2,1)S(1)}, u32[]{:S(2)}, u32[]{:S(2)}) collective-permute-start(bf16[80,512]{1,0:T(8,128)(2,1)S(1)} %collective-permute-done.2.refs_2_), channel_id=1, source_target_pairs={{0,1},{1,0},{2,3},{3,2},{4,5},{5,4},{6,7},{7,6},{8,9},{9,8},{10,11... | collective-permute-start | bytes 245768 | tf_op jit(solution)/shard_map/ppermute | solution.py:170
  9.8 0.7 %collective-permute-done.3.refs_3_ = bf16[80,512]{1,0:T(8,128)(2,1)S(1)} collective-permute-done((bf16[80,512]{1,0:T(8,128)(2,1)S(1)}, bf16[80,512]{1,0:T(8,128)(2,1)S(1)}, u32[]{:S(2)}, u32[]{:S(2)}) %collective-permute-start.3) | collective-permute-done | bytes 81952 | tf_op jit(solution)/shard_map/ppermute | solution.py:170
  10.6 0.1 collective-permute-start.7
  10.7 0.0 collective-permute-done
  10.7 0.1 pad_maximum_fusion.rows
  10.8 1.6 %collective-permute-start.8 = (bf16[64,128]{1,0:T(8,128)(2,1)S(1)}, bf16[64,128]{1,0:T(8,128)(2,1)S(1)}, u32[]{:S(2)}, u32[]{:S(2)}) collective-permute-start(bf16[64,128]{1,0:T(8,128)(2,1)S(1)} %pad_maximum_fusion.rows), channel_id=1, source_target_pairs={{0,5},{1,4},{2,7},{3,6},{4,1},{5,0},{6,3},{7,2},{8,13},{9,12},{10,... | collective-permute-start | bytes 49160 | tf_op jit(solution)/shard_map/ppermute | solution.py:170
  13.0 0.2 terms.1
  13.2 0.7 %collective-permute-done.8.rows = bf16[64,128]{1,0:T(8,128)(2,1)S(1)} collective-permute-done((bf16[64,128]{1,0:T(8,128)(2,1)S(1)}, bf16[64,128]{1,0:T(8,128)(2,1)S(1)}, u32[]{:S(2)}, u32[]{:S(2)}) %collective-permute-start.8) | collective-permute-done | bytes 16416 | tf_op jit(solution)/shard_map/ppermute | solution.py:170
  14.0 0.0 collective-permute-done.4.refs_4_
  14.0 0.0 collective-permute-done.5.refs_5_
  14.0 0.0 collective-permute-done.6.refs_6_
  14.0 0.0 collective-permute-done.7.refs_7_
  14.0 1.1 %sums_away.1 = f32[1,128]{1,0:T(1,128)S(1)} custom-call(bf16[64,128]{1,0:T(8,128)(2,1)S(1)} %collective-permute-done.8.rows, bf16[80,512]{1,0:T(8,128)(2,1)S(1)} %get-tuple-element.16.payload.refs_0_, bf16[80,512]{1,0:T(8,128)(2,1)S(1)} %collective-permute-done.1.refs_1_, bf16[80,512]{1,0:T(8,128)(2,1)S(1)} %collective-permute-done.2.refs_2_, ...), custom_call_target="tpu_custom_call" | custom-call | flops 67108864 | bytes 65536 | tf_op jit(solution)/shard_map/sums_away/pallas_call | solution.py:146
  15.1 1.7 %collective-permute-start.9 = (f32[1,128]{1,0:T(1,128)S(1)}, f32[1,128]{1,0:T(1,128)S(1)}, u32[]{:S(2)}, u32[]{:S(2)}) collective-permute-start(f32[1,128]{1,0:T(1,128)S(1)} %sums_away.1), channel_id=1, source_target_pairs={{0,5},{1,4},{2,7},{3,6},{4,1},{5,0},{6,3},{7,2},{8,13},{9,12},{10,... | collective-permute-start | bytes 1544 | tf_op jit(solution)/shard_map/ppermute | solution.py:170
  16.8 1.1 %sums_here.1 = f32[1,128]{1,0:T(1,128)S(1)} custom-call(bf16[64,128]{1,0:T(8,128)(2,1)S(1)} %pad_maximum_fusion.rows, bf16[80,512]{1,0:T(8,128)(2,1)S(1)} %get-tuple-element.16.payload.refs_0_, bf16[80,512]{1,0:T(8,128)(2,1)S(1)} %collective-permute-done.1.refs_1_, bf16[80,512]{1,0:T(8,128)(2,1)S(1)} %collective-permute-done.2.refs_2_, ...), custom_call_target="tpu_custom_call" | custom-call | flops 67108864 | bytes 65536 | tf_op jit(solution)/shard_map/sums_here/pallas_call | solution.py:146
  17.9 0.3 %collective-permute-done.9 = f32[1,128]{1,0:T(1,128)S(1)} collective-permute-done((f32[1,128]{1,0:T(1,128)S(1)}, f32[1,128]{1,0:T(1,128)S(1)}, u32[]{:S(2)}, u32[]{:S(2)}) %collective-permute-start.9) | collective-permute-done | bytes 544 | tf_op jit(solution)/shard_map/ppermute | solution.py:170
  18.1 0.1 fusion
  18.2 2.6 %collective-permute-start.10 = (f32[1,64]{1,0:T(1,128)S(1)}, f32[1,64]{1,0:T(1,128)S(1)}, u32[]{:S(2)}, u32[]{:S(2)}) collective-permute-start(f32[1,64]{1,0:T(1,128)S(1)} %get-tuple-element.28), channel_id=1, source_target_pairs={{0,9},{1,8},{2,11},{3,10},{4,13},{5,12},{6,15},{7,14},{8,1},{9,0},... | collective-permute-start | bytes 776 | tf_op jit(solution)/shard_map/ppermute | solution.py:170
  20.8 1.3 %collective-permute-done.10.other = f32[1,64]{1,0:T(1,128)S(1)} collective-permute-done((f32[1,64]{1,0:T(1,128)S(1)}, f32[1,64]{1,0:T(1,128)S(1)}, u32[]{:S(2)}, u32[]{:S(2)}) %collective-permute-start.10) | collective-permute-done | bytes 288 | tf_op jit(solution)/shard_map/ppermute | solution.py:170
  22.1 0.7 %finish.1 = (f32[1,512]{1,0:T(1,128)}, f32[1,512]{1,0:T(1,128)}) custom-call(f32[1,64]{1,0:T(1,128)S(1)} %get-tuple-element.29.own, f32[1,64]{1,0:T(1,128)S(1)} %collective-permute-done.10.other, f32[1,512]{1,0:T(1,128)S(1)} %get-tuple-element.23.base, f32[1,512]{1,0:T(1,128)S(1)} %get-tuple-element.24.coef, bf16[64,512]{1,0:T(8,128)(2,1)S(1)} %get-tuple-element.25.spots), custom_call_target="tpu_custom_call" | custom-call | tf_op jit(solution)/shard_map/finish/pallas_call | solution.py:146
  (2 shorter events, 0.0 us)
Async XLA Ops:
  1.6 7.3 %collective-permute-start.1 = (bf16[80,512]{1,0:T(8,128)(2,1)S(1)}, bf16[80,512]{1,0:T(8,128)(2,1)S(1)}, u32[]{:S(2)}, u32[]{:S(2)}) collective-permute-start(bf16[80,512]{1,0:T(8,128)(2,1)S(1)} %get-tuple-element.16.payload.refs_0_), channel_id=1, source_target_pairs={{0,19},{1,18},{2,17},{3,16},{4,23},{5,22},{6,21},{7,20},{8,27},{9,... | collective-permute-start | bytes 245768 | tf_op jit(solution)/shard_map/ppermute | solution.py:170
  5.0 4.6 %collective-permute-start.2 = (bf16[80,512]{1,0:T(8,128)(2,1)S(1)}, bf16[80,512]{1,0:T(8,128)(2,1)S(1)}, u32[]{:S(2)}, u32[]{:S(2)}) collective-permute-start(bf16[80,512]{1,0:T(8,128)(2,1)S(1)} %get-tuple-element.16.payload.refs_0_), channel_id=1, source_target_pairs={{0,3},{1,2},{2,1},{3,0},{4,7},{5,6},{6,5},{7,4},{8,11},{9,10},{10,... | collective-permute-start | bytes 245768 | tf_op jit(solution)/shard_map/ppermute | solution.py:170
  5.8 4.8 %collective-permute-start.3 = (bf16[80,512]{1,0:T(8,128)(2,1)S(1)}, bf16[80,512]{1,0:T(8,128)(2,1)S(1)}, u32[]{:S(2)}, u32[]{:S(2)}) collective-permute-start(bf16[80,512]{1,0:T(8,128)(2,1)S(1)} %get-tuple-element.16.payload.refs_0_), channel_id=1, source_target_pairs={{0,17},{1,16},{2,19},{3,18},{4,21},{5,20},{6,23},{7,22},{8,25},{9,... | collective-permute-start | bytes 245768 | tf_op jit(solution)/shard_map/ppermute | solution.py:170
  6.1 4.6 %collective-permute-start = (bf16[64,64]{1,0:T(8,128)(2,1)S(1)}, bf16[64,64]{1,0:T(8,128)(2,1)S(1)}, u32[]{:S(2)}, u32[]{:S(2)}) collective-permute-start(bf16[64,64]{1,0:T(8,128)(2,1)S(1)} %rows.1), channel_id=1, source_target_pairs={{0,9},{1,8},{2,11},{3,10},{4,13},{5,12},{6,15},{7,14},{8,1},{9,0},... | collective-permute-start | bytes 24584 | tf_op jit(solution)/shard_map/ppermute | solution.py:170
  8.8 5.1 %collective-permute-start.4 = (bf16[80,512]{1,0:T(8,128)(2,1)S(1)}, bf16[80,512]{1,0:T(8,128)(2,1)S(1)}, u32[]{:S(2)}, u32[]{:S(2)}) collective-permute-start(bf16[80,512]{1,0:T(8,128)(2,1)S(1)} %get-tuple-element.16.payload.refs_0_), channel_id=1, source_target_pairs={{0,1},{1,0},{2,3},{3,2},{4,5},{5,4},{6,7},{7,6},{8,9},{9,8},{10,11... | collective-permute-start | bytes 245768 | tf_op jit(solution)/shard_map/ppermute | solution.py:170
  8.8 5.1 %collective-permute-start.5 = (bf16[80,512]{1,0:T(8,128)(2,1)S(1)}, bf16[80,512]{1,0:T(8,128)(2,1)S(1)}, u32[]{:S(2)}, u32[]{:S(2)}) collective-permute-start(bf16[80,512]{1,0:T(8,128)(2,1)S(1)} %collective-permute-done.1.refs_1_), channel_id=1, source_target_pairs={{0,1},{1,0},{2,3},{3,2},{4,5},{5,4},{6,7},{7,6},{8,9},{9,8},{10,11... | collective-permute-start | bytes 245768 | tf_op jit(solution)/shard_map/ppermute | solution.py:170
  9.5 4.4 %collective-permute-start.6 = (bf16[80,512]{1,0:T(8,128)(2,1)S(1)}, bf16[80,512]{1,0:T(8,128)(2,1)S(1)}, u32[]{:S(2)}, u32[]{:S(2)}) collective-permute-start(bf16[80,512]{1,0:T(8,128)(2,1)S(1)} %collective-permute-done.2.refs_2_), channel_id=1, source_target_pairs={{0,1},{1,0},{2,3},{3,2},{4,5},{5,4},{6,7},{7,6},{8,9},{9,8},{10,11... | collective-permute-start | bytes 245768 | tf_op jit(solution)/shard_map/ppermute | solution.py:170
  10.6 3.4 %collective-permute-start.7 = (bf16[80,512]{1,0:T(8,128)(2,1)S(1)}, bf16[80,512]{1,0:T(8,128)(2,1)S(1)}, u32[]{:S(2)}, u32[]{:S(2)}) collective-permute-start(bf16[80,512]{1,0:T(8,128)(2,1)S(1)} %collective-permute-done.3.refs_3_), channel_id=1, source_target_pairs={{0,1},{1,0},{2,3},{3,2},{4,5},{5,4},{6,7},{7,6},{8,9},{9,8},{10,11... | collective-permute-start | bytes 245768 | tf_op jit(solution)/shard_map/ppermute | solution.py:170
  10.8 3.2 %collective-permute-start.8 = (bf16[64,128]{1,0:T(8,128)(2,1)S(1)}, bf16[64,128]{1,0:T(8,128)(2,1)S(1)}, u32[]{:S(2)}, u32[]{:S(2)}) collective-permute-start(bf16[64,128]{1,0:T(8,128)(2,1)S(1)} %pad_maximum_fusion.rows), channel_id=1, source_target_pairs={{0,5},{1,4},{2,7},{3,6},{4,1},{5,0},{6,3},{7,2},{8,13},{9,12},{10,... | collective-permute-start | bytes 49160 | tf_op jit(solution)/shard_map/ppermute | solution.py:170
  15.1 3.0 %collective-permute-start.9 = (f32[1,128]{1,0:T(1,128)S(1)}, f32[1,128]{1,0:T(1,128)S(1)}, u32[]{:S(2)}, u32[]{:S(2)}) collective-permute-start(f32[1,128]{1,0:T(1,128)S(1)} %sums_away.1), channel_id=1, source_target_pairs={{0,5},{1,4},{2,7},{3,6},{4,1},{5,0},{6,3},{7,2},{8,13},{9,12},{10,... | collective-permute-start | bytes 1544 | tf_op jit(solution)/shard_map/ppermute | solution.py:170
  18.2 3.9 %collective-permute-start.10 = (f32[1,64]{1,0:T(1,128)S(1)}, f32[1,64]{1,0:T(1,128)S(1)}, u32[]{:S(2)}, u32[]{:S(2)}) collective-permute-start(f32[1,64]{1,0:T(1,128)S(1)} %get-tuple-element.28), channel_id=1, source_target_pairs={{0,9},{1,8},{2,11},{3,10},{4,13},{5,12},{6,15},{7,14},{8,1},{9,0},... | collective-permute-start | bytes 776 | tf_op jit(solution)/shard_map/ppermute | solution.py:170

commit v7 on v5

--- a/solution.py
+++ b/solution.py
@@ -62,7 +62,7 @@
     ).astype(BF16)
 
 
-def terms_kernel(batch, count, preview, slowed, targets, base, spots):
+def terms_kernel(batch, count, preview, slowed, targets, after, base, spots):
     slots, size = spots.shape
     diagonal = lax.broadcasted_iota(jnp.int32, (slots, slots), 0) == lax.broadcasted_iota(
         jnp.int32, (slots, slots), 1
@@ -109,8 +109,7 @@
         pl.loop(0, amount // group)(lambda step: add_group(pl.multiple_of(step * group, group)))
 
 
-def sums_kernel(rows, *refs):
-    payloads, (sums, left, total) = refs[:-3], refs[-3:]
+def turn_rows(rows, left):
     feats, amount = rows.shape
     group = min(amount, 256)
     for at in range(0, amount, group):
@@ -121,12 +120,39 @@
         for k, part in enumerate(pieces(norms)):
             tail = jnp.where(line == ONE_AT + k, part, tail)
         left[at : at + group, :] = jnp.concatenate([-2.0 * features, tail], axis=0).T.astype(BF16)
+
+
+def row_sums(left, payloads, total):
     total[...] = jnp.zeros_like(total)
     for payload in payloads:
         add_sums(left, payload, total)
-    for at in range(0, amount, 128):
-        turned = total[at : at + 128, :].T
-        sums[:, at : at + 128] = jnp.sum(turned, axis=0, keepdims=True)
+    amount = total.shape[0]
+    width = min(amount, 128)
+    parts = [
+        jnp.sum(total[at : at + width, :].T, axis=0, keepdims=True)
+        for at in range(0, amount, width)
+    ]
+    return parts[0] if len(parts) == 1 else jnp.concatenate(parts, axis=1)
+
+
+def here_kernel(rows, *refs):
+    payloads, (sums, left, total) = refs[:-3], refs[-3:]
+    turn_rows(rows, left)
+    sums[...] = row_sums(left, payloads, total)
+
+
+def send_kernel(rows, here, *refs):
+    payloads, (sums, left, total) = refs[:-3], refs[-3:]
+    half = total.shape[0]
+    turn_rows(rows, left)
+    mine = row_sums(left.at[half : 2 * half], payloads, total)
+    sums[...] = jnp.concatenate([here[:, half:], mine], axis=1)
+
+
+def keep_kernel(rows, *refs):
+    payloads, (sums, left, total) = refs[:-3], refs[-3:]
+    turn_rows(rows, left)
+    sums[...] = row_sums(left.at[: total.shape[0]], payloads, total)
 
 
 def finish_kernel(own, other, base, coef, spots, new_coef, new_velocity):
@@ -193,31 +219,41 @@
     )
     (rows,) = call(rows_kernel, "rows", [((feats, slots), BF16)], batch, payload)
     beside = exchange(payload, other_core)
-    rows, beside = lax.optimization_barrier((rows, beside))
-    for step in row_steps[:-1]:
-        rows = jnp.concatenate([rows, exchange(rows, step)], axis=1)
+    halves = [rows, exchange(rows, row_steps[0])]
+    rows = jnp.concatenate(halves, axis=1)
+    for step in row_steps[1:-1]:
+        other = exchange(rows, step)
+        split = other.shape[1] // 2
+        halves = [
+            jnp.concatenate([halves[0], other[:, :split]], axis=1),
+            jnp.concatenate([halves[1], other[:, split:]], axis=1),
+        ]
+        rows = jnp.concatenate(halves, axis=1)
     more_rows = exchange(rows, row_steps[-1])
     payloads = [payload] + [exchange(payload, o) for o in point_offsets]
     payloads = payloads + [beside] + [exchange(p, other_core) for p in payloads[1:]]
 
-    half = rows.shape[1]
-    amount = half * size * len(payloads)
-    cost = pl.CostEstimate(
-        flops=2 * feats * amount, bytes_accessed=1 << 16, transcendentals=2 * amount
-    )
-    (keep,), (send,) = (
-        call(
-            sums_kernel,
+    amount = rows.shape[1]
+    half = amount // 2
+
+    def sums(kernel, name, outs, kept, *operands):
+        work = kept * size * len(payloads)
+        return call(
+            kernel,
             name,
-            [((1, half), F32)],
-            some_rows,
+            [((1, outs), F32)],
+            *operands,
             *payloads,
             limit=16 << 20,
-            scratch=[pltpu.VMEM((half, 128), BF16), pltpu.VMEM((half, 128), F32)],
-            cost=cost,
-        )
-        for name, some_rows in (("sums_here", rows), ("sums_away", more_rows))
-    )
+            scratch=[pltpu.VMEM((amount, 128), BF16), pltpu.VMEM((kept, 128), F32)],
+            cost=pl.CostEstimate(
+                flops=2 * feats * work, bytes_accessed=1 << 16, transcendentals=2 * work
+            ),
+        )[0]
+
+    here = sums(here_kernel, "sums_here", amount, amount, rows)
+    send = sums(send_kernel, "sums_send", amount, half, more_rows, here)
+    keep = sums(keep_kernel, "sums_keep", half, half, more_rows)
     count = jnp.pad(counts, ((0, 0), (0, slots - counts.shape[1])))
     base, spots = call(
         terms_kernel,
@@ -228,17 +264,21 @@
         preview,
         slowed,
         targets,
+        keep,
     )
     keep, base, spots = lax.optimization_barrier((keep, base, spots))
 
-    for step in row_steps[:0:-1]:
-        both = keep + exchange(send, step)
+    back = exchange(send, row_steps[0])
+    mine, send = here[:, :half] + back[:, :half], keep + back[:, half:]
+    steps = [row_steps[-1]] + row_steps[1:-1][::-1]
+    for step in steps[:-1]:
+        both = mine + exchange(send, step)
         half = half // 2
-        keep, send = both[:, :half], both[:, half:]
-    other = exchange(send, row_steps[0])
+        mine, send = both[:, :half], both[:, half:]
+    other = exchange(send, steps[-1])
 
     new_coef, new_velocity = call(
-        finish_kernel, "finish", [(line, F32)] * 2, keep, other, base, coef, spots
+        finish_kernel, "finish", [(line, F32)] * 2, mine, other, base, coef, spots
     )
     return new_coef.reshape(size), new_velocity.reshape(size)
 

time: 23.6 us -> 22.9 us (0.970)
  waiting for transfers between devices: 4.73 us -> 2.98 us
  starting transfers between devices: 13 us -> 13.5 us
  Pallas kernels: 4.22 us -> 4.68 us
    ppermute x11, waiting for transfers between devices: 4.73 us -> 2.98 us  [exchange(): return lax.ppermute(value, AXES, pairs)]
    ppermute x11, starting transfers between devices: 13 us -> 13.5 us  [exchange(): return lax.ppermute(value, AXES, pairs)]
    pallas_call x6 -> x7, Pallas kernels: 4.22 us -> 4.68 us  [call(): pl.pallas_call(kernel, out_shape=[jax.ShapeDtypeStruct(shape, kind) for s...]
  transfers between devices with their start and end apart: 11 -> 11, of which waited for: 5 -> 4; matrix products, arithmetic and copies ran while one was open for 0% -> 0% of each run, Pallas kernels for 6% -> 10%
where the time goes in v7:
time: 22.9 us; the launch traced here: 22.7 us
  starting transfers between devices  13.5 us (59%)
  Pallas kernels  4.68 us (20%)
  waiting for transfers between devices  2.98 us (13%)
  between operations  1.36 us (6%)
    ppermute x11, starting transfers between devices, exchange(): return lax.ppermute(value, AXES, pairs)  13.5 us
    pallas_call x7, Pallas kernels, call(): pl.pallas_call(kernel, out_shape=[jax.ShapeDtypeStruct(shape, kind) for s...  4.68 us
    ppermute x11, waiting for transfers between devices, exchange(): return lax.ppermute(value, AXES, pairs)  2.98 us
  transfers between devices with their start and end apart: 11, of which 4 were waited for; matrix products, arithmetic and copies ran while one was open for 0% of the time, Pallas kernels for 10%

profile of v7, /device:TPU:0, one launch (start us, length us, event | category | flops | bytes accessed | tf_op | source)
XLA Modules:
  0.0 22.7 jit_solution(9322647835160665426)
XLA Ops:
  0.6 0.9 %payload.1 = (bf16[80,512]{1,0:T(8,128)(2,1)S(1)}, s32[1,64]{1,0:T(1,128)S(1)}, f32[1,512]{1,0:T(1,128)S(1)}, f32[1,512]{1,0:T(1,128)S(1)}, f32[1,512]{1,0:T(1,128)S(1)}, /*index=5*/f32[1,512]{1,0:T(1,128)S(1)}) custom-call(bf16[64,512]{1,0:T(8,128)(2,1)} %bitcast.7, s32[1,64]{1,0:T(1,128)} %bitcast.11, f32[1,512]{1,0:T(1,128)} %bitcast.8, ...), custom_call_target="tpu_custom_call" | custom-call | tf_op jit(solution)/shard_map/payload/pallas_call | solution.py:172
  1.6 3.4 %collective-permute-start.3 = (bf16[80,512]{1,0:T(8,128)(2,1)S(1)}, bf16[80,512]{1,0:T(8,128)(2,1)S(1)}, u32[]{:S(2)}, u32[]{:S(2)}) collective-permute-start(bf16[80,512]{1,0:T(8,128)(2,1)S(1)} %get-tuple-element.16.payload.refs_0_), channel_id=1, source_target_pairs={{0,19},{1,18},{2,17},{3,16},{4,23},{5,22},{6,21},{7,20},{8,27},{9,... | collective-permute-start | bytes 245768 | tf_op jit(solution)/shard_map/ppermute | solution.py:196
  5.0 0.8 %collective-permute-start.2 = (bf16[80,512]{1,0:T(8,128)(2,1)S(1)}, bf16[80,512]{1,0:T(8,128)(2,1)S(1)}, u32[]{:S(2)}, u32[]{:S(2)}) collective-permute-start(bf16[80,512]{1,0:T(8,128)(2,1)S(1)} %get-tuple-element.16.payload.refs_0_), channel_id=1, source_target_pairs={{0,3},{1,2},{2,1},{3,0},{4,7},{5,6},{6,5},{7,4},{8,11},{9,10},{10,... | collective-permute-start | bytes 245768 | tf_op jit(solution)/shard_map/ppermute | solution.py:196
  5.8 0.1 collective-permute-start.1
  5.9 0.2 rows.1
  6.1 2.8 %collective-permute-start = (bf16[64,64]{1,0:T(8,128)(2,1)S(1)}, bf16[64,64]{1,0:T(8,128)(2,1)S(1)}, u32[]{:S(2)}, u32[]{:S(2)}) collective-permute-start(bf16[64,64]{1,0:T(8,128)(2,1)S(1)} %rows.1), channel_id=1, source_target_pairs={{0,9},{1,8},{2,11},{3,10},{4,13},{5,12},{6,15},{7,14},{8,1},{9,0},... | collective-permute-start | bytes 24584 | tf_op jit(solution)/shard_map/ppermute | solution.py:196
  8.8 0.0 collective-permute-start.4
  8.8 0.0 collective-permute-done.3.refs_3_
  8.8 0.5 %collective-permute-start.7 = (bf16[80,512]{1,0:T(8,128)(2,1)S(1)}, bf16[80,512]{1,0:T(8,128)(2,1)S(1)}, u32[]{:S(2)}, u32[]{:S(2)}) collective-permute-start(bf16[80,512]{1,0:T(8,128)(2,1)S(1)} %collective-permute-done.3.refs_3_), channel_id=1, source_target_pairs={{0,1},{1,0},{2,3},{3,2},{4,5},{5,4},{6,7},{7,6},{8,9},{9,8},{10,11... | collective-permute-start | bytes 245768 | tf_op jit(solution)/shard_map/ppermute | solution.py:196
  9.3 0.2 collective-permute-done.2.refs_2_
  9.5 0.3 %collective-permute-start.6 = (bf16[80,512]{1,0:T(8,128)(2,1)S(1)}, bf16[80,512]{1,0:T(8,128)(2,1)S(1)}, u32[]{:S(2)}, u32[]{:S(2)}) collective-permute-start(bf16[80,512]{1,0:T(8,128)(2,1)S(1)} %collective-permute-done.2.refs_2_), channel_id=1, source_target_pairs={{0,1},{1,0},{2,3},{3,2},{4,5},{5,4},{6,7},{7,6},{8,9},{9,8},{10,11... | collective-permute-start | bytes 245768 | tf_op jit(solution)/shard_map/ppermute | solution.py:196
  9.8 0.7 %collective-permute-done.1.refs_1_ = bf16[80,512]{1,0:T(8,128)(2,1)S(1)} collective-permute-done((bf16[80,512]{1,0:T(8,128)(2,1)S(1)}, bf16[80,512]{1,0:T(8,128)(2,1)S(1)}, u32[]{:S(2)}, u32[]{:S(2)}) %collective-permute-start.1) | collective-permute-done | bytes 81952 | tf_op jit(solution)/shard_map/ppermute | solution.py:196
  10.6 0.1 collective-permute-start.5
  10.7 0.0 collective-permute-done
  10.7 0.1 pad_maximum_fusion.rows
  10.8 1.6 %collective-permute-start.8 = (bf16[64,128]{1,0:T(8,128)(2,1)S(1)}, bf16[64,128]{1,0:T(8,128)(2,1)S(1)}, u32[]{:S(2)}, u32[]{:S(2)}) collective-permute-start(bf16[64,128]{1,0:T(8,128)(2,1)S(1)} %pad_maximum_fusion.rows), channel_id=1, source_target_pairs={{0,5},{1,4},{2,7},{3,6},{4,1},{5,0},{6,3},{7,2},{8,13},{9,12},{10,... | collective-permute-start | bytes 49160 | tf_op jit(solution)/shard_map/ppermute | solution.py:196
  13.0 0.0 collective-permute-done.4.refs_4_
  13.1 0.0 collective-permute-done.7.refs_7_
  13.1 0.0 collective-permute-done.6.refs_6_
  13.1 0.0 collective-permute-done.5.refs_5_
  13.1 1.1 %sums_here.1.here = f32[1,128]{1,0:T(1,128)S(1)} custom-call(bf16[64,128]{1,0:T(8,128)(2,1)S(1)} %pad_maximum_fusion.rows, bf16[80,512]{1,0:T(8,128)(2,1)S(1)} %get-tuple-element.16.payload.refs_0_, bf16[80,512]{1,0:T(8,128)(2,1)S(1)} %collective-permute-done.1.refs_1_, bf16[80,512]{1,0:T(8,128)(2,1)S(1)} %collective-permute-done.2.refs_2_, ...), custom_call_target="tpu_custom_call" | custom-call | flops 67108864 | bytes 65536 | tf_op jit(solution)/shard_map/sums_here/pallas_call | solution.py:172
  14.2 0.0 collective-permute-done.8.rows
  14.2 0.8 %sums_send.1 = f32[1,128]{1,0:T(1,128)S(1)} custom-call(bf16[64,128]{1,0:T(8,128)(2,1)S(1)} %collective-permute-done.8.rows, f32[1,128]{1,0:T(1,128)S(1)} %sums_here.1.here, bf16[80,512]{1,0:T(8,128)(2,1)S(1)} %get-tuple-element.16.payload.refs_0_, bf16[80,512]{1,0:T(8,128)(2,1)S(1)} %collective-permute-done.1.refs_1_, ...), custom_call_target="tpu_custom_call" | custom-call | flops 33554432 | bytes 65536 | tf_op jit(solution)/shard_map/sums_send/pallas_call | solution.py:172
  15.0 2.5 %collective-permute-start.9 = (f32[1,128]{1,0:T(1,128)S(1)}, f32[1,128]{1,0:T(1,128)S(1)}, u32[]{:S(2)}, u32[]{:S(2)}) collective-permute-start(f32[1,128]{1,0:T(1,128)S(1)} %sums_send.1), channel_id=1, source_target_pairs={{0,9},{1,8},{2,11},{3,10},{4,13},{5,12},{6,15},{7,14},{8,1},{9,0},... | collective-permute-start | bytes 1544 | tf_op jit(solution)/shard_map/ppermute | solution.py:196
  17.5 0.7 %sums_keep.1.after = f32[1,64]{1,0:T(1,128)S(1)} custom-call(bf16[64,128]{1,0:T(8,128)(2,1)S(1)} %collective-permute-done.8.rows, bf16[80,512]{1,0:T(8,128)(2,1)S(1)} %get-tuple-element.16.payload.refs_0_, bf16[80,512]{1,0:T(8,128)(2,1)S(1)} %collective-permute-done.1.refs_1_, bf16[80,512]{1,0:T(8,128)(2,1)S(1)} %collective-permute-done.2.refs_2_, ...), custom_call_target="tpu_custom_call" | custom-call | flops 33554432 | bytes 65536 | tf_op jit(solution)/shard_map/sums_keep/pallas_call | solution.py:172
  18.3 0.2 terms.1
  18.5 0.4 %collective-permute-done.9 = f32[1,128]{1,0:T(1,128)S(1)} collective-permute-done((f32[1,128]{1,0:T(1,128)S(1)}, f32[1,128]{1,0:T(1,128)S(1)}, u32[]{:S(2)}, u32[]{:S(2)}) %collective-permute-start.9) | collective-permute-done | bytes 544 | tf_op jit(solution)/shard_map/ppermute | solution.py:196
  18.9 0.1 slice_add_fusion
  19.0 1.3 %collective-permute-start.10 = (f32[1,64]{1,0:T(1,128)S(1)}, f32[1,64]{1,0:T(1,128)S(1)}, u32[]{:S(2)}, u32[]{:S(2)}) collective-permute-start(f32[1,64]{1,0:T(1,128)S(1)} %get-tuple-element.28), channel_id=1, source_target_pairs={{0,5},{1,4},{2,7},{3,6},{4,1},{5,0},{6,3},{7,2},{8,13},{9,12},{10,... | collective-permute-start | bytes 776 | tf_op jit(solution)/shard_map/ppermute | solution.py:196
  20.3 1.6 %collective-permute-done.10.other = f32[1,64]{1,0:T(1,128)S(1)} collective-permute-done((f32[1,64]{1,0:T(1,128)S(1)}, f32[1,64]{1,0:T(1,128)S(1)}, u32[]{:S(2)}, u32[]{:S(2)}) %collective-permute-start.10) | collective-permute-done | bytes 288 | tf_op jit(solution)/shard_map/ppermute | solution.py:196
  22.0 0.7 %finish.1 = (f32[1,512]{1,0:T(1,128)}, f32[1,512]{1,0:T(1,128)}) custom-call(f32[1,64]{1,0:T(1,128)S(1)} %get-tuple-element.29.own, f32[1,64]{1,0:T(1,128)S(1)} %collective-permute-done.10.other, f32[1,512]{1,0:T(1,128)S(1)} %get-tuple-element.23.base, f32[1,512]{1,0:T(1,128)S(1)} %get-tuple-element.24.coef, bf16[64,512]{1,0:T(8,128)(2,1)S(1)} %get-tuple-element.25.spots), custom_call_target="tpu_custom_call" | custom-call | tf_op jit(solution)/shard_map/finish/pallas_call | solution.py:172
  (1 shorter events, 0.0 us)
Async XLA Ops:
  1.6 7.3 %collective-permute-start.3 = (bf16[80,512]{1,0:T(8,128)(2,1)S(1)}, bf16[80,512]{1,0:T(8,128)(2,1)S(1)}, u32[]{:S(2)}, u32[]{:S(2)}) collective-permute-start(bf16[80,512]{1,0:T(8,128)(2,1)S(1)} %get-tuple-element.16.payload.refs_0_), channel_id=1, source_target_pairs={{0,19},{1,18},{2,17},{3,16},{4,23},{5,22},{6,21},{7,20},{8,27},{9,... | collective-permute-start | bytes 245768 | tf_op jit(solution)/shard_map/ppermute | solution.py:196
  5.0 4.6 %collective-permute-start.2 = (bf16[80,512]{1,0:T(8,128)(2,1)S(1)}, bf16[80,512]{1,0:T(8,128)(2,1)S(1)}, u32[]{:S(2)}, u32[]{:S(2)}) collective-permute-start(bf16[80,512]{1,0:T(8,128)(2,1)S(1)} %get-tuple-element.16.payload.refs_0_), channel_id=1, source_target_pairs={{0,3},{1,2},{2,1},{3,0},{4,7},{5,6},{6,5},{7,4},{8,11},{9,10},{10,... | collective-permute-start | bytes 245768 | tf_op jit(solution)/shard_map/ppermute | solution.py:196
  5.8 4.8 %collective-permute-start.1 = (bf16[80,512]{1,0:T(8,128)(2,1)S(1)}, bf16[80,512]{1,0:T(8,128)(2,1)S(1)}, u32[]{:S(2)}, u32[]{:S(2)}) collective-permute-start(bf16[80,512]{1,0:T(8,128)(2,1)S(1)} %get-tuple-element.16.payload.refs_0_), channel_id=1, source_target_pairs={{0,17},{1,16},{2,19},{3,18},{4,21},{5,20},{6,23},{7,22},{8,25},{9,... | collective-permute-start | bytes 245768 | tf_op jit(solution)/shard_map/ppermute | solution.py:196
  6.1 4.6 %collective-permute-start = (bf16[64,64]{1,0:T(8,128)(2,1)S(1)}, bf16[64,64]{1,0:T(8,128)(2,1)S(1)}, u32[]{:S(2)}, u32[]{:S(2)}) collective-permute-start(bf16[64,64]{1,0:T(8,128)(2,1)S(1)} %rows.1), channel_id=1, source_target_pairs={{0,9},{1,8},{2,11},{3,10},{4,13},{5,12},{6,15},{7,14},{8,1},{9,0},... | collective-permute-start | bytes 24584 | tf_op jit(solution)/shard_map/ppermute | solution.py:196
  8.8 4.2 %collective-permute-start.4 = (bf16[80,512]{1,0:T(8,128)(2,1)S(1)}, bf16[80,512]{1,0:T(8,128)(2,1)S(1)}, u32[]{:S(2)}, u32[]{:S(2)}) collective-permute-start(bf16[80,512]{1,0:T(8,128)(2,1)S(1)} %get-tuple-element.16.payload.refs_0_), channel_id=1, source_target_pairs={{0,1},{1,0},{2,3},{3,2},{4,5},{5,4},{6,7},{7,6},{8,9},{9,8},{10,11... | collective-permute-start | bytes 245768 | tf_op jit(solution)/shard_map/ppermute | solution.py:196
  8.8 4.2 %collective-permute-start.7 = (bf16[80,512]{1,0:T(8,128)(2,1)S(1)}, bf16[80,512]{1,0:T(8,128)(2,1)S(1)}, u32[]{:S(2)}, u32[]{:S(2)}) collective-permute-start(bf16[80,512]{1,0:T(8,128)(2,1)S(1)} %collective-permute-done.3.refs_3_), channel_id=1, source_target_pairs={{0,1},{1,0},{2,3},{3,2},{4,5},{5,4},{6,7},{7,6},{8,9},{9,8},{10,11... | collective-permute-start | bytes 245768 | tf_op jit(solution)/shard_map/ppermute | solution.py:196
  9.5 3.5 %collective-permute-start.6 = (bf16[80,512]{1,0:T(8,128)(2,1)S(1)}, bf16[80,512]{1,0:T(8,128)(2,1)S(1)}, u32[]{:S(2)}, u32[]{:S(2)}) collective-permute-start(bf16[80,512]{1,0:T(8,128)(2,1)S(1)} %collective-permute-done.2.refs_2_), channel_id=1, source_target_pairs={{0,1},{1,0},{2,3},{3,2},{4,5},{5,4},{6,7},{7,6},{8,9},{9,8},{10,11... | collective-permute-start | bytes 245768 | tf_op jit(solution)/shard_map/ppermute | solution.py:196
  10.6 2.5 %collective-permute-start.5 = (bf16[80,512]{1,0:T(8,128)(2,1)S(1)}, bf16[80,512]{1,0:T(8,128)(2,1)S(1)}, u32[]{:S(2)}, u32[]{:S(2)}) collective-permute-start(bf16[80,512]{1,0:T(8,128)(2,1)S(1)} %collective-permute-done.1.refs_1_), channel_id=1, source_target_pairs={{0,1},{1,0},{2,3},{3,2},{4,5},{5,4},{6,7},{7,6},{8,9},{9,8},{10,11... | collective-permute-start | bytes 245768 | tf_op jit(solution)/shard_map/ppermute | solution.py:196
  10.8 3.5 %collective-permute-start.8 = (bf16[64,128]{1,0:T(8,128)(2,1)S(1)}, bf16[64,128]{1,0:T(8,128)(2,1)S(1)}, u32[]{:S(2)}, u32[]{:S(2)}) collective-permute-start(bf16[64,128]{1,0:T(8,128)(2,1)S(1)} %pad_maximum_fusion.rows), channel_id=1, source_target_pairs={{0,5},{1,4},{2,7},{3,6},{4,1},{5,0},{6,3},{7,2},{8,13},{9,12},{10,... | collective-permute-start | bytes 49160 | tf_op jit(solution)/shard_map/ppermute | solution.py:196
  15.0 3.9 %collective-permute-start.9 = (f32[1,128]{1,0:T(1,128)S(1)}, f32[1,128]{1,0:T(1,128)S(1)}, u32[]{:S(2)}, u32[]{:S(2)}) collective-permute-start(f32[1,128]{1,0:T(1,128)S(1)} %sums_send.1), channel_id=1, source_target_pairs={{0,9},{1,8},{2,11},{3,10},{4,13},{5,12},{6,15},{7,14},{8,1},{9,0},... | collective-permute-start | bytes 1544 | tf_op jit(solution)/shard_map/ppermute | solution.py:196
  19.0 3.0 %collective-permute-start.10 = (f32[1,64]{1,0:T(1,128)S(1)}, f32[1,64]{1,0:T(1,128)S(1)}, u32[]{:S(2)}, u32[]{:S(2)}) collective-permute-start(f32[1,64]{1,0:T(1,128)S(1)} %get-tuple-element.28), channel_id=1, source_target_pairs={{0,5},{1,4},{2,7},{3,6},{4,1},{5,0},{6,3},{7,2},{8,13},{9,12},{10,... | collective-permute-start | bytes 776 | tf_op jit(solution)/shard_map/ppermute | solution.py:196

commit v8 on v7

--- a/solution.py
+++ b/solution.py
@@ -77,15 +77,11 @@
     base[...] = slowed[...] - STEP_SIZE * (times * (NOISE_VAR * preview[...] - targets[...]))
 
 
-def add_sums(left, payload, total):
+def add_sums(left, payload, weight, total):
     depth = payload.shape[0]
     amount = left.shape[0]
     group = min(amount, 256)
-    at = depth - EXTRA + COEF_AT
-    lane = lax.broadcasted_iota(jnp.int32, (8, depth), 1)
-    pick = jnp.where((lane >= at) & (lane < at + 3), 1.0, 0.0).astype(BF16)
     block = payload[...]
-    weight = jnp.dot(pick, block, preferred_element_type=F32)
     scaled_weight = KERNEL_RATE * weight
 
     def add_group(start):
@@ -122,10 +118,10 @@
         left[at : at + group, :] = jnp.concatenate([-2.0 * features, tail], axis=0).T.astype(BF16)
 
 
-def row_sums(left, payloads, total):
+def row_sums(left, payloads, weights, total):
     total[...] = jnp.zeros_like(total)
-    for payload in payloads:
-        add_sums(left, payload, total)
+    for k, payload in enumerate(payloads):
+        add_sums(left, payload, weights[8 * k : 8 * k + 8, :], total)
     amount = total.shape[0]
     width = min(amount, 128)
     parts = [
@@ -136,23 +132,29 @@
 
 
 def here_kernel(rows, *refs):
-    payloads, (sums, left, total) = refs[:-3], refs[-3:]
+    payloads, (sums, weights, left, total) = refs[:-4], refs[-4:]
     turn_rows(rows, left)
-    sums[...] = row_sums(left, payloads, total)
-
-
-def send_kernel(rows, here, *refs):
+    depth = payloads[0].shape[0]
+    at = depth - EXTRA + COEF_AT
+    lane = lax.broadcasted_iota(jnp.int32, (8, depth), 1)
+    pick = jnp.where((lane >= at) & (lane < at + 3), 1.0, 0.0).astype(BF16)
+    for k, payload in enumerate(payloads):
+        weights[8 * k : 8 * k + 8, :] = jnp.dot(pick, payload[...], preferred_element_type=F32)
+    sums[...] = row_sums(left, payloads, weights, total)
+
+
+def send_kernel(rows, here, weights, *refs):
     payloads, (sums, left, total) = refs[:-3], refs[-3:]
     half = total.shape[0]
     turn_rows(rows, left)
-    mine = row_sums(left.at[half : 2 * half], payloads, total)
+    mine = row_sums(left.at[half : 2 * half], payloads, weights, total)
     sums[...] = jnp.concatenate([here[:, half:], mine], axis=1)
 
 
-def keep_kernel(rows, *refs):
+def keep_kernel(rows, weights, *refs):
     payloads, (sums, left, total) = refs[:-3], refs[-3:]
     turn_rows(rows, left)
-    sums[...] = row_sums(left.at[: total.shape[0]], payloads, total)
+    sums[...] = row_sums(left.at[: total.shape[0]], payloads, weights, total)
 
 
 def finish_kernel(own, other, base, coef, spots, new_coef, new_velocity):
@@ -236,12 +238,12 @@
     amount = rows.shape[1]
     half = amount // 2
 
-    def sums(kernel, name, outs, kept, *operands):
+    def sums(kernel, name, outs, kept, *operands, more=()):
         work = kept * size * len(payloads)
         return call(
             kernel,
             name,
-            [((1, outs), F32)],
+            [((1, outs), F32), *more],
             *operands,
             *payloads,
             limit=16 << 20,
@@ -249,11 +251,12 @@
             cost=pl.CostEstimate(
                 flops=2 * feats * work, bytes_accessed=1 << 16, transcendentals=2 * work
             ),
-        )[0]
-
-    here = sums(here_kernel, "sums_here", amount, amount, rows)
-    send = sums(send_kernel, "sums_send", amount, half, more_rows, here)
-    keep = sums(keep_kernel, "sums_keep", half, half, more_rows)
+        )
+
+    weights = ((8 * len(payloads), size), F32)
+    here, weights = sums(here_kernel, "sums_here", amount, amount, rows, more=[weights])
+    (send,) = sums(send_kernel, "sums_send", amount, half, more_rows, here, weights)
+    (keep,) = sums(keep_kernel, "sums_keep", half, half, more_rows, weights)
     count = jnp.pad(counts, ((0, 0), (0, slots - counts.shape[1])))
     base, spots = call(
         terms_kernel,

time: 22.9 us -> 22.8 us (level)
  no operation moved by 1% of the time
where the time goes in v8:
time: 22.8 us; the launch traced here: 22.7 us
  starting transfers between devices  13.5 us (59%)
  Pallas kernels  4.59 us (20%)
  waiting for transfers between devices  3.05 us (13%)
  between operations  1.36 us (6%)
    ppermute x11, starting transfers between devices, exchange(): return lax.ppermute(value, AXES, pairs)  13.5 us
    pallas_call x7, Pallas kernels, call(): pl.pallas_call(kernel, out_shape=[jax.ShapeDtypeStruct(shape, kind) for s...  4.59 us
    ppermute x11, waiting for transfers between devices, exchange(): return lax.ppermute(value, AXES, pairs)  3.05 us
  transfers between devices with their start and end apart: 11, of which 4 were waited for; matrix products, arithmetic and copies ran while one was open for 0% of the time, Pallas kernels for 10%

profile of v8, /device:TPU:0, one launch (start us, length us, event | category | flops | bytes accessed | tf_op | source)
XLA Modules:
  0.0 22.7 jit_solution(16051011370800529081)
XLA Ops:
  0.6 0.9 %payload.1 = (bf16[80,512]{1,0:T(8,128)(2,1)S(1)}, s32[1,64]{1,0:T(1,128)S(1)}, f32[1,512]{1,0:T(1,128)S(1)}, f32[1,512]{1,0:T(1,128)S(1)}, f32[1,512]{1,0:T(1,128)S(1)}, /*index=5*/f32[1,512]{1,0:T(1,128)S(1)}) custom-call(bf16[64,512]{1,0:T(8,128)(2,1)} %bitcast.7, s32[1,64]{1,0:T(1,128)} %bitcast.11, f32[1,512]{1,0:T(1,128)} %bitcast.8, ...), custom_call_target="tpu_custom_call" | custom-call | tf_op jit(solution)/shard_map/payload/pallas_call | solution.py:174
  1.6 3.4 %collective-permute-start.3 = (bf16[80,512]{1,0:T(8,128)(2,1)S(1)}, bf16[80,512]{1,0:T(8,128)(2,1)S(1)}, u32[]{:S(2)}, u32[]{:S(2)}) collective-permute-start(bf16[80,512]{1,0:T(8,128)(2,1)S(1)} %get-tuple-element.18.payload.refs_0_), channel_id=1, source_target_pairs={{0,19},{1,18},{2,17},{3,16},{4,23},{5,22},{6,21},{7,20},{8,27},{9,... | collective-permute-start | bytes 245768 | tf_op jit(solution)/shard_map/ppermute | solution.py:198
  5.0 0.8 %collective-permute-start.2 = (bf16[80,512]{1,0:T(8,128)(2,1)S(1)}, bf16[80,512]{1,0:T(8,128)(2,1)S(1)}, u32[]{:S(2)}, u32[]{:S(2)}) collective-permute-start(bf16[80,512]{1,0:T(8,128)(2,1)S(1)} %get-tuple-element.18.payload.refs_0_), channel_id=1, source_target_pairs={{0,3},{1,2},{2,1},{3,0},{4,7},{5,6},{6,5},{7,4},{8,11},{9,10},{10,... | collective-permute-start | bytes 245768 | tf_op jit(solution)/shard_map/ppermute | solution.py:198
  5.8 0.1 collective-permute-start.1
  5.9 0.2 rows.1
  6.1 2.8 %collective-permute-start = (bf16[64,64]{1,0:T(8,128)(2,1)S(1)}, bf16[64,64]{1,0:T(8,128)(2,1)S(1)}, u32[]{:S(2)}, u32[]{:S(2)}) collective-permute-start(bf16[64,64]{1,0:T(8,128)(2,1)S(1)} %rows.1), channel_id=1, source_target_pairs={{0,9},{1,8},{2,11},{3,10},{4,13},{5,12},{6,15},{7,14},{8,1},{9,0},... | collective-permute-start | bytes 24584 | tf_op jit(solution)/shard_map/ppermute | solution.py:198
  8.8 0.0 collective-permute-start.4
  8.8 0.0 collective-permute-done.3.refs_3_
  8.8 0.5 %collective-permute-start.7 = (bf16[80,512]{1,0:T(8,128)(2,1)S(1)}, bf16[80,512]{1,0:T(8,128)(2,1)S(1)}, u32[]{:S(2)}, u32[]{:S(2)}) collective-permute-start(bf16[80,512]{1,0:T(8,128)(2,1)S(1)} %collective-permute-done.3.refs_3_), channel_id=1, source_target_pairs={{0,1},{1,0},{2,3},{3,2},{4,5},{5,4},{6,7},{7,6},{8,9},{9,8},{10,11... | collective-permute-start | bytes 245768 | tf_op jit(solution)/shard_map/ppermute | solution.py:198
  9.3 0.2 collective-permute-done.2.refs_2_
  9.5 0.3 %collective-permute-start.6 = (bf16[80,512]{1,0:T(8,128)(2,1)S(1)}, bf16[80,512]{1,0:T(8,128)(2,1)S(1)}, u32[]{:S(2)}, u32[]{:S(2)}) collective-permute-start(bf16[80,512]{1,0:T(8,128)(2,1)S(1)} %collective-permute-done.2.refs_2_), channel_id=1, source_target_pairs={{0,1},{1,0},{2,3},{3,2},{4,5},{5,4},{6,7},{7,6},{8,9},{9,8},{10,11... | collective-permute-start | bytes 245768 | tf_op jit(solution)/shard_map/ppermute | solution.py:198
  9.8 0.7 %collective-permute-done.1.refs_1_ = bf16[80,512]{1,0:T(8,128)(2,1)S(1)} collective-permute-done((bf16[80,512]{1,0:T(8,128)(2,1)S(1)}, bf16[80,512]{1,0:T(8,128)(2,1)S(1)}, u32[]{:S(2)}, u32[]{:S(2)}) %collective-permute-start.1) | collective-permute-done | bytes 81952 | tf_op jit(solution)/shard_map/ppermute | solution.py:198
  10.6 0.1 collective-permute-start.5
  10.7 0.0 collective-permute-done
  10.7 0.1 pad_maximum_fusion.rows
  10.8 1.6 %collective-permute-start.8 = (bf16[64,128]{1,0:T(8,128)(2,1)S(1)}, bf16[64,128]{1,0:T(8,128)(2,1)S(1)}, u32[]{:S(2)}, u32[]{:S(2)}) collective-permute-start(bf16[64,128]{1,0:T(8,128)(2,1)S(1)} %pad_maximum_fusion.rows), channel_id=1, source_target_pairs={{0,5},{1,4},{2,7},{3,6},{4,1},{5,0},{6,3},{7,2},{8,13},{9,12},{10,... | collective-permute-start | bytes 49160 | tf_op jit(solution)/shard_map/ppermute | solution.py:198
  13.0 0.0 collective-permute-done.4.refs_4_
  13.1 0.0 collective-permute-done.7.refs_7_
  13.1 0.0 collective-permute-done.6.refs_6_
  13.1 0.0 collective-permute-done.5.refs_5_
  13.1 1.1 %sums_here.1 = (f32[1,128]{1,0:T(1,128)S(1)}, f32[64,512]{1,0:T(8,128)S(1)}) custom-call(bf16[64,128]{1,0:T(8,128)(2,1)S(1)} %pad_maximum_fusion.rows, bf16[80,512]{1,0:T(8,128)(2,1)S(1)} %get-tuple-element.18.payload.refs_0_, bf16[80,512]{1,0:T(8,128)(2,1)S(1)} %collective-permute-done.1.refs_1_, bf16[80,512]{1,0:T(8,128)(2,1)S(1)} %collective-permute-done.2.refs_2_, ...), custom_call_target="tpu_custom_call" | custom-call | flops 67108864 | bytes 65536 | tf_op jit(solution)/shard_map/sums_here/pallas_call | solution.py:174
  14.2 0.0 collective-permute-done.8.rows
  14.2 0.8 %sums_send.1 = f32[1,128]{1,0:T(1,128)S(1)} custom-call(bf16[64,128]{1,0:T(8,128)(2,1)S(1)} %collective-permute-done.8.rows, f32[1,128]{1,0:T(1,128)S(1)} %get-tuple-element.19.here, f32[64,512]{1,0:T(8,128)S(1)} %get-tuple-element.20.weights, bf16[80,512]{1,0:T(8,128)(2,1)S(1)} %get-tuple-element.18.payload.refs_0_, ...), custom_call_target="tpu_custom_call" | custom-call | flops 33554432 | bytes 65536 | tf_op jit(solution)/shard_map/sums_send/pallas_call | solution.py:174
  15.0 2.5 %collective-permute-start.9 = (f32[1,128]{1,0:T(1,128)S(1)}, f32[1,128]{1,0:T(1,128)S(1)}, u32[]{:S(2)}, u32[]{:S(2)}) collective-permute-start(f32[1,128]{1,0:T(1,128)S(1)} %sums_send.1), channel_id=1, source_target_pairs={{0,9},{1,8},{2,11},{3,10},{4,13},{5,12},{6,15},{7,14},{8,1},{9,0},... | collective-permute-start | bytes 1544 | tf_op jit(solution)/shard_map/ppermute | solution.py:198
  17.5 0.7 %sums_keep.1.after = f32[1,64]{1,0:T(1,128)S(1)} custom-call(bf16[64,128]{1,0:T(8,128)(2,1)S(1)} %collective-permute-done.8.rows, f32[64,512]{1,0:T(8,128)S(1)} %get-tuple-element.20.weights, bf16[80,512]{1,0:T(8,128)(2,1)S(1)} %get-tuple-element.18.payload.refs_0_, bf16[80,512]{1,0:T(8,128)(2,1)S(1)} %collective-permute-done.1.refs_1_, ...), custom_call_target="tpu_custom_call" | custom-call | flops 33554432 | bytes 65536 | tf_op jit(solution)/shard_map/sums_keep/pallas_call | solution.py:174
  18.2 0.2 terms.1
  18.4 0.5 %collective-permute-done.9 = f32[1,128]{1,0:T(1,128)S(1)} collective-permute-done((f32[1,128]{1,0:T(1,128)S(1)}, f32[1,128]{1,0:T(1,128)S(1)}, u32[]{:S(2)}, u32[]{:S(2)}) %collective-permute-start.9) | collective-permute-done | bytes 544 | tf_op jit(solution)/shard_map/ppermute | solution.py:198
  18.9 0.1 slice_add_fusion
  19.0 1.3 %collective-permute-start.10 = (f32[1,64]{1,0:T(1,128)S(1)}, f32[1,64]{1,0:T(1,128)S(1)}, u32[]{:S(2)}, u32[]{:S(2)}) collective-permute-start(f32[1,64]{1,0:T(1,128)S(1)} %get-tuple-element.32), channel_id=1, source_target_pairs={{0,5},{1,4},{2,7},{3,6},{4,1},{5,0},{6,3},{7,2},{8,13},{9,12},{10,... | collective-permute-start | bytes 776 | tf_op jit(solution)/shard_map/ppermute | solution.py:198
  20.3 1.6 %collective-permute-done.10.other = f32[1,64]{1,0:T(1,128)S(1)} collective-permute-done((f32[1,64]{1,0:T(1,128)S(1)}, f32[1,64]{1,0:T(1,128)S(1)}, u32[]{:S(2)}, u32[]{:S(2)}) %collective-permute-start.10) | collective-permute-done | bytes 288 | tf_op jit(solution)/shard_map/ppermute | solution.py:198
  21.9 0.7 %finish.1 = (f32[1,512]{1,0:T(1,128)}, f32[1,512]{1,0:T(1,128)}) custom-call(f32[1,64]{1,0:T(1,128)S(1)} %get-tuple-element.33.own, f32[1,64]{1,0:T(1,128)S(1)} %collective-permute-done.10.other, f32[1,512]{1,0:T(1,128)S(1)} %get-tuple-element.27.base, f32[1,512]{1,0:T(1,128)S(1)} %get-tuple-element.28.coef, bf16[64,512]{1,0:T(8,128)(2,1)S(1)} %get-tuple-element.29.spots), custom_call_target="tpu_custom_call" | custom-call | tf_op jit(solution)/shard_map/finish/pallas_call | solution.py:174
  (1 shorter events, 0.0 us)
Async XLA Ops:
  1.6 7.3 %collective-permute-start.3 = (bf16[80,512]{1,0:T(8,128)(2,1)S(1)}, bf16[80,512]{1,0:T(8,128)(2,1)S(1)}, u32[]{:S(2)}, u32[]{:S(2)}) collective-permute-start(bf16[80,512]{1,0:T(8,128)(2,1)S(1)} %get-tuple-element.18.payload.refs_0_), channel_id=1, source_target_pairs={{0,19},{1,18},{2,17},{3,16},{4,23},{5,22},{6,21},{7,20},{8,27},{9,... | collective-permute-start | bytes 245768 | tf_op jit(solution)/shard_map/ppermute | solution.py:198
  5.0 4.6 %collective-permute-start.2 = (bf16[80,512]{1,0:T(8,128)(2,1)S(1)}, bf16[80,512]{1,0:T(8,128)(2,1)S(1)}, u32[]{:S(2)}, u32[]{:S(2)}) collective-permute-start(bf16[80,512]{1,0:T(8,128)(2,1)S(1)} %get-tuple-element.18.payload.refs_0_), channel_id=1, source_target_pairs={{0,3},{1,2},{2,1},{3,0},{4,7},{5,6},{6,5},{7,4},{8,11},{9,10},{10,... | collective-permute-start | bytes 245768 | tf_op jit(solution)/shard_map/ppermute | solution.py:198
  5.8 4.8 %collective-permute-start.1 = (bf16[80,512]{1,0:T(8,128)(2,1)S(1)}, bf16[80,512]{1,0:T(8,128)(2,1)S(1)}, u32[]{:S(2)}, u32[]{:S(2)}) collective-permute-start(bf16[80,512]{1,0:T(8,128)(2,1)S(1)} %get-tuple-element.18.payload.refs_0_), channel_id=1, source_target_pairs={{0,17},{1,16},{2,19},{3,18},{4,21},{5,20},{6,23},{7,22},{8,25},{9,... | collective-permute-start | bytes 245768 | tf_op jit(solution)/shard_map/ppermute | solution.py:198
  6.1 4.6 %collective-permute-start = (bf16[64,64]{1,0:T(8,128)(2,1)S(1)}, bf16[64,64]{1,0:T(8,128)(2,1)S(1)}, u32[]{:S(2)}, u32[]{:S(2)}) collective-permute-start(bf16[64,64]{1,0:T(8,128)(2,1)S(1)} %rows.1), channel_id=1, source_target_pairs={{0,9},{1,8},{2,11},{3,10},{4,13},{5,12},{6,15},{7,14},{8,1},{9,0},... | collective-permute-start | bytes 24584 | tf_op jit(solution)/shard_map/ppermute | solution.py:198
  8.8 4.2 %collective-permute-start.4 = (bf16[80,512]{1,0:T(8,128)(2,1)S(1)}, bf16[80,512]{1,0:T(8,128)(2,1)S(1)}, u32[]{:S(2)}, u32[]{:S(2)}) collective-permute-start(bf16[80,512]{1,0:T(8,128)(2,1)S(1)} %get-tuple-element.18.payload.refs_0_), channel_id=1, source_target_pairs={{0,1},{1,0},{2,3},{3,2},{4,5},{5,4},{6,7},{7,6},{8,9},{9,8},{10,11... | collective-permute-start | bytes 245768 | tf_op jit(solution)/shard_map/ppermute | solution.py:198
  8.8 4.2 %collective-permute-start.7 = (bf16[80,512]{1,0:T(8,128)(2,1)S(1)}, bf16[80,512]{1,0:T(8,128)(2,1)S(1)}, u32[]{:S(2)}, u32[]{:S(2)}) collective-permute-start(bf16[80,512]{1,0:T(8,128)(2,1)S(1)} %collective-permute-done.3.refs_3_), channel_id=1, source_target_pairs={{0,1},{1,0},{2,3},{3,2},{4,5},{5,4},{6,7},{7,6},{8,9},{9,8},{10,11... | collective-permute-start | bytes 245768 | tf_op jit(solution)/shard_map/ppermute | solution.py:198
  9.5 3.5 %collective-permute-start.6 = (bf16[80,512]{1,0:T(8,128)(2,1)S(1)}, bf16[80,512]{1,0:T(8,128)(2,1)S(1)}, u32[]{:S(2)}, u32[]{:S(2)}) collective-permute-start(bf16[80,512]{1,0:T(8,128)(2,1)S(1)} %collective-permute-done.2.refs_2_), channel_id=1, source_target_pairs={{0,1},{1,0},{2,3},{3,2},{4,5},{5,4},{6,7},{7,6},{8,9},{9,8},{10,11... | collective-permute-start | bytes 245768 | tf_op jit(solution)/shard_map/ppermute | solution.py:198
  10.6 2.5 %collective-permute-start.5 = (bf16[80,512]{1,0:T(8,128)(2,1)S(1)}, bf16[80,512]{1,0:T(8,128)(2,1)S(1)}, u32[]{:S(2)}, u32[]{:S(2)}) collective-permute-start(bf16[80,512]{1,0:T(8,128)(2,1)S(1)} %collective-permute-done.1.refs_1_), channel_id=1, source_target_pairs={{0,1},{1,0},{2,3},{3,2},{4,5},{5,4},{6,7},{7,6},{8,9},{9,8},{10,11... | collective-permute-start | bytes 245768 | tf_op jit(solution)/shard_map/ppermute | solution.py:198
  10.8 3.5 %collective-permute-start.8 = (bf16[64,128]{1,0:T(8,128)(2,1)S(1)}, bf16[64,128]{1,0:T(8,128)(2,1)S(1)}, u32[]{:S(2)}, u32[]{:S(2)}) collective-permute-start(bf16[64,128]{1,0:T(8,128)(2,1)S(1)} %pad_maximum_fusion.rows), channel_id=1, source_target_pairs={{0,5},{1,4},{2,7},{3,6},{4,1},{5,0},{6,3},{7,2},{8,13},{9,12},{10,... | collective-permute-start | bytes 49160 | tf_op jit(solution)/shard_map/ppermute | solution.py:198
  15.0 3.9 %collective-permute-start.9 = (f32[1,128]{1,0:T(1,128)S(1)}, f32[1,128]{1,0:T(1,128)S(1)}, u32[]{:S(2)}, u32[]{:S(2)}) collective-permute-start(f32[1,128]{1,0:T(1,128)S(1)} %sums_send.1), channel_id=1, source_target_pairs={{0,9},{1,8},{2,11},{3,10},{4,13},{5,12},{6,15},{7,14},{8,1},{9,0},... | collective-permute-start | bytes 1544 | tf_op jit(solution)/shard_map/ppermute | solution.py:198
  19.0 3.0 %collective-permute-start.10 = (f32[1,64]{1,0:T(1,128)S(1)}, f32[1,64]{1,0:T(1,128)S(1)}, u32[]{:S(2)}, u32[]{:S(2)}) collective-permute-start(f32[1,64]{1,0:T(1,128)S(1)} %get-tuple-element.32), channel_id=1, source_target_pairs={{0,5},{1,4},{2,7},{3,6},{4,1},{5,0},{6,3},{7,2},{8,13},{9,12},{10,... | collective-permute-start | bytes 776 | tf_op jit(solution)/shard_map/ppermute | solution.py:198
